TPU v7x, 32 devices: a whole 2x2x4 slice. The times are simulated.
32 devices in a mesh: grp: 1, ex: 32 (over z, y, x, core).
Axes of the slice: x: 2, y: 2, z: 4, core: 2. Of those that a mesh axis runs over, the one named last changes fastest.
Arguments:
- example_inputs: bfloat16 [32, 1024, 4096], P(('grp', 'ex')), may hold values from -70 to 70, as said below
- output_grads: bfloat16 [32, 1024, 1024], P(('grp', 'ex')), may hold values from -70 to 70, as said below
- proj_in: bfloat16 [128, 4096], replicated, may hold values from -0.09375 to 0.09375
- proj_out: bfloat16 [64, 1024], replicated, may hold values from -0.1875 to 0.1875
- test_grads: bfloat16 [128, 8192], P('ex'), may hold values from -6 to 6
Outputs:
- scores: float32 [32, 128], P(('grp', 'ex'))
Inputs may be any that keep to these rules, and one draw needn't show every extreme that they name: `example_inputs`: entries of the candidates' layer inputs lie within this range. `output_grads`: entries of the output gradients lie within this range.
All inputs are finite; a program needn't handle non-finite values.
Results may differ from a plain program's by a relative error of at most 0.0082.
Values may be sent and summed in bfloat16 or wider, within the bound.
No kernel may reach another device: no remote copies, remote signals or barrier semaphores. Data moves between devices by JAX's collectives and lax.ppermute only.
A program may use at most 128 MiB of HBM per device.

v0:
```python
import jax
import jax.numpy as jnp
from jax import lax
from jax.sharding import PartitionSpec as P

K_IN = 128
K_OUT = 64
TOK_EX = 1024


def damped_inverse(cov, width):
    identity = jnp.eye(width, dtype=jnp.float32)
    damped = cov + 0.1 * jnp.trace(cov) / width * identity
    factor = jnp.linalg.cholesky(damped)
    lower_inv = lax.linalg.triangular_solve(factor, identity, left_side=True, lower=True)
    return jnp.dot(lower_inv.T, lower_inv, precision=lax.Precision.HIGHEST)


def on_device(example_inputs, output_grads, proj_in, proj_out, test_grads):
    examples_here = example_inputs.shape[0]
    devices = lax.axis_size("ex")
    feat_proj = jnp.einsum(
        "etd,kd->etk", example_inputs, proj_in, preferred_element_type=jnp.float32
    ).astype(jnp.bfloat16)
    grad_proj = jnp.einsum(
        "etv,kv->etk", output_grads, proj_out, preferred_element_type=jnp.float32
    ).astype(jnp.bfloat16)
    grads = jnp.einsum("eto,eti->eoi", grad_proj, feat_proj, preferred_element_type=jnp.float32)
    flat_feat = feat_proj.reshape(-1, K_IN)
    flat_grad = grad_proj.reshape(-1, K_OUT)
    local_in = jnp.einsum("ti,tj->ij", flat_feat, flat_feat, preferred_element_type=jnp.float32)
    local_out = jnp.einsum("ti,tj->ij", flat_grad, flat_grad, preferred_element_type=jnp.float32)
    sum_in, sum_out = lax.psum((local_in, local_out), "ex")
    total_tokens = examples_here * TOK_EX * devices
    inverse_in = damped_inverse(sum_in / total_tokens, K_IN)
    inverse_out = damped_inverse(sum_out / total_tokens, K_OUT)
    scale = 4.0 / (K_IN * K_OUT * TOK_EX) ** 0.5
    left = jnp.einsum("oa,eai->eoi", inverse_out, grads, precision=lax.Precision.HIGHEST)
    both = jnp.einsum("eoa,ai->eoi", left, inverse_in, precision=lax.Precision.HIGHEST)
    precond = both.reshape(grads.shape[0], K_OUT * K_IN).astype(jnp.bfloat16)
    score_block = lax.dot_general(
        precond,
        lax.all_gather(test_grads, "ex", axis=0, tiled=True),
        (((1,), (1,)), ((), ())),
        preferred_element_type=jnp.float32,
    )
    return score_block * scale


def solution(mesh):
    return jax.shard_map(
        on_device,
        mesh=mesh,
        in_specs=(
            P(("grp", "ex"), None, None),
            P(("grp", "ex"), None, None),
            P(),
            P(),
            P("ex", None),
        ),
        out_specs=P(("grp", "ex"), None),
        check_vma=False,
    )
```

profile of v0, /device:TPU:1, one launch (start us, length us, event | category | flops | bytes accessed | tf_op | source)
XLA Modules:
  0.0 207.8 jit_solution(5839962891657765232)
XLA Ops:
  6.5 0.0 copy-start
  6.5 0.0 copy-start.1
  6.5 0.0 all-reduce.2.cloned.1.call-start
  6.5 6.1 %fusion.4 = bf16[1024,128]{1,0:T(8,128)(2,1)S(1)} fusion(bf16[128,4096]{1,0:T(8,128)(2,1)} %param.7, bf16[1,1024,4096]{2,1,0:T(8,128)(2,1)} %param.5), kind=kOutput, calls=%fused_computation.4 | convolution fusion | flops 1073872896 | bytes 9699328 | tf_op jit(solution)/shard_map/etd,kd->etk/dot_general | solution.py:22
  12.6 0.9 fusion.24
  13.5 0.0 all-reduce.2.cloned.1.call-update
  13.5 0.0 all-gather.3.cloned.1.call-start
  13.6 0.7 all-gather.3.cloned.1.call-update
  14.3 0.0 copy-done
  14.3 0.0 copy-done.1
  14.3 0.8 fusion.7
  15.1 0.2 fusion.22
  15.3 41.3 %psum.14 = f32[64,64]{1,0:T(8,128)S(1)} all-reduce(f32[64,64]{1,0:T(8,128)S(1)} %fusion.22), channel_id=1, replica_groups=mesh['grp'=1,'ex'=32] {'ex'}, use_global_device_ids=true, to_apply=%region_0.0 | all-reduce | flops 4096 | bytes 32768 | tf_op jit(solution)/shard_map/psum | solution.py:33
  56.6 0.6 select_reduce_fusion.3
  57.9 0.1 copy.8
  58.0 5.8 %cholesky.33 = f32[64,64]{1,0:T(8,128)S(1)} custom-call(f32[64,64]{1,0:T(8,128)S(1)} %fusion.20), custom_call_target="Cholesky" | custom-call | tf_op jit(solution)/shard_map/jit(cholesky)/cholesky | solution.py:14
  63.9 0.6 compare_reduce_fusion.1
  64.5 0.7 fusion.17
  65.2 4.9 %custom-call.12 = f32[1,64,64]{1,2,0:T(8,128)S(1)} custom-call(f32[1,64,64]{2,1,0:T(8,128)S(1)} %fusion.17), custom_call_target="InvertDiagBlocksLowerTriangular" | custom-call | tf_op jit(solution)/shard_map/triangular_solve | solution.py:15
  70.1 0.2 fusion.18
  70.3 0.2 fusion.23
  70.6 0.2 fusion.21
  70.7 0.2 convolution_bitcast_fusion
  70.9 64.5 %all-reduce.2.cloned.1.call-done = f32[128,128]{1,0:T(8,128)} async-done(((f32[128,128]{1,0:T(8,128)}), f32[128,128]{1,0:T(8,128)}) %all-reduce.2.cloned.1.call-update) | async-done | bytes 65552 | tf_op jit(solution)/shard_map/psum | solution.py:33
  135.4 1.5 select_reduce_fusion.1
  137.5 0.9 select_add_fusion
  138.4 0.1 copy.9
  138.5 0.9 fusion.16
  139.3 11.7 %cholesky.68 = f32[128,128]{1,0:T(8,128)S(1)} custom-call(f32[128,128]{1,0:T(8,128)S(1)} %fusion.16), custom_call_target="Cholesky" | custom-call | tf_op jit(solution)/shard_map/jit(cholesky)/cholesky | solution.py:14
  151.1 0.6 compare_reduce_fusion
  151.7 0.7 fusion.13
  152.4 9.8 %custom-call.13 = f32[1,128,128]{1,2,0:T(8,128)S(1)} custom-call(f32[1,128,128]{2,1,0:T(8,128)S(1)} %fusion.13), custom_call_target="InvertDiagBlocksLowerTriangular" | custom-call | tf_op jit(solution)/shard_map/triangular_solve | solution.py:15
  162.2 0.2 fusion.14
  162.4 0.3 fusion.25
  162.7 0.2 fusion.10
  163.0 31.3 %all-gather.3.cloned.1.call-done = bf16[32,4,8192]{2,1,0:T(4,128)(2,1)} async-done(((bf16[1,4,8192]{2,1,0:T(4,128)(2,1)}), bf16[32,4,8192]{2,1,0:T(4,128)(2,1)}) %all-gather.3.cloned.1.call-update) | async-done | bytes 2097168 | tf_op jit(solution)/shard_map/all_gather | solution.py:43
  194.3 4.0 %reshape.57 = bf16[128,8192]{1,0:T(8,128)(2,1)} reshape(bf16[32,4,8192]{2,1,0:T(4,128)(2,1)} %all-gather.3.cloned.1.call-done) | data formatting | bytes 4194304
  198.2 2.8 %fusion.12 = f32[1,128]{1,0:T(1,128)} fusion(bf16[8192,1]{0,1:T(2,128)(2,1)S(1)} %reshape.58, bf16[128,8192]{1,0:T(8,128)(2,1)} %reshape.57), kind=kOutput, calls=%fused_computation.11 | convolution fusion | flops 2097280 | bytes 2114048 | tf_op jit(solution)/shard_map/dot_general | solution.py:41
  (5 shorter events, 0.1 us)
Async XLA Ops:
  6.5 7.8 %copy-start = (bf16[1,1024,1024]{2,1,0:T(8,128)(2,1)S(1)}, bf16[1,1024,1024]{2,1,0:T(8,128)(2,1)}, u32[]{:S(2)}) copy-start(bf16[1,1024,1024]{2,1,0:T(8,128)(2,1)} %param.6) | copy-start | bytes 6291460
  6.5 7.8 %copy-start.1 = (bf16[64,1024]{1,0:T(8,128)(2,1)S(1)}, bf16[64,1024]{1,0:T(8,128)(2,1)}, u32[]{:S(2)}) copy-start(bf16[64,1024]{1,0:T(8,128)(2,1)} %param.8) | copy-start | bytes 393220
  6.5 128.8 %all-reduce.2.cloned.1.call-start = ((), (), s32[]{:S(2)}) async-start(), calls=%async_computation | async-start | bytes 131072 | tf_op jit(solution)/shard_map/psum | solution.py:33
  13.5 180.7 %all-gather.3.cloned.1.call-start = ((), (), s32[]{:S(2)}) async-start(), calls=%async_computation.1 | async-start | bytes 2162688 | tf_op jit(solution)/shard_map/all_gather | solution.py:43
Sparse Core Ops, SparseCore 0:
  13.7 121.6 all-reduce.1
  138.2 55.9 all-gather.2
where the time goes:
time: 208 us
  waiting for transfers between devices  96.5 us (46%)
  blocking collectives  41.3 us (20%)
  other arithmetic  38.8 us (19%)
  between operations  14.9 us (7%)
  matrix products  12.2 us (6%)
  local copies, waits for them, and re-layouts  4.16 us (2%)
    psum x1, waiting for transfers between devices, on_device(): sum_in, sum_out = lax.psum((local_in, local_out), 'ex')  64.5 us
    psum x1, blocking collectives, on_device(): sum_in, sum_out = lax.psum((local_in, local_out), 'ex')  41.3 us
    all_gather x1, waiting for transfers between devices, on_device(): lax.all_gather(test_grads, 'ex', axis=0, tiled=True)  31.3 us
    another operation x6, other arithmetic, damped_inverse(): factor = jnp.linalg.cholesky(damped)  18.9 us
    another operation x4, other arithmetic, damped_inverse(): lax.linalg.triangular_solve(factor, identity, left_side=True, lower=True)  16 us
    dot_general x1, matrix products, on_device(): jnp.einsum('etd,kd->etk', example_inputs, proj_in, preferred_element_type...  6.09 us
  transfers between devices with their start and end apart: 2, of which 2 were waited for; matrix products, arithmetic and copies ran while one was open for 20% of the time, Pallas kernels for 0%

commit v1 on v0

--- a/solution.py
+++ b/solution.py
@@ -16,9 +16,42 @@
     return jnp.dot(lower_inv.T, lower_inv, precision=lax.Precision.HIGHEST)
 
 
+def exchange(x, bit, devices):
+    return lax.ppermute(x, "ex", [(i, i ^ bit) for i in range(devices)])
+
+
+def sum_over_devices(x, devices):
+    bit = 1
+    while bit < devices:
+        x = x + exchange(x, bit, devices)
+        bit *= 2
+    return x
+
+
+def gather_tests(tests, devices):
+    bit = devices // 2
+    while bit:
+        tests = jnp.concatenate([tests, exchange(tests, bit, devices)], axis=0)
+        bit //= 2
+    return tests
+
+
+def arrival_order(devices):
+    order = [0]
+    bit = devices // 2
+    while bit:
+        order = order + [k ^ bit for k in order]
+        bit //= 2
+    return order
+
+
 def on_device(example_inputs, output_grads, proj_in, proj_out, test_grads):
     examples_here = example_inputs.shape[0]
     devices = lax.axis_size("ex")
+    if devices & (devices - 1):
+        everyone = lax.all_gather(test_grads, "ex", axis=0, tiled=True)
+    else:
+        everyone = gather_tests(test_grads, devices)
     feat_proj = jnp.einsum(
         "etd,kd->etk", example_inputs, proj_in, preferred_element_type=jnp.float32
     ).astype(jnp.bfloat16)
@@ -30,7 +63,16 @@
     flat_grad = grad_proj.reshape(-1, K_OUT)
     local_in = jnp.einsum("ti,tj->ij", flat_feat, flat_feat, preferred_element_type=jnp.float32)
     local_out = jnp.einsum("ti,tj->ij", flat_grad, flat_grad, preferred_element_type=jnp.float32)
-    sum_in, sum_out = lax.psum((local_in, local_out), "ex")
+    half = K_OUT // 2
+    packed = jnp.concatenate(
+        [local_in, jnp.concatenate([local_out[:half], local_out[half:]], axis=1)], axis=0
+    )
+    if devices & (devices - 1):
+        packed = lax.psum(packed, "ex")
+    else:
+        packed = sum_over_devices(packed, devices)
+    sum_in = packed[:K_IN]
+    sum_out = jnp.concatenate([packed[K_IN:, :K_OUT], packed[K_IN:, K_OUT:]], axis=0)
     total_tokens = examples_here * TOK_EX * devices
     inverse_in = damped_inverse(sum_in / total_tokens, K_IN)
     inverse_out = damped_inverse(sum_out / total_tokens, K_OUT)
@@ -39,11 +81,14 @@
     both = jnp.einsum("eoa,ai->eoi", left, inverse_in, precision=lax.Precision.HIGHEST)
     precond = both.reshape(grads.shape[0], K_OUT * K_IN).astype(jnp.bfloat16)
     score_block = lax.dot_general(
-        precond,
-        lax.all_gather(test_grads, "ex", axis=0, tiled=True),
-        (((1,), (1,)), ((), ())),
-        preferred_element_type=jnp.float32,
+        precond, everyone, (((1,), (1,)), ((), ())), preferred_element_type=jnp.float32
     )
+    if devices & (devices - 1) == 0:
+        per = test_grads.shape[0]
+        order = jnp.array(arrival_order(devices), jnp.int32) ^ lax.axis_index("ex")
+        place = (order[:, None] * per + jnp.arange(per)[None, :]).reshape(-1)
+        hot = (place[:, None] == jnp.arange(devices * per)[None, :]).astype(jnp.float32)
+        score_block = jnp.dot(score_block, hot, precision=lax.Precision.HIGHEST)
     return score_block * scale
 
 

time: 208 us -> 89.7 us (0.43)
  waiting for transfers between devices: 96.5 us -> 9.12 us
  blocking collectives: 41.3 us -> 0 us
  starting transfers between devices: 0.04 us -> 16.1 us
  between operations: 14.9 us -> 1.55 us
  local copies, waits for them, and re-layouts: 4.16 us -> 12.6 us
    psum x1 -> x0, waiting for transfers between devices: 64.5 us -> none  [on_device(): sum_in, sum_out = lax.psum((local_in, local_out), 'ex')]
    psum x1 -> x0, blocking collectives: 41.3 us -> none  [on_device(): sum_in, sum_out = lax.psum((local_in, local_out), 'ex')]
    all_gather x1 -> x0, waiting for transfers between devices: 31.3 us -> none  [on_device(): lax.all_gather(test_grads, 'ex', axis=0, tiled=True)]
    ppermute x0 -> x10, starting transfers between devices: none -> 16.1 us  [exchange(): return lax.ppermute(x, 'ex', [(i, i ^ bit) for i in range(devices)])]
    concatenate x0 -> x2, local copies, waits for them, and re-layouts: none -> 12.3 us  [gather_tests(): tests = jnp.concatenate([tests, exchange(tests, bit, devices)], axis=0)]
    ppermute x0 -> x10, waiting for transfers between devices: none -> 9.12 us  [exchange(): return lax.ppermute(x, 'ex', [(i, i ^ bit) for i in range(devices)])]
    unnamed x5 -> x8, local copies, waits for them, and re-layouts: 3.98 us -> 0.02 us
  transfers between devices with their start and end apart: 2 -> 10, of which waited for: 2 -> 5; matrix products, arithmetic and copies ran while one was open for 20% -> 52% of each run, Pallas kernels for 0% -> 0%
where the time goes in v1:
time: 89.7 us; the launch traced here: 89.3 us
  other arithmetic  37.6 us (42%)
  starting transfers between devices  16.1 us (18%)
  local copies, waits for them, and re-layouts  12.6 us (14%)
  matrix products  12.3 us (14%)
  waiting for transfers between devices  9.12 us (10%)
  between operations  1.55 us (2%)
    another operation x6, other arithmetic, damped_inverse(): factor = jnp.linalg.cholesky(damped)  18.9 us
    ppermute x10, starting transfers between devices, exchange(): return lax.ppermute(x, 'ex', [(i, i ^ bit) for i in range(devices)])  16.1 us
    another operation x4, other arithmetic, damped_inverse(): lax.linalg.triangular_solve(factor, identity, left_side=True, lower=True)  16 us
    concatenate x2, local copies, waits for them, and re-layouts, gather_tests(): tests = jnp.concatenate([tests, exchange(tests, bit, devices)], axis=0)  12.3 us
    ppermute x10, waiting for transfers between devices, exchange(): return lax.ppermute(x, 'ex', [(i, i ^ bit) for i in range(devices)])  9.12 us
    dot_general x1, matrix products, on_device(): jnp.einsum('etd,kd->etk', example_inputs, proj_in, preferred_element_type...  5.74 us
    dot_general x1, matrix products, on_device(): lax.dot_general(precond, everyone, (((1,), (1,)), ((), ())), preferred_el...  2.23 us
  transfers between devices with their start and end apart: 10, of which 5 were waited for; matrix products, arithmetic and copies ran while one was open for 52% of the time, Pallas kernels for 0%

profile of v1, /device:TPU:1, one launch (start us, length us, event | category | flops | bytes accessed | tf_op | source)
XLA Modules:
  0.0 89.3 jit_solution(14400813360981970710)
XLA Ops:
  0.0 0.0 copy-start
  0.0 0.0 copy-start.2
  0.0 3.1 %collective-permute-start.5 = (bf16[4,8192]{1,0:T(4,128)(2,1)}, bf16[4,8192]{1,0:T(4,128)(2,1)S(1)}, u32[]{:S(2)}, u32[]{:S(2)}) collective-permute-start(bf16[4,8192]{1,0:T(4,128)(2,1)} %param.10), channel_id=1, source_target_pairs={{0,16},{1,17},{2,18},{3,19},{4,20},{5,21},{6,22},{7,23},{8,24},{9,... | collective-permute-start | bytes 196616 | tf_op jit(solution)/shard_map/ppermute | solution.py:20
  3.1 0.0 copy-done
  3.1 1.7 %fusion.7 = bf16[1024,64]{0,1:T(8,128)(2,1)S(1)} fusion(bf16[64,1024]{1,0:T(8,128)(2,1)} %param.9, bf16[1,1024,1024]{2,1,0:T(8,128)(2,1)S(1)} %copy-done), kind=kOutput, calls=%fused_computation.5 | convolution fusion | flops 134283264 | bytes 2359296 | tf_op jit(solution)/shard_map/etv,kv->etk/dot_general | solution.py:58
  4.8 0.2 fusion.26
  5.0 0.0 copy-done.2
  5.0 0.0 copy-start.3
  5.0 0.0 copy-start.1
  5.0 5.7 %fusion.4 = bf16[1024,128]{1,0:T(8,128)(2,1)S(1)} fusion(bf16[128,4096]{1,0:T(8,128)(2,1)S(1)} %copy-done.2, bf16[1,1024,4096]{2,1,0:T(8,128)(2,1)} %param.6), kind=kOutput, calls=%fused_computation.4 | convolution fusion | flops 1073872896 | bytes 9699328 | tf_op jit(solution)/shard_map/etd,kd->etk/dot_general | solution.py:55
  10.8 0.3 fusion.25
  11.1 0.1 maximum_maximum_fusion
  11.1 1.0 %collective-permute-start = (f32[160,128]{1,0:T(8,128)S(1)}, f32[160,128]{1,0:T(8,128)S(1)}, u32[]{:S(2)}, u32[]{:S(2)}) collective-permute-start(f32[160,128]{1,0:T(8,128)S(1)} %maximum_maximum_fusion), channel_id=1, source_target_pairs={{0,1},{1,0},{2,3},{3,2},{4,5},{5,4},{6,7},{7,6},{8,9},{9,8},{10,11... | collective-permute-start | bytes 245768 | tf_op jit(solution)/shard_map/ppermute | solution.py:20
  12.1 0.2 fusion.24
  12.3 0.7 collective-permute-done
  13.0 0.1 fusion.48
  13.1 1.2 %collective-permute-start.1 = (f32[160,128]{1,0:T(8,128)S(1)}, f32[160,128]{1,0:T(8,128)S(1)}, u32[]{:S(2)}, u32[]{:S(2)}) collective-permute-start(f32[160,128]{1,0:T(8,128)S(1)} %fusion.48), channel_id=1, source_target_pairs={{0,2},{1,3},{2,0},{3,1},{4,6},{5,7},{6,4},{7,5},{8,10},{9,11},{10,... | collective-permute-start | bytes 245768 | tf_op jit(solution)/shard_map/ppermute | solution.py:20
  14.3 0.0 copy-done.3
  14.3 2.5 %collective-permute-done.1 = f32[160,128]{1,0:T(8,128)S(1)} collective-permute-done((f32[160,128]{1,0:T(8,128)S(1)}, f32[160,128]{1,0:T(8,128)S(1)}, u32[]{:S(2)}, u32[]{:S(2)}) %collective-permute-start.1) | collective-permute-done | bytes 81952 | tf_op jit(solution)/shard_map/ppermute | solution.py:20
  16.8 1.3 %collective-permute-start.2 = (f32[160,128]{1,0:T(8,128)S(1)}, f32[160,128]{1,0:T(8,128)S(1)}, u32[]{:S(2)}, u32[]{:S(2)}) collective-permute-start(f32[160,128]{1,0:T(8,128)S(1)} %add.64), channel_id=1, source_target_pairs={{0,4},{1,5},{2,6},{3,7},{4,0},{5,1},{6,2},{7,3},{8,12},{9,13},{10,... | collective-permute-start | bytes 245768 | tf_op jit(solution)/shard_map/ppermute | solution.py:20
  18.1 0.0 collective-permute-done.5
  18.1 0.0 copy-done.1
  18.1 0.1 pad_maximum_fusion.2
  18.2 1.4 %collective-permute-start.6 = (bf16[8,8192]{1,0:T(8,128)(2,1)S(1)}, bf16[8,8192]{1,0:T(8,128)(2,1)S(1)}, u32[]{:S(2)}, u32[]{:S(2)}) collective-permute-start(bf16[8,8192]{1,0:T(8,128)(2,1)S(1)} %pad_maximum_fusion.2), channel_id=1, source_target_pairs={{0,8},{1,9},{2,10},{3,11},{4,12},{5,13},{6,14},{7,15},{8,0},{9,1},... | collective-permute-start | bytes 393224 | tf_op jit(solution)/shard_map/ppermute | solution.py:20
  19.5 0.6 collective-permute-done.2
  20.2 1.4 %collective-permute-start.3 = (f32[160,128]{1,0:T(8,128)S(1)}, f32[160,128]{1,0:T(8,128)S(1)}, u32[]{:S(2)}, u32[]{:S(2)}) collective-permute-start(f32[160,128]{1,0:T(8,128)S(1)} %add.65), channel_id=1, source_target_pairs={{0,8},{1,9},{2,10},{3,11},{4,12},{5,13},{6,14},{7,15},{8,0},{9,1},... | collective-permute-start | bytes 245768 | tf_op jit(solution)/shard_map/ppermute | solution.py:20
  21.5 0.1 iota_add_fusion
  21.6 0.1 add.75
  21.7 3.0 %collective-permute-done.3 = f32[160,128]{1,0:T(8,128)S(1)} collective-permute-done((f32[160,128]{1,0:T(8,128)S(1)}, f32[160,128]{1,0:T(8,128)S(1)}, u32[]{:S(2)}, u32[]{:S(2)}) %collective-permute-start.3) | collective-permute-done | bytes 81952 | tf_op jit(solution)/shard_map/ppermute | solution.py:20
  24.7 1.4 %collective-permute-start.4 = (f32[160,128]{1,0:T(8,128)S(1)}, f32[160,128]{1,0:T(8,128)S(1)}, u32[]{:S(2)}, u32[]{:S(2)}) collective-permute-start(f32[160,128]{1,0:T(8,128)S(1)} %add.66), channel_id=1, source_target_pairs={{0,16},{1,17},{2,18},{3,19},{4,20},{5,21},{6,22},{7,23},{8,24},{9,... | collective-permute-start | bytes 245768 | tf_op jit(solution)/shard_map/ppermute | solution.py:20
  26.1 0.0 collective-permute-done.6
  26.1 0.1 pad_maximum_fusion.1
  26.2 0.5 collective-permute-start.7
  26.7 2.3 %collective-permute-done.4 = f32[160,128]{1,0:T(8,128)S(1)} collective-permute-done((f32[160,128]{1,0:T(8,128)S(1)}, f32[160,128]{1,0:T(8,128)S(1)}, u32[]{:S(2)}, u32[]{:S(2)}) %collective-permute-start.4) | collective-permute-done | bytes 81952 | tf_op jit(solution)/shard_map/ppermute | solution.py:20
  29.0 0.6 select_reduce_fusion.1
  29.6 0.1 fusion.22
  30.4 0.6 select_reduce_fusion.3
  31.6 0.1 copy.9
  31.7 5.8 %cholesky.33 = f32[64,64]{1,0:T(8,128)S(1)} custom-call(f32[64,64]{1,0:T(8,128)S(1)} %fusion.20), custom_call_target="Cholesky" | custom-call | tf_op jit(solution)/shard_map/jit(cholesky)/cholesky | solution.py:14
  37.6 0.6 compare_reduce_fusion.1
  38.3 0.1 copy.10
  38.4 0.0 collective-permute-done.7
  38.4 0.9 %pad_maximum_fusion = bf16[32,8192]{1,0:T(8,128)(2,1)} fusion(bf16[16,8192]{1,0:T(8,128)(2,1)S(1)} %collective-permute-done.7, bf16[8,8192]{1,0:T(8,128)(2,1)S(1)} %collective-permute-done.6, bf16[4,8192]{1,0:T(4,128)(2,1)S(1)} %collective-permute-done.5, bf16[4,8192]{1,0:T(4,128)(2,1)S(1)} %copy-done.1), kind=kLoop, calls=%fused_computation.13 | loop fusion | flops 2097152 | bytes 1048576 | tf_op jit(solution)/shard_map/concatenate | solution.py:34
  39.3 1.2 %collective-permute-start.8 = (bf16[32,8192]{1,0:T(8,128)(2,1)}, bf16[32,8192]{1,0:T(8,128)(2,1)S(1)}, u32[]{:S(2)}, u32[]{:S(2)}) collective-permute-start(bf16[32,8192]{1,0:T(8,128)(2,1)} %pad_maximum_fusion), channel_id=1, source_target_pairs={{0,2},{1,3},{2,0},{3,1},{4,6},{5,7},{6,4},{7,5},{8,10},{9,11},{10,... | collective-permute-start | bytes 1572872 | tf_op jit(solution)/shard_map/ppermute | solution.py:20
  40.5 0.7 fusion.17
  41.2 11.7 %cholesky.68 = f32[128,128]{1,0:T(8,128)S(1)} custom-call(f32[128,128]{1,0:T(8,128)S(1)} %fusion.16), custom_call_target="Cholesky" | custom-call | tf_op jit(solution)/shard_map/jit(cholesky)/cholesky | solution.py:14
  52.9 4.9 %custom-call.12 = f32[1,64,64]{1,2,0:T(8,128)S(1)} custom-call(f32[1,64,64]{2,1,0:T(8,128)S(1)} %fusion.17), custom_call_target="InvertDiagBlocksLowerTriangular" | custom-call | tf_op jit(solution)/shard_map/triangular_solve | solution.py:15
  57.8 0.6 compare_reduce_fusion
  58.5 0.7 fusion.13
  59.1 0.0 collective-permute-done.8
  59.1 3.6 %concatenate.34 = bf16[64,8192]{1,0:T(8,128)(2,1)} concatenate(bf16[4,8192]{1,0:T(4,128)(2,1)S(1)} %copy-done.1, bf16[4,8192]{1,0:T(4,128)(2,1)S(1)} %collective-permute-done.5, bf16[8,8192]{1,0:T(8,128)(2,1)S(1)} %collective-permute-done.6, bf16[16,8192]{1,0:T(8,128)(2,1)S(1)} %collective-permute-done.7, bf16[32,8192]{1,0:T(8,128)(2,1)S(1)} %collective-permute-done.8), dimensions={0} | concatenate | bytes 2097152 | tf_op jit(solution)/shard_map/concatenate | solution.py:34
  62.7 3.7 %collective-permute-start.9 = (bf16[64,8192]{1,0:T(8,128)(2,1)}, bf16[64,8192]{1,0:T(8,128)(2,1)}, u32[]{:S(2)}, u32[]{:S(2)}) collective-permute-start(bf16[64,8192]{1,0:T(8,128)(2,1)} %concatenate.34), channel_id=1, source_target_pairs={{0,1},{1,0},{2,3},{3,2},{4,5},{5,4},{6,7},{7,6},{8,9},{9,8},{10,11... | collective-permute-start | bytes 3145736 | tf_op jit(solution)/shard_map/ppermute | solution.py:20
  66.4 0.2 fusion.18
  66.7 9.8 %custom-call.13 = f32[1,128,128]{1,2,0:T(8,128)S(1)} custom-call(f32[1,128,128]{2,1,0:T(8,128)S(1)} %fusion.13), custom_call_target="InvertDiagBlocksLowerTriangular" | custom-call | tf_op jit(solution)/shard_map/triangular_solve | solution.py:15
  76.5 0.2 fusion.27
  76.7 0.2 convolution_bitcast_fusion
  76.9 0.2 fusion.14
  77.1 0.3 fusion.28
  77.4 0.2 fusion.10
  77.6 0.0 collective-permute-done.9
  77.7 8.7 %concatenate.35 = bf16[128,8192]{1,0:T(8,128)(2,1)} concatenate(bf16[4,8192]{1,0:T(4,128)(2,1)S(1)} %copy-done.1, bf16[4,8192]{1,0:T(4,128)(2,1)S(1)} %collective-permute-done.5, bf16[8,8192]{1,0:T(8,128)(2,1)S(1)} %collective-permute-done.6, bf16[16,8192]{1,0:T(8,128)(2,1)S(1)} %collective-permute-done.7, bf16[32,8192]{1,0:T(8,128)(2,1)S(1)} %collective-permute-done.8, ...), dimensions={0} | concatenate | bytes 4194304 | tf_op jit(solution)/shard_map/concatenate | solution.py:34
  86.4 2.2 %convolution_bitcast_fusion.2 = f32[128,1]{0,1:T(1,128)S(1)} fusion(bf16[8192,1]{0,1:T(2,128)(2,1)S(1)} %reshape.75, bf16[128,8192]{1,0:T(8,128)(2,1)} %concatenate.35), kind=kOutput, calls=%fused_computation.12 | convolution fusion | flops 2097152 | bytes 2114048 | tf_op jit(solution)/shard_map/dot_general | solution.py:83
  88.6 0.8 fusion.12
  (13 shorter events, 0.2 us)
Async XLA Ops:
  0.0 3.1 %copy-start = (bf16[1,1024,1024]{2,1,0:T(8,128)(2,1)S(1)}, bf16[1,1024,1024]{2,1,0:T(8,128)(2,1)}, u32[]{:S(2)}) copy-start(bf16[1,1024,1024]{2,1,0:T(8,128)(2,1)} %param.7) | copy-start | bytes 6291460
  0.0 5.0 %copy-start.2 = (bf16[128,4096]{1,0:T(8,128)(2,1)S(1)}, bf16[128,4096]{1,0:T(8,128)(2,1)}, u32[]{:S(2)}) copy-start(bf16[128,4096]{1,0:T(8,128)(2,1)} %param.8) | copy-start | bytes 3145732
  0.0 18.1 %collective-permute-start.5 = (bf16[4,8192]{1,0:T(4,128)(2,1)}, bf16[4,8192]{1,0:T(4,128)(2,1)S(1)}, u32[]{:S(2)}, u32[]{:S(2)}) collective-permute-start(bf16[4,8192]{1,0:T(4,128)(2,1)} %param.10), channel_id=1, source_target_pairs={{0,16},{1,17},{2,18},{3,19},{4,20},{5,21},{6,22},{7,23},{8,24},{9,... | collective-permute-start | bytes 196616 | tf_op jit(solution)/shard_map/ppermute | solution.py:20
  5.0 9.3 %copy-start.3 = (s32[32]{0:T(128)S(1)}, s32[32]{0:T(128)}, u32[]{:S(2)}) copy-start(s32[32]{0:T(128)} %constant.111.clone) | copy-start | bytes 388
  5.0 13.1 %copy-start.1 = (bf16[4,8192]{1,0:T(4,128)(2,1)S(1)}, bf16[4,8192]{1,0:T(4,128)(2,1)}, u32[]{:S(2)}) copy-start(bf16[4,8192]{1,0:T(4,128)(2,1)} %param.10) | copy-start | bytes 196612
  11.1 1.9 %collective-permute-start = (f32[160,128]{1,0:T(8,128)S(1)}, f32[160,128]{1,0:T(8,128)S(1)}, u32[]{:S(2)}, u32[]{:S(2)}) collective-permute-start(f32[160,128]{1,0:T(8,128)S(1)} %maximum_maximum_fusion), channel_id=1, source_target_pairs={{0,1},{1,0},{2,3},{3,2},{4,5},{5,4},{6,7},{7,6},{8,9},{9,8},{10,11... | collective-permute-start | bytes 245768 | tf_op jit(solution)/shard_map/ppermute | solution.py:20
  13.1 3.7 %collective-permute-start.1 = (f32[160,128]{1,0:T(8,128)S(1)}, f32[160,128]{1,0:T(8,128)S(1)}, u32[]{:S(2)}, u32[]{:S(2)}) collective-permute-start(f32[160,128]{1,0:T(8,128)S(1)} %fusion.48), channel_id=1, source_target_pairs={{0,2},{1,3},{2,0},{3,1},{4,6},{5,7},{6,4},{7,5},{8,10},{9,11},{10,... | collective-permute-start | bytes 245768 | tf_op jit(solution)/shard_map/ppermute | solution.py:20
  16.8 3.4 %collective-permute-start.2 = (f32[160,128]{1,0:T(8,128)S(1)}, f32[160,128]{1,0:T(8,128)S(1)}, u32[]{:S(2)}, u32[]{:S(2)}) collective-permute-start(f32[160,128]{1,0:T(8,128)S(1)} %add.64), channel_id=1, source_target_pairs={{0,4},{1,5},{2,6},{3,7},{4,0},{5,1},{6,2},{7,3},{8,12},{9,13},{10,... | collective-permute-start | bytes 245768 | tf_op jit(solution)/shard_map/ppermute | solution.py:20
  18.2 7.9 %collective-permute-start.6 = (bf16[8,8192]{1,0:T(8,128)(2,1)S(1)}, bf16[8,8192]{1,0:T(8,128)(2,1)S(1)}, u32[]{:S(2)}, u32[]{:S(2)}) collective-permute-start(bf16[8,8192]{1,0:T(8,128)(2,1)S(1)} %pad_maximum_fusion.2), channel_id=1, source_target_pairs={{0,8},{1,9},{2,10},{3,11},{4,12},{5,13},{6,14},{7,15},{8,0},{9,1},... | collective-permute-start | bytes 393224 | tf_op jit(solution)/shard_map/ppermute | solution.py:20
  20.2 4.5 %collective-permute-start.3 = (f32[160,128]{1,0:T(8,128)S(1)}, f32[160,128]{1,0:T(8,128)S(1)}, u32[]{:S(2)}, u32[]{:S(2)}) collective-permute-start(f32[160,128]{1,0:T(8,128)S(1)} %add.65), channel_id=1, source_target_pairs={{0,8},{1,9},{2,10},{3,11},{4,12},{5,13},{6,14},{7,15},{8,0},{9,1},... | collective-permute-start | bytes 245768 | tf_op jit(solution)/shard_map/ppermute | solution.py:20
  24.7 4.3 %collective-permute-start.4 = (f32[160,128]{1,0:T(8,128)S(1)}, f32[160,128]{1,0:T(8,128)S(1)}, u32[]{:S(2)}, u32[]{:S(2)}) collective-permute-start(f32[160,128]{1,0:T(8,128)S(1)} %add.66), channel_id=1, source_target_pairs={{0,16},{1,17},{2,18},{3,19},{4,20},{5,21},{6,22},{7,23},{8,24},{9,... | collective-permute-start | bytes 245768 | tf_op jit(solution)/shard_map/ppermute | solution.py:20
  26.2 12.2 %collective-permute-start.7 = (bf16[16,8192]{1,0:T(8,128)(2,1)S(1)}, bf16[16,8192]{1,0:T(8,128)(2,1)S(1)}, u32[]{:S(2)}, u32[]{:S(2)}) collective-permute-start(bf16[16,8192]{1,0:T(8,128)(2,1)S(1)} %pad_maximum_fusion.1), channel_id=1, source_target_pairs={{0,4},{1,5},{2,6},{3,7},{4,0},{5,1},{6,2},{7,3},{8,12},{9,13},{10,... | collective-permute-start | bytes 786440 | tf_op jit(solution)/shard_map/ppermute | solution.py:20
  39.3 19.8 %collective-permute-start.8 = (bf16[32,8192]{1,0:T(8,128)(2,1)}, bf16[32,8192]{1,0:T(8,128)(2,1)S(1)}, u32[]{:S(2)}, u32[]{:S(2)}) collective-permute-start(bf16[32,8192]{1,0:T(8,128)(2,1)} %pad_maximum_fusion), channel_id=1, source_target_pairs={{0,2},{1,3},{2,0},{3,1},{4,6},{5,7},{6,4},{7,5},{8,10},{9,11},{10,... | collective-permute-start | bytes 1572872 | tf_op jit(solution)/shard_map/ppermute | solution.py:20
  62.7 15.0 %collective-permute-start.9 = (bf16[64,8192]{1,0:T(8,128)(2,1)}, bf16[64,8192]{1,0:T(8,128)(2,1)}, u32[]{:S(2)}, u32[]{:S(2)}) collective-permute-start(bf16[64,8192]{1,0:T(8,128)(2,1)} %concatenate.34), channel_id=1, source_target_pairs={{0,1},{1,0},{2,3},{3,2},{4,5},{5,4},{6,7},{7,6},{8,9},{9,8},{10,11... | collective-permute-start | bytes 3145736 | tf_op jit(solution)/shard_map/ppermute | solution.py:20

commit v2 on v0

v2 whole, which is shorter than its diff:
```python
import functools

import jax
import jax.numpy as jnp
from jax import lax
from jax.experimental import pallas as pl
from jax.experimental.pallas import tpu as pltpu
from jax.sharding import PartitionSpec as P

HIGHEST = lax.Precision.HIGHEST
DAMP = 0.1
DEPTH = 2
VMEM = pltpu.MemorySpace.VMEM
SMEM = pltpu.MemorySpace.SMEM


def dot(a, b):
    return jnp.dot(a, b, preferred_element_type=jnp.float32)


def exact(a, b):
    return jnp.dot(a, b, precision=HIGHEST, preferred_element_type=jnp.float32)


def over_last(a, b):
    return lax.dot_general(a, b, (((1,), (1,)), ((), ())), preferred_element_type=jnp.float32)


def over_first(a, b):
    return lax.dot_general(a, b, (((0,), (0,)), ((), ())), preferred_element_type=jnp.float32)


def divisor(n, most):
    return max(d for d in range(1, most + 1) if n % d == 0)


def project_kernel(x_hbm, g_hbm, pin_hbm, pout_hbm, packed_ref, grads_ref, x, g, pin, pout, pin_t, both, sx, sg, sp):
    examples = x_hbm.shape[0]
    wide, narrow = pin.shape[0], pout.shape[0]
    chunks, rows = x.shape[:2]
    per = chunks // examples
    pin_copy = pltpu.make_async_copy(pin_hbm, pin, sp.at[0])
    pout_copy = pltpu.make_async_copy(pout_hbm, pout, sp.at[1])
    pin_copy.start()
    pout_copy.start()

    def place(i):
        return i // per, pl.ds(pl.multiple_of((i % per) * rows, rows), rows)

    def copies(i):
        return (
            pltpu.make_async_copy(x_hbm.at[place(i)], x.at[i], sx.at[i]),
            pltpu.make_async_copy(g_hbm.at[place(i)], g.at[i], sg.at[i]),
        )

    for i in range(min(DEPTH, chunks)):
        for copy in copies(i):
            copy.start()
    pin_copy.wait()
    pin_t[...] = pin[...].T
    pout_copy.wait()

    @pl.loop(0, chunks)
    def _(i):
        for copy in copies(i):
            copy.wait()

        @pl.when(i + DEPTH < chunks)
        def _():
            for copy in copies(i + DEPTH):
                copy.start()

        e, tokens = place(i)
        both[e, tokens, :wide] = dot(x[i], pin_t[...]).astype(jnp.bfloat16)
        both[e, tokens, wide:] = over_last(g[i], pout[...]).astype(jnp.bfloat16)

    for e in range(examples):
        sums = over_first(both[e], both[e])
        grads_ref[e] = sums[wide:, :wide]
        low = jnp.concatenate([sums[wide:, wide:], sums[narrow:wide, narrow:wide]], axis=1)
        if e == 0:
            packed_ref[:narrow] = sums[:narrow, :wide]
            packed_ref[narrow:] = low
        else:
            packed_ref[:narrow] += sums[:narrow, :wide]
            packed_ref[narrow:] += low


def project(x, g, pin, pout):
    examples, tokens, d = x.shape
    v = g.shape[2]
    wide, narrow = pin.shape[0], pout.shape[0]
    rows = divisor(tokens, 256)
    chunks = examples * (tokens // rows)
    return pl.pallas_call(
        project_kernel,
        out_shape=[
            jax.ShapeDtypeStruct((wide, wide), jnp.float32),
            jax.ShapeDtypeStruct((examples, narrow, wide), jnp.float32),
        ],
        in_specs=[pl.BlockSpec(memory_space=pl.ANY)] * 4,
        out_specs=[pl.BlockSpec(memory_space=VMEM)] * 2,
        scratch_shapes=[
            pltpu.VMEM((chunks, rows, d), x.dtype),
            pltpu.VMEM((chunks, rows, v), g.dtype),
            pltpu.VMEM((wide, d), pin.dtype),
            pltpu.VMEM((narrow, v), pout.dtype),
            pltpu.VMEM((d, wide), pin.dtype),
            pltpu.VMEM((examples, tokens, wide + narrow), jnp.bfloat16),
            pltpu.SemaphoreType.DMA((chunks,)),
            pltpu.SemaphoreType.DMA((chunks,)),
            pltpu.SemaphoreType.DMA((2,)),
        ],
        compiler_params=pltpu.CompilerParams(vmem_limit_bytes=60 * 2**20),
        name="project",
    )(x, g, pin, pout)


def factors(n):
    spread = n / (n + 2 * DAMP)
    result = []
    while spread > 2e-6:
        result.append(2 / (2 - spread * spread))
        spread = spread * spread / (2 - spread * spread)
    return result


def normalised(s):
    n = s.shape[0]
    eye = lax.broadcasted_iota(jnp.int32, (n, n), 0) == lax.broadcasted_iota(jnp.int32, (n, n), 1)
    diagonal = jnp.sum(jnp.where(eye, s, 0.0), axis=0, keepdims=True)
    mean = jnp.sum(diagonal, axis=1, keepdims=True) / n
    first = 2 / (n + 2 * DAMP)
    return (s / mean + jnp.where(eye, DAMP, 0.0)) * first, first / mean, eye


def precond_kernel(tokens, packed_ref, grads_ref, out_ref):
    wide = packed_ref.shape[0]
    examples, narrow, _ = grads_ref.shape
    upper = packed_ref[:narrow, :]
    lower = jnp.concatenate([upper[:, narrow:].T, packed_ref[narrow:, narrow:]], axis=1)
    yi, scale_in, _ = normalised(jnp.concatenate([upper, lower], axis=0))
    yo, scale_out, eye = normalised(packed_ref[narrow:, :narrow])
    w = grads_ref[...].reshape(examples * narrow, wide)
    xo = jnp.where(eye, 1.0, 0.0)
    wides, narrows = factors(wide), factors(narrow)
    for k in range(max(len(wides), len(narrows))):
        if k < len(wides):
            if k < len(wides) - 1:
                both = jnp.concatenate([yi, w], axis=0)
                both = wides[k] * (2 * both - exact(both, yi))
                yi, w = both[:wide], both[wide:]
            else:
                w = wides[k] * (2 * w - exact(w, yi))
        if k < len(narrows):
            if k < len(narrows) - 1:
                both = jnp.concatenate([yo, xo], axis=0)
                both = narrows[k] * (2 * both - exact(both, yo))
                yo, xo = both[:narrow], both[narrow:]
            else:
                xo = narrows[k] * (2 * xo - exact(xo, yo))
    scale = (scale_in * tokens) * (scale_out * tokens)
    for e in range(examples):
        both = exact(xo, w[e * narrow : (e + 1) * narrow]) * scale
        out_ref[e] = both.astype(jnp.bfloat16).astype(jnp.float32)


def precondition(packed, grads, tokens):
    return pl.pallas_call(
        functools.partial(precond_kernel, float(tokens)),
        out_shape=jax.ShapeDtypeStruct(grads.shape, jnp.float32),
        in_specs=[pl.BlockSpec(memory_space=VMEM)] * 2,
        out_specs=pl.BlockSpec(memory_space=VMEM),
        name="precondition",
    )(packed, grads)


def score_kernel(sources, scale, me_ref, p_ref, *refs):
    pieces, out_ref = refs[:-1], refs[-1]
    examples, narrow, wide = p_ref.shape
    tests = out_ref.shape[1]
    me = me_ref[0]
    lane = lax.broadcasted_iota(jnp.int32, (1, tests), 1)
    for e in range(examples):

        def add(o, sums):
            p = p_ref[e, pl.ds(o, 1), :]
            here = pl.ds(pl.multiple_of(o * wide, wide), wide)
            return tuple(s + t[:, here].astype(jnp.float32) * p for s, t in zip(sums, pieces))

        zeros = tuple(jnp.zeros((t.shape[0], wide), jnp.float32) for t in pieces)
        sums = lax.fori_loop(0, narrow, add, zeros, unroll=4)
        total = jnp.zeros((1, tests), jnp.float32)
        for s, offsets in zip(sums, sources):
            rows = s.shape[0]
            per = rows // len(offsets)
            row = lax.broadcasted_iota(jnp.int32, (rows, 1), 0)
            target = jnp.zeros((rows, 1), jnp.int32)
            for i, offset in enumerate(offsets):
                inside = (row >= i * per) & (row < (i + 1) * per)
                target = jnp.where(inside, (me ^ offset) * per + row - i * per, target)
            by_row = jnp.sum(s, axis=1, keepdims=True)
            total += jnp.sum(jnp.where(target == lane, by_row, 0.0), axis=0, keepdims=True)
        out_ref[pl.ds(e, 1), :] = total * scale


def score(me, precond, pieces, sources, scale):
    tests = sum(t.shape[0] for t in pieces)
    return pl.pallas_call(
        functools.partial(score_kernel, sources, scale),
        out_shape=jax.ShapeDtypeStruct((precond.shape[0], tests), jnp.float32),
        in_specs=[pl.BlockSpec(memory_space=SMEM)] + [pl.BlockSpec(memory_space=VMEM)] * (1 + len(pieces)),
        out_specs=pl.BlockSpec(memory_space=VMEM),
        compiler_params=pltpu.CompilerParams(vmem_limit_bytes=32 * 2**20),
        name="score",
    )(me, precond, *pieces)


def exchange(x, bit, devices):
    return lax.ppermute(x, "ex", [(i, i ^ bit) for i in range(devices)])


def sum_over_devices(x, devices):
    bit = 1
    while bit < devices:
        x = x + exchange(x, bit, devices)
        bit *= 2
    return x


def gather_tests(tests, devices):
    offsets = [0]
    bit = devices // 2
    while bit > 4:
        tests = jnp.concatenate([tests, exchange(tests, bit, devices)], axis=0)
        offsets = offsets + [k ^ bit for k in offsets]
        bit //= 2
    pieces = [(tests, offsets)]
    if bit == 4:
        half, rows = len(offsets) // 2, tests.shape[0] // 2
        a, a_off = exchange(tests, 2, devices), [k ^ 2 for k in offsets]
        b, b_off = exchange(tests, 4, devices), [k ^ 4 for k in offsets]
        pieces += [(a, a_off), (b, b_off)]
        if half:
            pieces.append((exchange(b[:rows], 2, devices), [k ^ 2 for k in b_off[:half]]))
            pieces.append((exchange(a[rows:], 4, devices), [k ^ 4 for k in a_off[half:]]))
        else:
            pieces.append((exchange(b, 2, devices), [k ^ 2 for k in b_off]))
        bit = 1
    while bit:
        pieces += [(exchange(t, bit, devices), [k ^ bit for k in off]) for t, off in pieces]
        bit //= 2
    return [t for t, _ in pieces], [off for _, off in pieces]


def on_device(example_inputs, output_grads, proj_in, proj_out, test_grads):
    examples, tokens, _ = example_inputs.shape
    wide, narrow = proj_in.shape[0], proj_out.shape[0]
    devices = lax.axis_size("ex")
    me = lax.axis_index("ex").astype(jnp.int32)
    packed, grads = project(example_inputs, output_grads, proj_in, proj_out)
    if devices & (devices - 1):
        packed = lax.psum(packed, "ex")
        pieces = [lax.all_gather(test_grads, "ex", axis=0, tiled=True)]
        sources = [list(range(devices))]
        me = me * 0
    else:
        packed = sum_over_devices(packed, devices)
        pieces, sources = gather_tests(test_grads, devices)
    precond = precondition(packed, grads, examples * tokens * devices)
    scale = 4.0 / (wide * narrow * tokens) ** 0.5
    return score(me[None], precond, pieces, sources, scale)


def solution(mesh):
    return jax.shard_map(
        on_device,
        mesh=mesh,
        in_specs=(
            P(("grp", "ex"), None, None),
            P(("grp", "ex"), None, None),
            P(),
            P(),
            P("ex", None),
        ),
        out_specs=P(("grp", "ex"), None),
        check_vma=False,
    )
```

time: 208 us -> 52.1 us (0.25)
  waiting for transfers between devices: 96.5 us -> 13.4 us
  blocking collectives: 41.3 us -> 0 us
  other arithmetic: 38.8 us -> 2.53 us
  starting transfers between devices: 0.04 us -> 23 us
  between operations: 14.9 us -> 0.1 us
  matrix products: 12.2 us -> 0 us
  Pallas kernels: 0 us -> 11.9 us
  local copies, waits for them, and re-layouts: 4.16 us -> 0.77 us
    psum x1 -> x0, waiting for transfers between devices: 64.5 us -> none  [on_device(): sum_in, sum_out = lax.psum((local_in, local_out), 'ex')]
    psum x1 -> x0, blocking collectives: 41.3 us -> none  [on_device(): sum_in, sum_out = lax.psum((local_in, local_out), 'ex')]
    another operation x10 -> x0, other arithmetic: 34.9 us -> none  [the longest x6 18.9 us: damped_inverse(): factor = jnp.linalg.cholesky(damped)]
    all_gather x1 -> x0, waiting for transfers between devices: 31.3 us -> none  [on_device(): lax.all_gather(test_grads, 'ex', axis=0, tiled=True)]
    ppermute x0 -> x16, starting transfers between devices: none -> 23 us  [exchange(): return lax.ppermute(x, 'ex', [(i, i ^ bit) for i in range(devices)])]
    ppermute x0 -> x16, waiting for transfers between devices: none -> 13.4 us  [exchange(): return lax.ppermute(x, 'ex', [(i, i ^ bit) for i in range(devices)])]
    pallas_call x0 -> x3, Pallas kernels: none -> 11.9 us  [the longest x1 6.62 us: project(): pl.pallas_call(project_kernel, out_shape=[jax.ShapeDtypeStruct((wide, wid...]
    dot_general x10 -> x0, matrix products: 11.7 us -> none  [the longest x1 6.09 us: on_device(): jnp.einsum('etd,kd->etk', example_inputs, proj_in, preferred_element_type...]
  transfers between devices with their start and end apart: 2 -> 16, of which waited for: 2 -> 7; matrix products, arithmetic and copies ran while one was open for 20% -> 3% of each run, Pallas kernels for 0% -> 21%
where the time goes in v2:
time: 52.1 us; the launch traced here: 51.8 us
  starting transfers between devices  23 us (44%)
  waiting for transfers between devices  13.4 us (26%)
  Pallas kernels  11.9 us (23%)
  other arithmetic  2.53 us (5%)
  local copies, waits for them, and re-layouts  0.77 us (1%)
    ppermute x16, starting transfers between devices, exchange(): return lax.ppermute(x, 'ex', [(i, i ^ bit) for i in range(devices)])  23 us
    ppermute x16, waiting for transfers between devices, exchange(): return lax.ppermute(x, 'ex', [(i, i ^ bit) for i in range(devices)])  13.4 us
    pallas_call x1, Pallas kernels, project(): pl.pallas_call(project_kernel, out_shape=[jax.ShapeDtypeStruct((wide, wid...  6.62 us
    pallas_call x1, Pallas kernels, precondition(): pl.pallas_call(functools.partial(precond_kernel, float(tokens)), out_shap...  4.02 us
    add x5, other arithmetic, sum_over_devices(): x = x + exchange(x, bit, devices)  1.52 us
    pallas_call x1, Pallas kernels, score(): pl.pallas_call(functools.partial(score_kernel, sources, scale), out_shape...  1.27 us
  transfers between devices with their start and end apart: 16, of which 7 were waited for; matrix products, arithmetic and copies ran while one was open for 3% of the time, Pallas kernels for 21%

profile of v2, /device:TPU:1, one launch (start us, length us, event | category | flops | bytes accessed | tf_op | source)
XLA Modules:
  0.0 51.8 jit_solution(15250474332547240917)
XLA Ops:
  0.0 0.0 copy-start.1
  0.0 3.1 %collective-permute-start.5 = (bf16[4,8192]{1,0:T(4,128)(2,1)}, bf16[4,8192]{1,0:T(4,128)(2,1)S(1)}, u32[]{:S(2)}, u32[]{:S(2)}) collective-permute-start(bf16[4,8192]{1,0:T(4,128)(2,1)} %param.9), channel_id=1, source_target_pairs={{0,16},{1,17},{2,18},{3,19},{4,20},{5,21},{6,22},{7,23},{8,24},{9,... | collective-permute-start | bytes 196616 | tf_op jit(solution)/shard_map/ppermute | solution.py:220
  3.1 1.9 %collective-permute-done.5 = bf16[4,8192]{1,0:T(4,128)(2,1)S(1)} collective-permute-done((bf16[4,8192]{1,0:T(4,128)(2,1)}, bf16[4,8192]{1,0:T(4,128)(2,1)S(1)}, u32[]{:S(2)}, u32[]{:S(2)}) %collective-permute-start.5) | collective-permute-done | bytes 65568 | tf_op jit(solution)/shard_map/ppermute | solution.py:220
  5.1 0.9 %pad_maximum_fusion.1 = bf16[8,8192]{1,0:T(8,128)(2,1)S(1)} fusion(bf16[4,8192]{1,0:T(4,128)(2,1)S(1)} %collective-permute-done.5, bf16[4,8192]{1,0:T(4,128)(2,1)} %param.9), kind=kLoop, calls=%fused_computation.1 | loop fusion | flops 262144 | bytes 262144 | tf_op jit(solution)/shard_map/concatenate | solution.py:235
  6.0 2.4 %collective-permute-start.6 = (bf16[8,8192]{1,0:T(8,128)(2,1)S(1)}, bf16[8,8192]{1,0:T(8,128)(2,1)S(1)}, u32[]{:S(2)}, u32[]{:S(2)}) collective-permute-start(bf16[8,8192]{1,0:T(8,128)(2,1)S(1)} %pad_maximum_fusion.1), channel_id=1, source_target_pairs={{0,8},{1,9},{2,10},{3,11},{4,12},{5,13},{6,14},{7,15},{8,0},{9,1},... | collective-permute-start | bytes 393224 | tf_op jit(solution)/shard_map/ppermute | solution.py:220
  8.3 6.6 %project.1 = (f32[128,128]{1,0:T(8,128)}, f32[1,64,128]{2,1,0:T(8,128)}) custom-call(bf16[1,1024,4096]{2,1,0:T(8,128)(2,1)} %x_hbm.1, bf16[1,1024,1024]{2,1,0:T(8,128)(2,1)} %g_hbm.1, bf16[128,4096]{1,0:T(8,128)(2,1)} %pin_hbm.1, bf16[64,1024]{1,0:T(8,128)(2,1)} %pout_hbm.1), custom_call_target="tpu_custom_call" | custom-call | tf_op jit(solution)/shard_map/project/pallas_call | solution.py:95
  15.0 1.3 %collective-permute-start = (f32[128,128]{1,0:T(8,128)}, f32[128,128]{1,0:T(8,128)S(1)}, u32[]{:S(2)}, u32[]{:S(2)}) collective-permute-start(f32[128,128]{1,0:T(8,128)} %get-tuple-element.7), channel_id=1, source_target_pairs={{0,1},{1,0},{2,3},{3,2},{4,5},{5,4},{6,7},{7,6},{8,9},{9,8},{10,11... | collective-permute-start | bytes 196616 | tf_op jit(solution)/shard_map/ppermute | solution.py:220
  16.3 1.1 %collective-permute-done = f32[128,128]{1,0:T(8,128)S(1)} collective-permute-done((f32[128,128]{1,0:T(8,128)}, f32[128,128]{1,0:T(8,128)S(1)}, u32[]{:S(2)}, u32[]{:S(2)}) %collective-permute-start) | collective-permute-done | bytes 65568 | tf_op jit(solution)/shard_map/ppermute | solution.py:220
  17.4 0.9 %add.15 = f32[128,128]{1,0:T(8,128)S(1)} add(f32[128,128]{1,0:T(8,128)} %get-tuple-element.7, f32[128,128]{1,0:T(8,128)S(1)} %collective-permute-done) | non-fusion elementwise | flops 16384 | bytes 196608 | tf_op jit(solution)/shard_map/add | solution.py:226
  18.3 0.0 collective-permute-done.6
  18.3 0.0 copy-done.1
  18.3 0.1 pad_maximum_fusion.refs_0_
  18.4 1.3 %collective-permute-start.8 = (bf16[16,8192]{1,0:T(8,128)(2,1)S(1)}, bf16[16,8192]{1,0:T(8,128)(2,1)S(1)}, u32[]{:S(2)}, u32[]{:S(2)}) collective-permute-start(bf16[16,8192]{1,0:T(8,128)(2,1)S(1)} %pad_maximum_fusion.refs_0_), channel_id=1, source_target_pairs={{0,4},{1,5},{2,6},{3,7},{4,0},{5,1},{6,2},{7,3},{8,12},{9,13},{10,... | collective-permute-start | bytes 786440 | tf_op jit(solution)/shard_map/ppermute | solution.py:220
  19.7 1.2 %collective-permute-start.1 = (f32[128,128]{1,0:T(8,128)S(1)}, f32[128,128]{1,0:T(8,128)S(1)}, u32[]{:S(2)}, u32[]{:S(2)}) collective-permute-start(f32[128,128]{1,0:T(8,128)S(1)} %add.15), channel_id=1, source_target_pairs={{0,2},{1,3},{2,0},{3,1},{4,6},{5,7},{6,4},{7,5},{8,10},{9,11},{10,... | collective-permute-start | bytes 196616 | tf_op jit(solution)/shard_map/ppermute | solution.py:220
  20.9 0.3 collective-permute-start.7
  21.2 1.9 %collective-permute-done.1 = f32[128,128]{1,0:T(8,128)S(1)} collective-permute-done((f32[128,128]{1,0:T(8,128)S(1)}, f32[128,128]{1,0:T(8,128)S(1)}, u32[]{:S(2)}, u32[]{:S(2)}) %collective-permute-start.1) | collective-permute-done | bytes 65568 | tf_op jit(solution)/shard_map/ppermute | solution.py:220
  23.1 0.3 collective-permute-start.2
  23.4 4.0 %collective-permute-done.2 = f32[128,128]{1,0:T(8,128)S(1)} collective-permute-done((f32[128,128]{1,0:T(8,128)S(1)}, f32[128,128]{1,0:T(8,128)S(1)}, u32[]{:S(2)}, u32[]{:S(2)}) %collective-permute-start.2) | collective-permute-done | bytes 65568 | tf_op jit(solution)/shard_map/ppermute | solution.py:220
  27.4 1.3 %collective-permute-start.3 = (f32[128,128]{1,0:T(8,128)S(1)}, f32[128,128]{1,0:T(8,128)S(1)}, u32[]{:S(2)}, u32[]{:S(2)}) collective-permute-start(f32[128,128]{1,0:T(8,128)S(1)} %add.17), channel_id=1, source_target_pairs={{0,8},{1,9},{2,10},{3,11},{4,12},{5,13},{6,14},{7,15},{8,0},{9,1},... | collective-permute-start | bytes 196616 | tf_op jit(solution)/shard_map/ppermute | solution.py:220
  28.7 1.9 %collective-permute-done.3 = f32[128,128]{1,0:T(8,128)S(1)} collective-permute-done((f32[128,128]{1,0:T(8,128)S(1)}, f32[128,128]{1,0:T(8,128)S(1)}, u32[]{:S(2)}, u32[]{:S(2)}) %collective-permute-start.3) | collective-permute-done | bytes 65568 | tf_op jit(solution)/shard_map/ppermute | solution.py:220
  30.6 3.1 %collective-permute-start.4 = (f32[128,128]{1,0:T(8,128)S(1)}, f32[128,128]{1,0:T(8,128)S(1)}, u32[]{:S(2)}, u32[]{:S(2)}) collective-permute-start(f32[128,128]{1,0:T(8,128)S(1)} %add.18), channel_id=1, source_target_pairs={{0,16},{1,17},{2,18},{3,19},{4,20},{5,21},{6,22},{7,23},{8,24},{9,... | collective-permute-start | bytes 196616 | tf_op jit(solution)/shard_map/ppermute | solution.py:220
  33.7 4.0 %collective-permute-start.11 = (bf16[16,8192]{1,0:T(8,128)(2,1)S(1)}, bf16[16,8192]{1,0:T(8,128)(2,1)S(1)}, u32[]{:S(2)}, u32[]{:S(2)}) collective-permute-start(bf16[16,8192]{1,0:T(8,128)(2,1)S(1)} %pad_maximum_fusion.refs_0_), channel_id=1, source_target_pairs={{0,1},{1,0},{2,3},{3,2},{4,5},{5,4},{6,7},{7,6},{8,9},{9,8},{10,11... | collective-permute-start | bytes 786440 | tf_op jit(solution)/shard_map/ppermute | solution.py:220
  37.7 0.0 collective-permute-done.8.refs_2_
  37.7 1.3 %collective-permute-start.9 = (bf16[8,8192]{1,0:T(8,128)(2,1)S(1)}, bf16[8,8192]{1,0:T(8,128)(2,1)S(1)}, u32[]{:S(2)}, u32[]{:S(2)}) collective-permute-start(bf16[8,8192]{1,0:T(8,128)(2,1)S(1)} %slice.8), channel_id=1, source_target_pairs={{0,2},{1,3},{2,0},{3,1},{4,6},{5,7},{6,4},{7,5},{8,10},{9,11},{10,... | collective-permute-start | bytes 393224 | tf_op jit(solution)/shard_map/ppermute | solution.py:220
  39.0 0.0 collective-permute-done.7.refs_1_
  39.1 0.1 collective-permute-start.10
  39.1 0.4 collective-permute-start.12
  39.6 0.0 collective-permute-done.4
  39.6 1.0 %collective-permute-start.13 = (bf16[16,8192]{1,0:T(8,128)(2,1)S(1)}, bf16[16,8192]{1,0:T(8,128)(2,1)S(1)}, u32[]{:S(2)}, u32[]{:S(2)}) collective-permute-start(bf16[16,8192]{1,0:T(8,128)(2,1)S(1)} %collective-permute-done.8.refs_2_), channel_id=1, source_target_pairs={{0,1},{1,0},{2,3},{3,2},{4,5},{5,4},{6,7},{7,6},{8,9},{9,8},{10,11... | collective-permute-start | bytes 786440 | tf_op jit(solution)/shard_map/ppermute | solution.py:220
  40.6 2.3 %collective-permute-done.9.refs_3_ = bf16[8,8192]{1,0:T(8,128)(2,1)S(1)} collective-permute-done((bf16[8,8192]{1,0:T(8,128)(2,1)S(1)}, bf16[8,8192]{1,0:T(8,128)(2,1)S(1)}, u32[]{:S(2)}, u32[]{:S(2)}) %collective-permute-start.9) | collective-permute-done | bytes 131104 | tf_op jit(solution)/shard_map/ppermute | solution.py:220
  42.9 0.8 %collective-permute-start.14 = (bf16[8,8192]{1,0:T(8,128)(2,1)S(1)}, bf16[8,8192]{1,0:T(8,128)(2,1)S(1)}, u32[]{:S(2)}, u32[]{:S(2)}) collective-permute-start(bf16[8,8192]{1,0:T(8,128)(2,1)S(1)} %collective-permute-done.9.refs_3_), channel_id=1, source_target_pairs={{0,1},{1,0},{2,3},{3,2},{4,5},{5,4},{6,7},{7,6},{8,9},{9,8},{10,11... | collective-permute-start | bytes 393224 | tf_op jit(solution)/shard_map/ppermute | solution.py:220
  43.7 0.3 collective-permute-done.10.refs_4_
  43.9 1.1 %collective-permute-start.15 = (bf16[8,8192]{1,0:T(8,128)(2,1)S(1)}, bf16[8,8192]{1,0:T(8,128)(2,1)S(1)}, u32[]{:S(2)}, u32[]{:S(2)}) collective-permute-start(bf16[8,8192]{1,0:T(8,128)(2,1)S(1)} %collective-permute-done.10.refs_4_), channel_id=1, source_target_pairs={{0,1},{1,0},{2,3},{3,2},{4,5},{5,4},{6,7},{7,6},{8,9},{9,8},{10,11... | collective-permute-start | bytes 393224 | tf_op jit(solution)/shard_map/ppermute | solution.py:220
  45.0 0.6 %add.19.packed_ref = f32[128,128]{1,0:T(8,128)} add(f32[128,128]{1,0:T(8,128)S(1)} %add.18, f32[128,128]{1,0:T(8,128)S(1)} %collective-permute-done.4) | non-fusion elementwise | flops 16384 | bytes 196608 | tf_op jit(solution)/shard_map/add | solution.py:226
  45.7 4.0 %precondition.1.p_ref = f32[1,64,128]{2,1,0:T(8,128)} custom-call(f32[128,128]{1,0:T(8,128)} %add.19.packed_ref, f32[1,64,128]{2,1,0:T(8,128)} %get-tuple-element.8.grads_ref), custom_call_target="tpu_custom_call" | custom-call | tf_op jit(solution)/shard_map/precondition/pallas_call | solution.py:169
  49.7 0.0 collective-permute-done.11.refs_5_
  49.7 0.0 collective-permute-done.14.refs_8_
  49.7 0.0 collective-permute-done.15.refs_9_
  49.7 0.0 collective-permute-done.12.refs_6_
  49.7 0.0 collective-permute-done.13.refs_7_
  49.7 0.0 copy-start
  49.7 0.7 %copy-done = f32[1,64,128]{2,1,0:T(8,128)S(1)} copy-done((f32[1,64,128]{2,1,0:T(8,128)S(1)}, f32[1,64,128]{2,1,0:T(8,128)}, u32[]{:S(2)}) %copy-start) | copy-done | bytes 32792
  50.5 1.3 %score.1 = f32[1,128]{1,0:T(1,128)} custom-call(s32[1]{0:T(128)} %bitcast.me_ref, f32[1,64,128]{2,1,0:T(8,128)S(1)} %copy-done, bf16[16,8192]{1,0:T(8,128)(2,1)S(1)} %pad_maximum_fusion.refs_0_, bf16[16,8192]{1,0:T(8,128)(2,1)S(1)} %collective-permute-done.7.refs_1_, bf16[16,8192]{1,0:T(8,128)(2,1)S(1)} %collective-permute-done.8.refs_2_, ...), custom_call_target="tpu_custom_call" | custom-call | tf_op jit(solution)/shard_map/score/pallas_call | solution.py:209
  (5 shorter events, 0.0 us)
Async XLA Ops:
  0.0 18.3 %copy-start.1 = (bf16[4,8192]{1,0:T(4,128)(2,1)S(1)}, bf16[4,8192]{1,0:T(4,128)(2,1)}, u32[]{:S(2)}) copy-start(bf16[4,8192]{1,0:T(4,128)(2,1)} %param.9) | copy-start | bytes 196612
  0.0 5.1 %collective-permute-start.5 = (bf16[4,8192]{1,0:T(4,128)(2,1)}, bf16[4,8192]{1,0:T(4,128)(2,1)S(1)}, u32[]{:S(2)}, u32[]{:S(2)}) collective-permute-start(bf16[4,8192]{1,0:T(4,128)(2,1)} %param.9), channel_id=1, source_target_pairs={{0,16},{1,17},{2,18},{3,19},{4,20},{5,21},{6,22},{7,23},{8,24},{9,... | collective-permute-start | bytes 196616 | tf_op jit(solution)/shard_map/ppermute | solution.py:220
  6.0 12.3 %collective-permute-start.6 = (bf16[8,8192]{1,0:T(8,128)(2,1)S(1)}, bf16[8,8192]{1,0:T(8,128)(2,1)S(1)}, u32[]{:S(2)}, u32[]{:S(2)}) collective-permute-start(bf16[8,8192]{1,0:T(8,128)(2,1)S(1)} %pad_maximum_fusion.1), channel_id=1, source_target_pairs={{0,8},{1,9},{2,10},{3,11},{4,12},{5,13},{6,14},{7,15},{8,0},{9,1},... | collective-permute-start | bytes 393224 | tf_op jit(solution)/shard_map/ppermute | solution.py:220
  15.0 2.4 %collective-permute-start = (f32[128,128]{1,0:T(8,128)}, f32[128,128]{1,0:T(8,128)S(1)}, u32[]{:S(2)}, u32[]{:S(2)}) collective-permute-start(f32[128,128]{1,0:T(8,128)} %get-tuple-element.7), channel_id=1, source_target_pairs={{0,1},{1,0},{2,3},{3,2},{4,5},{5,4},{6,7},{7,6},{8,9},{9,8},{10,11... | collective-permute-start | bytes 196616 | tf_op jit(solution)/shard_map/ppermute | solution.py:220
  18.4 19.3 %collective-permute-start.8 = (bf16[16,8192]{1,0:T(8,128)(2,1)S(1)}, bf16[16,8192]{1,0:T(8,128)(2,1)S(1)}, u32[]{:S(2)}, u32[]{:S(2)}) collective-permute-start(bf16[16,8192]{1,0:T(8,128)(2,1)S(1)} %pad_maximum_fusion.refs_0_), channel_id=1, source_target_pairs={{0,4},{1,5},{2,6},{3,7},{4,0},{5,1},{6,2},{7,3},{8,12},{9,13},{10,... | collective-permute-start | bytes 786440 | tf_op jit(solution)/shard_map/ppermute | solution.py:220
  19.7 3.4 %collective-permute-start.1 = (f32[128,128]{1,0:T(8,128)S(1)}, f32[128,128]{1,0:T(8,128)S(1)}, u32[]{:S(2)}, u32[]{:S(2)}) collective-permute-start(f32[128,128]{1,0:T(8,128)S(1)} %add.15), channel_id=1, source_target_pairs={{0,2},{1,3},{2,0},{3,1},{4,6},{5,7},{6,4},{7,5},{8,10},{9,11},{10,... | collective-permute-start | bytes 196616 | tf_op jit(solution)/shard_map/ppermute | solution.py:220
  20.9 18.1 %collective-permute-start.7 = (bf16[16,8192]{1,0:T(8,128)(2,1)S(1)}, bf16[16,8192]{1,0:T(8,128)(2,1)S(1)}, u32[]{:S(2)}, u32[]{:S(2)}) collective-permute-start(bf16[16,8192]{1,0:T(8,128)(2,1)S(1)} %pad_maximum_fusion.refs_0_), channel_id=1, source_target_pairs={{0,2},{1,3},{2,0},{3,1},{4,6},{5,7},{6,4},{7,5},{8,10},{9,11},{10,... | collective-permute-start | bytes 786440 | tf_op jit(solution)/shard_map/ppermute | solution.py:220
  23.1 4.3 %collective-permute-start.2 = (f32[128,128]{1,0:T(8,128)S(1)}, f32[128,128]{1,0:T(8,128)S(1)}, u32[]{:S(2)}, u32[]{:S(2)}) collective-permute-start(f32[128,128]{1,0:T(8,128)S(1)} %add.16), channel_id=1, source_target_pairs={{0,4},{1,5},{2,6},{3,7},{4,0},{5,1},{6,2},{7,3},{8,12},{9,13},{10,... | collective-permute-start | bytes 196616 | tf_op jit(solution)/shard_map/ppermute | solution.py:220
  27.4 3.2 %collective-permute-start.3 = (f32[128,128]{1,0:T(8,128)S(1)}, f32[128,128]{1,0:T(8,128)S(1)}, u32[]{:S(2)}, u32[]{:S(2)}) collective-permute-start(f32[128,128]{1,0:T(8,128)S(1)} %add.17), channel_id=1, source_target_pairs={{0,8},{1,9},{2,10},{3,11},{4,12},{5,13},{6,14},{7,15},{8,0},{9,1},... | collective-permute-start | bytes 196616 | tf_op jit(solution)/shard_map/ppermute | solution.py:220
  30.6 9.0 %collective-permute-start.4 = (f32[128,128]{1,0:T(8,128)S(1)}, f32[128,128]{1,0:T(8,128)S(1)}, u32[]{:S(2)}, u32[]{:S(2)}) collective-permute-start(f32[128,128]{1,0:T(8,128)S(1)} %add.18), channel_id=1, source_target_pairs={{0,16},{1,17},{2,18},{3,19},{4,20},{5,21},{6,22},{7,23},{8,24},{9,... | collective-permute-start | bytes 196616 | tf_op jit(solution)/shard_map/ppermute | solution.py:220
  33.7 16.0 %collective-permute-start.11 = (bf16[16,8192]{1,0:T(8,128)(2,1)S(1)}, bf16[16,8192]{1,0:T(8,128)(2,1)S(1)}, u32[]{:S(2)}, u32[]{:S(2)}) collective-permute-start(bf16[16,8192]{1,0:T(8,128)(2,1)S(1)} %pad_maximum_fusion.refs_0_), channel_id=1, source_target_pairs={{0,1},{1,0},{2,3},{3,2},{4,5},{5,4},{6,7},{7,6},{8,9},{9,8},{10,11... | collective-permute-start | bytes 786440 | tf_op jit(solution)/shard_map/ppermute | solution.py:220
  37.7 5.2 %collective-permute-start.9 = (bf16[8,8192]{1,0:T(8,128)(2,1)S(1)}, bf16[8,8192]{1,0:T(8,128)(2,1)S(1)}, u32[]{:S(2)}, u32[]{:S(2)}) collective-permute-start(bf16[8,8192]{1,0:T(8,128)(2,1)S(1)} %slice.8), channel_id=1, source_target_pairs={{0,2},{1,3},{2,0},{3,1},{4,6},{5,7},{6,4},{7,5},{8,10},{9,11},{10,... | collective-permute-start | bytes 393224 | tf_op jit(solution)/shard_map/ppermute | solution.py:220
  39.1 4.9 %collective-permute-start.10 = (bf16[8,8192]{1,0:T(8,128)(2,1)S(1)}, bf16[8,8192]{1,0:T(8,128)(2,1)S(1)}, u32[]{:S(2)}, u32[]{:S(2)}) collective-permute-start(bf16[8,8192]{1,0:T(8,128)(2,1)S(1)} %slice.9), channel_id=1, source_target_pairs={{0,4},{1,5},{2,6},{3,7},{4,0},{5,1},{6,2},{7,3},{8,12},{9,13},{10,... | collective-permute-start | bytes 393224 | tf_op jit(solution)/shard_map/ppermute | solution.py:220
  39.1 10.6 %collective-permute-start.12 = (bf16[16,8192]{1,0:T(8,128)(2,1)S(1)}, bf16[16,8192]{1,0:T(8,128)(2,1)S(1)}, u32[]{:S(2)}, u32[]{:S(2)}) collective-permute-start(bf16[16,8192]{1,0:T(8,128)(2,1)S(1)} %collective-permute-done.7.refs_1_), channel_id=1, source_target_pairs={{0,1},{1,0},{2,3},{3,2},{4,5},{5,4},{6,7},{7,6},{8,9},{9,8},{10,11... | collective-permute-start | bytes 786440 | tf_op jit(solution)/shard_map/ppermute | solution.py:220
  39.6 10.1 %collective-permute-start.13 = (bf16[16,8192]{1,0:T(8,128)(2,1)S(1)}, bf16[16,8192]{1,0:T(8,128)(2,1)S(1)}, u32[]{:S(2)}, u32[]{:S(2)}) collective-permute-start(bf16[16,8192]{1,0:T(8,128)(2,1)S(1)} %collective-permute-done.8.refs_2_), channel_id=1, source_target_pairs={{0,1},{1,0},{2,3},{3,2},{4,5},{5,4},{6,7},{7,6},{8,9},{9,8},{10,11... | collective-permute-start | bytes 786440 | tf_op jit(solution)/shard_map/ppermute | solution.py:220
  42.9 6.8 %collective-permute-start.14 = (bf16[8,8192]{1,0:T(8,128)(2,1)S(1)}, bf16[8,8192]{1,0:T(8,128)(2,1)S(1)}, u32[]{:S(2)}, u32[]{:S(2)}) collective-permute-start(bf16[8,8192]{1,0:T(8,128)(2,1)S(1)} %collective-permute-done.9.refs_3_), channel_id=1, source_target_pairs={{0,1},{1,0},{2,3},{3,2},{4,5},{5,4},{6,7},{7,6},{8,9},{9,8},{10,11... | collective-permute-start | bytes 393224 | tf_op jit(solution)/shard_map/ppermute | solution.py:220
  43.9 5.8 %collective-permute-start.15 = (bf16[8,8192]{1,0:T(8,128)(2,1)S(1)}, bf16[8,8192]{1,0:T(8,128)(2,1)S(1)}, u32[]{:S(2)}, u32[]{:S(2)}) collective-permute-start(bf16[8,8192]{1,0:T(8,128)(2,1)S(1)} %collective-permute-done.10.refs_4_), channel_id=1, source_target_pairs={{0,1},{1,0},{2,3},{3,2},{4,5},{5,4},{6,7},{7,6},{8,9},{9,8},{10,11... | collective-permute-start | bytes 393224 | tf_op jit(solution)/shard_map/ppermute | solution.py:220
  49.7 0.8 %copy-start = (f32[1,64,128]{2,1,0:T(8,128)S(1)}, f32[1,64,128]{2,1,0:T(8,128)}, u32[]{:S(2)}) copy-start(f32[1,64,128]{2,1,0:T(8,128)} %precondition.1.p_ref) | copy-start | bytes 98308

commit v3 on v2

--- a/solution.py
+++ b/solution.py
@@ -95,8 +95,8 @@
     return pl.pallas_call(
         project_kernel,
         out_shape=[
-            jax.ShapeDtypeStruct((wide, wide), jnp.float32),
-            jax.ShapeDtypeStruct((examples, narrow, wide), jnp.float32),
+            pltpu.VMEM((wide, wide), jnp.float32),
+            pltpu.VMEM((examples, narrow, wide), jnp.float32),
         ],
         in_specs=[pl.BlockSpec(memory_space=pl.ANY)] * 4,
         out_specs=[pl.BlockSpec(memory_space=VMEM)] * 2,
@@ -134,13 +134,14 @@
     return (s / mean + jnp.where(eye, DAMP, 0.0)) * first, first / mean, eye
 
 
-def precond_kernel(tokens, packed_ref, grads_ref, out_ref):
-    wide = packed_ref.shape[0]
+def precond_kernel(tokens, here_ref, there_ref, grads_ref, out_ref):
+    wide = here_ref.shape[0]
     examples, narrow, _ = grads_ref.shape
-    upper = packed_ref[:narrow, :]
-    lower = jnp.concatenate([upper[:, narrow:].T, packed_ref[narrow:, narrow:]], axis=1)
+    packed = here_ref[...] + there_ref[...]
+    upper = packed[:narrow]
+    lower = jnp.concatenate([upper[:, narrow:].T, packed[narrow:, narrow:]], axis=1)
     yi, scale_in, _ = normalised(jnp.concatenate([upper, lower], axis=0))
-    yo, scale_out, eye = normalised(packed_ref[narrow:, :narrow])
+    yo, scale_out, eye = normalised(packed[narrow:, :narrow])
     w = grads_ref[...].reshape(examples * narrow, wide)
     xo = jnp.where(eye, 1.0, 0.0)
     wides, narrows = factors(wide), factors(narrow)
@@ -165,14 +166,14 @@
         out_ref[e] = both.astype(jnp.bfloat16).astype(jnp.float32)
 
 
-def precondition(packed, grads, tokens):
+def precondition(here, there, grads, tokens):
     return pl.pallas_call(
         functools.partial(precond_kernel, float(tokens)),
-        out_shape=jax.ShapeDtypeStruct(grads.shape, jnp.float32),
-        in_specs=[pl.BlockSpec(memory_space=VMEM)] * 2,
+        out_shape=pltpu.VMEM(grads.shape, jnp.float32),
+        in_specs=[pl.BlockSpec(memory_space=VMEM)] * 3,
         out_specs=pl.BlockSpec(memory_space=VMEM),
         name="precondition",
-    )(packed, grads)
+    )(*[pltpu.with_memory_space_constraint(a, VMEM) for a in (here, there, grads)])
 
 
 def score_kernel(sources, scale, me_ref, p_ref, *refs):
@@ -213,44 +214,48 @@
         out_specs=pl.BlockSpec(memory_space=VMEM),
         compiler_params=pltpu.CompilerParams(vmem_limit_bytes=32 * 2**20),
         name="score",
-    )(me, precond, *pieces)
+    )(me, *[pltpu.with_memory_space_constraint(a, VMEM) for a in (precond, *pieces)])
 
 
 def exchange(x, bit, devices):
     return lax.ppermute(x, "ex", [(i, i ^ bit) for i in range(devices)])
 
 
-def sum_over_devices(x, devices):
-    bit = 1
-    while bit < devices:
-        x = x + exchange(x, bit, devices)
+def join(tests, offsets, bit, devices):
+    both = jnp.concatenate([tests, exchange(tests, bit, devices)], axis=0)
+    return both, offsets + [k ^ bit for k in offsets]
+
+
+def exchange_all(packed, tests, tests_offsets, devices):
+    far = devices // 4
+    packed, tests = lax.optimization_barrier((packed, tests))
+    packed = packed + exchange(packed, 1, devices)
+    packed = packed + exchange(packed, 2, devices)
+    offsets = tests_offsets
+    while far > 4:
+        tests, offsets = join(tests, offsets, far, devices)
+        far //= 2
+    packed, tests = lax.optimization_barrier((packed, tests))
+    half, rows = len(offsets) // 2, tests.shape[0] // 2
+    a, a_off = exchange(tests, 2, devices), [k ^ 2 for k in offsets]
+    b, b_off = exchange(tests, 4, devices), [k ^ 4 for k in offsets]
+    packed = packed + exchange(packed, 4, devices)
+    packed = packed + exchange(packed, 8, devices)
+    bit = 16
+    while bit < devices // 2:
+        packed = packed + exchange(packed, bit, devices)
         bit *= 2
-    return x
-
-
-def gather_tests(tests, devices):
-    offsets = [0]
-    bit = devices // 2
-    while bit > 4:
-        tests = jnp.concatenate([tests, exchange(tests, bit, devices)], axis=0)
-        offsets = offsets + [k ^ bit for k in offsets]
-        bit //= 2
-    pieces = [(tests, offsets)]
-    if bit == 4:
-        half, rows = len(offsets) // 2, tests.shape[0] // 2
-        a, a_off = exchange(tests, 2, devices), [k ^ 2 for k in offsets]
-        b, b_off = exchange(tests, 4, devices), [k ^ 4 for k in offsets]
-        pieces += [(a, a_off), (b, b_off)]
-        if half:
-            pieces.append((exchange(b[:rows], 2, devices), [k ^ 2 for k in b_off[:half]]))
-            pieces.append((exchange(a[rows:], 4, devices), [k ^ 4 for k in a_off[half:]]))
-        else:
-            pieces.append((exchange(b, 2, devices), [k ^ 2 for k in b_off]))
-        bit = 1
-    while bit:
-        pieces += [(exchange(t, bit, devices), [k ^ bit for k in off]) for t, off in pieces]
-        bit //= 2
-    return [t for t, _ in pieces], [off for _, off in pieces]
+    packed, a, b = lax.optimization_barrier((packed, a, b))
+    pieces = [
+        (tests, offsets),
+        (a, a_off),
+        (b, b_off),
+        (exchange(b[:rows], 2, devices), [k ^ 2 for k in b_off[:half]]),
+        (exchange(a[rows:], 4, devices), [k ^ 4 for k in a_off[half:]]),
+    ]
+    pieces += [(exchange(t, 1, devices), [k ^ 1 for k in off]) for t, off in pieces]
+    there = exchange(packed, bit, devices)
+    return packed, there, [t for t, _ in pieces], [off for _, off in pieces]
 
 
 def on_device(example_inputs, output_grads, proj_in, proj_out, test_grads):
@@ -258,16 +263,20 @@
     wide, narrow = proj_in.shape[0], proj_out.shape[0]
     devices = lax.axis_size("ex")
     me = lax.axis_index("ex").astype(jnp.int32)
+    simple = devices < 32 or devices & (devices - 1)
+    if not simple:
+        far = exchange(test_grads, devices // 2, devices)
     packed, grads = project(example_inputs, output_grads, proj_in, proj_out)
-    if devices & (devices - 1):
-        packed = lax.psum(packed, "ex")
+    if simple:
+        here, there = lax.psum(packed, "ex"), jnp.zeros_like(packed)
         pieces = [lax.all_gather(test_grads, "ex", axis=0, tiled=True)]
         sources = [list(range(devices))]
         me = me * 0
     else:
-        packed = sum_over_devices(packed, devices)
-        pieces, sources = gather_tests(test_grads, devices)
-    precond = precondition(packed, grads, examples * tokens * devices)
+        packed, far = lax.optimization_barrier((packed, far))
+        tests = jnp.concatenate([test_grads, far], axis=0)
+        here, there, pieces, sources = exchange_all(packed, tests, [0, devices // 2], devices)
+    precond = precondition(here, there, grads, examples * tokens * devices)
     scale = 4.0 / (wide * narrow * tokens) ** 0.5
     return score(me[None], precond, pieces, sources, scale)
 

time: 52.1 us -> 42 us (0.81)
  starting transfers between devices: 23 us -> 20.5 us
  other arithmetic: 2.53 us -> 0.12 us
  waiting for transfers between devices: 13.4 us -> 11.1 us
  Pallas kernels: 11.9 us -> 9.81 us
  local copies, waits for them, and re-layouts: 0.77 us -> 0.02 us
    ppermute x16, starting transfers between devices: 23 us -> 20.5 us  [exchange(): return lax.ppermute(x, 'ex', [(i, i ^ bit) for i in range(devices)])]
    ppermute x16, waiting for transfers between devices: 13.4 us -> 11.1 us  [exchange(): return lax.ppermute(x, 'ex', [(i, i ^ bit) for i in range(devices)])]
    add x5 -> x4, other arithmetic: 1.52 us -> 0.04 us  [the longest x1 0.01 us: exchange_all(): packed = packed + exchange(packed, 4, devices)]
    pallas_call x1, Pallas kernels: 4.02 us -> 2.55 us  [precondition(): pl.pallas_call(functools.partial(precond_kernel, float(tokens)), out_shap...]
    concatenate x2, other arithmetic: 1.01 us -> 0.09 us  [the longest x1 0.07 us: on_device(): tests = jnp.concatenate([test_grads, far], axis=0)]
    unnamed x4 -> x2, local copies, waits for them, and re-layouts: 0.75 us -> 0.01 us
    pallas_call x1, Pallas kernels: 6.62 us -> 5.98 us  [project(): pl.pallas_call(project_kernel, out_shape=[pltpu.VMEM((wide, wide), jnp.fl...]
  transfers between devices with their start and end apart: 16 -> 16, of which waited for: 7 -> 5; matrix products, arithmetic and copies ran while one was open for 3% -> 0% of each run, Pallas kernels for 21% -> 20%
where the time goes in v3:
time: 42 us; the launch traced here: 41.7 us
  starting transfers between devices  20.5 us (49%)
  waiting for transfers between devices  11.1 us (26%)
  Pallas kernels  9.81 us (23%)
    ppermute x16, starting transfers between devices, exchange(): return lax.ppermute(x, 'ex', [(i, i ^ bit) for i in range(devices)])  20.5 us
    ppermute x16, waiting for transfers between devices, exchange(): return lax.ppermute(x, 'ex', [(i, i ^ bit) for i in range(devices)])  11.1 us
    pallas_call x1, Pallas kernels, project(): pl.pallas_call(project_kernel, out_shape=[pltpu.VMEM((wide, wide), jnp.fl...  5.98 us
    pallas_call x1, Pallas kernels, precondition(): pl.pallas_call(functools.partial(precond_kernel, float(tokens)), out_shap...  2.55 us
    pallas_call x1, Pallas kernels, score(): pl.pallas_call(functools.partial(score_kernel, sources, scale), out_shape...  1.28 us
  transfers between devices with their start and end apart: 16, of which 5 were waited for; matrix products, arithmetic and copies ran while one was open for 0% of the time, Pallas kernels for 20%

profile of v3, /device:TPU:1, one launch (start us, length us, event | category | flops | bytes accessed | tf_op | source)
XLA Modules:
  0.0 41.7 jit_solution(1446571995250219199)
XLA Ops:
  0.0 0.0 copy-start
  0.0 3.1 %collective-permute-start = (bf16[4,8192]{1,0:T(4,128)(2,1)}, bf16[4,8192]{1,0:T(4,128)(2,1)S(1)}, u32[]{:S(2)}, u32[]{:S(2)}) collective-permute-start(bf16[4,8192]{1,0:T(4,128)(2,1)} %param.9), channel_id=1, source_target_pairs={{0,16},{1,17},{2,18},{3,19},{4,20},{5,21},{6,22},{7,23},{8,24},{9,... | collective-permute-start | bytes 196616 | tf_op jit(solution)/shard_map/ppermute | solution.py:221
  3.1 6.0 %project.1 = (f32[128,128]{1,0:T(8,128)S(1)}, f32[1,64,128]{2,1,0:T(8,128)S(1)}) custom-call(bf16[1,1024,4096]{2,1,0:T(8,128)(2,1)} %x_hbm.1, bf16[1,1024,1024]{2,1,0:T(8,128)(2,1)} %g_hbm.1, bf16[128,4096]{1,0:T(8,128)(2,1)} %pin_hbm.1, bf16[64,1024]{1,0:T(8,128)(2,1)} %pout_hbm.1), custom_call_target="tpu_custom_call" | custom-call | tf_op jit(solution)/shard_map/project/pallas_call | solution.py:95
  9.1 0.0 collective-permute-done
  9.1 0.0 copy-done
  9.2 0.1 pad_maximum_fusion.1
  9.2 1.0 %collective-permute-start.1 = (f32[128,128]{1,0:T(8,128)S(1)}, f32[128,128]{1,0:T(8,128)S(1)}, u32[]{:S(2)}, u32[]{:S(2)}) collective-permute-start(f32[128,128]{1,0:T(8,128)S(1)} %get-tuple-element.19), channel_id=1, source_target_pairs={{0,1},{1,0},{2,3},{3,2},{4,5},{5,4},{6,7},{7,6},{8,9},{9,8},{10,11... | collective-permute-start | bytes 196616 | tf_op jit(solution)/shard_map/ppermute | solution.py:221
  10.2 1.3 %collective-permute-start.3 = (bf16[8,8192]{1,0:T(8,128)(2,1)S(1)}, bf16[8,8192]{1,0:T(8,128)(2,1)S(1)}, u32[]{:S(2)}, u32[]{:S(2)}) collective-permute-start(bf16[8,8192]{1,0:T(8,128)(2,1)S(1)} %pad_maximum_fusion.1), channel_id=1, source_target_pairs={{0,8},{1,9},{2,10},{3,11},{4,12},{5,13},{6,14},{7,15},{8,0},{9,1},... | collective-permute-start | bytes 393224 | tf_op jit(solution)/shard_map/ppermute | solution.py:221
  11.6 0.0 collective-permute-done.1
  11.6 1.3 %collective-permute-start.2 = (f32[128,128]{1,0:T(8,128)S(1)}, f32[128,128]{1,0:T(8,128)S(1)}, u32[]{:S(2)}, u32[]{:S(2)}) collective-permute-start(f32[128,128]{1,0:T(8,128)S(1)} %add.12), channel_id=1, source_target_pairs={{0,2},{1,3},{2,0},{3,1},{4,6},{5,7},{6,4},{7,5},{8,10},{9,11},{10,... | collective-permute-start | bytes 196616 | tf_op jit(solution)/shard_map/ppermute | solution.py:221
  12.8 2.2 %collective-permute-done.2 = f32[128,128]{1,0:T(8,128)S(1)} collective-permute-done((f32[128,128]{1,0:T(8,128)S(1)}, f32[128,128]{1,0:T(8,128)S(1)}, u32[]{:S(2)}, u32[]{:S(2)}) %collective-permute-start.2) | collective-permute-done | bytes 65568 | tf_op jit(solution)/shard_map/ppermute | solution.py:221
  15.1 0.3 collective-permute-done.3
  15.3 1.3 %collective-permute-start.6 = (bf16[16,8192]{1,0:T(8,128)(2,1)S(1)}, bf16[16,8192]{1,0:T(8,128)(2,1)S(1)}, u32[]{:S(2)}, u32[]{:S(2)}) collective-permute-start(bf16[16,8192]{1,0:T(8,128)(2,1)S(1)} %pad_maximum_fusion.refs_0_), channel_id=1, source_target_pairs={{0,2},{1,3},{2,0},{3,1},{4,6},{5,7},{6,4},{7,5},{8,10},{9,11},{10,... | collective-permute-start | bytes 786440 | tf_op jit(solution)/shard_map/ppermute | solution.py:221
  16.6 1.2 %collective-permute-start.7 = (bf16[16,8192]{1,0:T(8,128)(2,1)S(1)}, bf16[16,8192]{1,0:T(8,128)(2,1)S(1)}, u32[]{:S(2)}, u32[]{:S(2)}) collective-permute-start(bf16[16,8192]{1,0:T(8,128)(2,1)S(1)} %pad_maximum_fusion.refs_0_), channel_id=1, source_target_pairs={{0,4},{1,5},{2,6},{3,7},{4,0},{5,1},{6,2},{7,3},{8,12},{9,13},{10,... | collective-permute-start | bytes 786440 | tf_op jit(solution)/shard_map/ppermute | solution.py:221
  17.9 0.2 collective-permute-start.4
  18.1 6.5 %collective-permute-done.4 = f32[128,128]{1,0:T(8,128)S(1)} collective-permute-done((f32[128,128]{1,0:T(8,128)S(1)}, f32[128,128]{1,0:T(8,128)S(1)}, u32[]{:S(2)}, u32[]{:S(2)}) %collective-permute-start.4) | collective-permute-done | bytes 65568 | tf_op jit(solution)/shard_map/ppermute | solution.py:221
  24.6 1.5 %collective-permute-start.5 = (f32[128,128]{1,0:T(8,128)S(1)}, f32[128,128]{1,0:T(8,128)S(1)}, u32[]{:S(2)}, u32[]{:S(2)}) collective-permute-start(f32[128,128]{1,0:T(8,128)S(1)} %add.14), channel_id=1, source_target_pairs={{0,8},{1,9},{2,10},{3,11},{4,12},{5,13},{6,14},{7,15},{8,0},{9,1},... | collective-permute-start | bytes 196616 | tf_op jit(solution)/shard_map/ppermute | solution.py:221
  26.1 1.7 %collective-permute-done.5 = f32[128,128]{1,0:T(8,128)S(1)} collective-permute-done((f32[128,128]{1,0:T(8,128)S(1)}, f32[128,128]{1,0:T(8,128)S(1)}, u32[]{:S(2)}, u32[]{:S(2)}) %collective-permute-start.5) | collective-permute-done | bytes 65568 | tf_op jit(solution)/shard_map/ppermute | solution.py:221
  27.8 0.0 collective-permute-done.6.refs_1_
  27.8 0.0 collective-permute-done.7.refs_2_
  27.8 0.1 collective-permute-start.8
  27.9 3.6 %collective-permute-start.11 = (bf16[16,8192]{1,0:T(8,128)(2,1)S(1)}, bf16[16,8192]{1,0:T(8,128)(2,1)S(1)}, u32[]{:S(2)}, u32[]{:S(2)}) collective-permute-start(bf16[16,8192]{1,0:T(8,128)(2,1)S(1)} %pad_maximum_fusion.refs_0_), channel_id=1, source_target_pairs={{0,1},{1,0},{2,3},{3,2},{4,5},{5,4},{6,7},{7,6},{8,9},{9,8},{10,11... | collective-permute-start | bytes 786440 | tf_op jit(solution)/shard_map/ppermute | solution.py:221
  31.5 0.3 collective-permute-start.9
  31.8 1.3 %collective-permute-start.10 = (bf16[8,8192]{1,0:T(8,128)(2,1)S(1)}, bf16[8,8192]{1,0:T(8,128)(2,1)S(1)}, u32[]{:S(2)}, u32[]{:S(2)}) collective-permute-start(bf16[8,8192]{1,0:T(8,128)(2,1)S(1)} %slice.7), channel_id=1, source_target_pairs={{0,4},{1,5},{2,6},{3,7},{4,0},{5,1},{6,2},{7,3},{8,12},{9,13},{10,... | collective-permute-start | bytes 393224 | tf_op jit(solution)/shard_map/ppermute | solution.py:221
  33.2 0.6 %collective-permute-start.12 = (bf16[16,8192]{1,0:T(8,128)(2,1)S(1)}, bf16[16,8192]{1,0:T(8,128)(2,1)S(1)}, u32[]{:S(2)}, u32[]{:S(2)}) collective-permute-start(bf16[16,8192]{1,0:T(8,128)(2,1)S(1)} %collective-permute-done.6.refs_1_), channel_id=1, source_target_pairs={{0,1},{1,0},{2,3},{3,2},{4,5},{5,4},{6,7},{7,6},{8,9},{9,8},{10,11... | collective-permute-start | bytes 786440 | tf_op jit(solution)/shard_map/ppermute | solution.py:221
  33.7 0.0 collective-permute-done.8.there_ref
  33.7 2.6 %collective-permute-start.13 = (bf16[16,8192]{1,0:T(8,128)(2,1)S(1)}, bf16[16,8192]{1,0:T(8,128)(2,1)S(1)}, u32[]{:S(2)}, u32[]{:S(2)}) collective-permute-start(bf16[16,8192]{1,0:T(8,128)(2,1)S(1)} %collective-permute-done.7.refs_2_), channel_id=1, source_target_pairs={{0,1},{1,0},{2,3},{3,2},{4,5},{5,4},{6,7},{7,6},{8,9},{9,8},{10,11... | collective-permute-start | bytes 786440 | tf_op jit(solution)/shard_map/ppermute | solution.py:221
  36.4 0.4 collective-permute-done.9.refs_3_
  36.7 0.8 %collective-permute-start.14 = (bf16[8,8192]{1,0:T(8,128)(2,1)S(1)}, bf16[8,8192]{1,0:T(8,128)(2,1)S(1)}, u32[]{:S(2)}, u32[]{:S(2)}) collective-permute-start(bf16[8,8192]{1,0:T(8,128)(2,1)S(1)} %collective-permute-done.9.refs_3_), channel_id=1, source_target_pairs={{0,1},{1,0},{2,3},{3,2},{4,5},{5,4},{6,7},{7,6},{8,9},{9,8},{10,11... | collective-permute-start | bytes 393224 | tf_op jit(solution)/shard_map/ppermute | solution.py:221
  37.5 0.0 collective-permute-done.10.refs_4_
  37.5 0.3 collective-permute-start.15
  37.8 2.6 %precondition.1.p_ref = f32[1,64,128]{2,1,0:T(8,128)S(1)} custom-call(f32[128,128]{1,0:T(8,128)S(1)} %add.15.here_ref, f32[128,128]{1,0:T(8,128)S(1)} %collective-permute-done.8.there_ref, f32[1,64,128]{2,1,0:T(8,128)S(1)} %get-tuple-element.24.grads_ref), custom_call_target="tpu_custom_call" | custom-call | tf_op jit(solution)/shard_map/precondition/pallas_call | solution.py:170
  40.4 0.0 collective-permute-done.11.refs_5_
  40.4 0.0 collective-permute-done.14.refs_8_
  40.4 0.0 collective-permute-done.15.refs_9_
  40.4 0.0 collective-permute-done.12.refs_6_
  40.4 0.0 collective-permute-done.13.refs_7_
  40.4 1.3 %score.1 = f32[1,128]{1,0:T(1,128)} custom-call(s32[1]{0:T(128)} %bitcast.me_ref, f32[1,64,128]{2,1,0:T(8,128)S(1)} %precondition.1.p_ref, bf16[16,8192]{1,0:T(8,128)(2,1)S(1)} %pad_maximum_fusion.refs_0_, bf16[16,8192]{1,0:T(8,128)(2,1)S(1)} %collective-permute-done.6.refs_1_, bf16[16,8192]{1,0:T(8,128)(2,1)S(1)} %collective-permute-done.7.refs_2_, ...), custom_call_target="tpu_custom_call" | custom-call | tf_op jit(solution)/shard_map/score/pallas_call | solution.py:210
  (7 shorter events, 0.1 us)
Async XLA Ops:
  0.0 9.1 %copy-start = (bf16[4,8192]{1,0:T(4,128)(2,1)S(1)}, bf16[4,8192]{1,0:T(4,128)(2,1)}, u32[]{:S(2)}) copy-start(bf16[4,8192]{1,0:T(4,128)(2,1)} %param.9) | copy-start | bytes 196612
  0.0 9.1 %collective-permute-start = (bf16[4,8192]{1,0:T(4,128)(2,1)}, bf16[4,8192]{1,0:T(4,128)(2,1)S(1)}, u32[]{:S(2)}, u32[]{:S(2)}) collective-permute-start(bf16[4,8192]{1,0:T(4,128)(2,1)} %param.9), channel_id=1, source_target_pairs={{0,16},{1,17},{2,18},{3,19},{4,20},{5,21},{6,22},{7,23},{8,24},{9,... | collective-permute-start | bytes 196616 | tf_op jit(solution)/shard_map/ppermute | solution.py:221
  9.2 2.3 %collective-permute-start.1 = (f32[128,128]{1,0:T(8,128)S(1)}, f32[128,128]{1,0:T(8,128)S(1)}, u32[]{:S(2)}, u32[]{:S(2)}) collective-permute-start(f32[128,128]{1,0:T(8,128)S(1)} %get-tuple-element.19), channel_id=1, source_target_pairs={{0,1},{1,0},{2,3},{3,2},{4,5},{5,4},{6,7},{7,6},{8,9},{9,8},{10,11... | collective-permute-start | bytes 196616 | tf_op jit(solution)/shard_map/ppermute | solution.py:221
  10.2 5.1 %collective-permute-start.3 = (bf16[8,8192]{1,0:T(8,128)(2,1)S(1)}, bf16[8,8192]{1,0:T(8,128)(2,1)S(1)}, u32[]{:S(2)}, u32[]{:S(2)}) collective-permute-start(bf16[8,8192]{1,0:T(8,128)(2,1)S(1)} %pad_maximum_fusion.1), channel_id=1, source_target_pairs={{0,8},{1,9},{2,10},{3,11},{4,12},{5,13},{6,14},{7,15},{8,0},{9,1},... | collective-permute-start | bytes 393224 | tf_op jit(solution)/shard_map/ppermute | solution.py:221
  11.6 3.5 %collective-permute-start.2 = (f32[128,128]{1,0:T(8,128)S(1)}, f32[128,128]{1,0:T(8,128)S(1)}, u32[]{:S(2)}, u32[]{:S(2)}) collective-permute-start(f32[128,128]{1,0:T(8,128)S(1)} %add.12), channel_id=1, source_target_pairs={{0,2},{1,3},{2,0},{3,1},{4,6},{5,7},{6,4},{7,5},{8,10},{9,11},{10,... | collective-permute-start | bytes 196616 | tf_op jit(solution)/shard_map/ppermute | solution.py:221
  15.3 12.5 %collective-permute-start.6 = (bf16[16,8192]{1,0:T(8,128)(2,1)S(1)}, bf16[16,8192]{1,0:T(8,128)(2,1)S(1)}, u32[]{:S(2)}, u32[]{:S(2)}) collective-permute-start(bf16[16,8192]{1,0:T(8,128)(2,1)S(1)} %pad_maximum_fusion.refs_0_), channel_id=1, source_target_pairs={{0,2},{1,3},{2,0},{3,1},{4,6},{5,7},{6,4},{7,5},{8,10},{9,11},{10,... | collective-permute-start | bytes 786440 | tf_op jit(solution)/shard_map/ppermute | solution.py:221
  16.6 11.2 %collective-permute-start.7 = (bf16[16,8192]{1,0:T(8,128)(2,1)S(1)}, bf16[16,8192]{1,0:T(8,128)(2,1)S(1)}, u32[]{:S(2)}, u32[]{:S(2)}) collective-permute-start(bf16[16,8192]{1,0:T(8,128)(2,1)S(1)} %pad_maximum_fusion.refs_0_), channel_id=1, source_target_pairs={{0,4},{1,5},{2,6},{3,7},{4,0},{5,1},{6,2},{7,3},{8,12},{9,13},{10,... | collective-permute-start | bytes 786440 | tf_op jit(solution)/shard_map/ppermute | solution.py:221
  17.9 6.7 %collective-permute-start.4 = (f32[128,128]{1,0:T(8,128)S(1)}, f32[128,128]{1,0:T(8,128)S(1)}, u32[]{:S(2)}, u32[]{:S(2)}) collective-permute-start(f32[128,128]{1,0:T(8,128)S(1)} %add.13), channel_id=1, source_target_pairs={{0,4},{1,5},{2,6},{3,7},{4,0},{5,1},{6,2},{7,3},{8,12},{9,13},{10,... | collective-permute-start | bytes 196616 | tf_op jit(solution)/shard_map/ppermute | solution.py:221
  24.6 3.2 %collective-permute-start.5 = (f32[128,128]{1,0:T(8,128)S(1)}, f32[128,128]{1,0:T(8,128)S(1)}, u32[]{:S(2)}, u32[]{:S(2)}) collective-permute-start(f32[128,128]{1,0:T(8,128)S(1)} %add.14), channel_id=1, source_target_pairs={{0,8},{1,9},{2,10},{3,11},{4,12},{5,13},{6,14},{7,15},{8,0},{9,1},... | collective-permute-start | bytes 196616 | tf_op jit(solution)/shard_map/ppermute | solution.py:221
  27.8 5.9 %collective-permute-start.8 = (f32[128,128]{1,0:T(8,128)S(1)}, f32[128,128]{1,0:T(8,128)S(1)}, u32[]{:S(2)}, u32[]{:S(2)}) collective-permute-start(f32[128,128]{1,0:T(8,128)S(1)} %add.15.here_ref), channel_id=1, source_target_pairs={{0,16},{1,17},{2,18},{3,19},{4,20},{5,21},{6,22},{7,23},{8,24},{9,... | collective-permute-start | bytes 196616 | tf_op jit(solution)/shard_map/ppermute | solution.py:221
  27.9 12.4 %collective-permute-start.11 = (bf16[16,8192]{1,0:T(8,128)(2,1)S(1)}, bf16[16,8192]{1,0:T(8,128)(2,1)S(1)}, u32[]{:S(2)}, u32[]{:S(2)}) collective-permute-start(bf16[16,8192]{1,0:T(8,128)(2,1)S(1)} %pad_maximum_fusion.refs_0_), channel_id=1, source_target_pairs={{0,1},{1,0},{2,3},{3,2},{4,5},{5,4},{6,7},{7,6},{8,9},{9,8},{10,11... | collective-permute-start | bytes 786440 | tf_op jit(solution)/shard_map/ppermute | solution.py:221
  31.5 5.2 %collective-permute-start.9 = (bf16[8,8192]{1,0:T(8,128)(2,1)S(1)}, bf16[8,8192]{1,0:T(8,128)(2,1)S(1)}, u32[]{:S(2)}, u32[]{:S(2)}) collective-permute-start(bf16[8,8192]{1,0:T(8,128)(2,1)S(1)} %slice.6), channel_id=1, source_target_pairs={{0,2},{1,3},{2,0},{3,1},{4,6},{5,7},{6,4},{7,5},{8,10},{9,11},{10,... | collective-permute-start | bytes 393224 | tf_op jit(solution)/shard_map/ppermute | solution.py:221
  31.8 5.7 %collective-permute-start.10 = (bf16[8,8192]{1,0:T(8,128)(2,1)S(1)}, bf16[8,8192]{1,0:T(8,128)(2,1)S(1)}, u32[]{:S(2)}, u32[]{:S(2)}) collective-permute-start(bf16[8,8192]{1,0:T(8,128)(2,1)S(1)} %slice.7), channel_id=1, source_target_pairs={{0,4},{1,5},{2,6},{3,7},{4,0},{5,1},{6,2},{7,3},{8,12},{9,13},{10,... | collective-permute-start | bytes 393224 | tf_op jit(solution)/shard_map/ppermute | solution.py:221
  33.2 7.2 %collective-permute-start.12 = (bf16[16,8192]{1,0:T(8,128)(2,1)S(1)}, bf16[16,8192]{1,0:T(8,128)(2,1)S(1)}, u32[]{:S(2)}, u32[]{:S(2)}) collective-permute-start(bf16[16,8192]{1,0:T(8,128)(2,1)S(1)} %collective-permute-done.6.refs_1_), channel_id=1, source_target_pairs={{0,1},{1,0},{2,3},{3,2},{4,5},{5,4},{6,7},{7,6},{8,9},{9,8},{10,11... | collective-permute-start | bytes 786440 | tf_op jit(solution)/shard_map/ppermute | solution.py:221
  33.7 6.7 %collective-permute-start.13 = (bf16[16,8192]{1,0:T(8,128)(2,1)S(1)}, bf16[16,8192]{1,0:T(8,128)(2,1)S(1)}, u32[]{:S(2)}, u32[]{:S(2)}) collective-permute-start(bf16[16,8192]{1,0:T(8,128)(2,1)S(1)} %collective-permute-done.7.refs_2_), channel_id=1, source_target_pairs={{0,1},{1,0},{2,3},{3,2},{4,5},{5,4},{6,7},{7,6},{8,9},{9,8},{10,11... | collective-permute-start | bytes 786440 | tf_op jit(solution)/shard_map/ppermute | solution.py:221
  36.7 3.6 %collective-permute-start.14 = (bf16[8,8192]{1,0:T(8,128)(2,1)S(1)}, bf16[8,8192]{1,0:T(8,128)(2,1)S(1)}, u32[]{:S(2)}, u32[]{:S(2)}) collective-permute-start(bf16[8,8192]{1,0:T(8,128)(2,1)S(1)} %collective-permute-done.9.refs_3_), channel_id=1, source_target_pairs={{0,1},{1,0},{2,3},{3,2},{4,5},{5,4},{6,7},{7,6},{8,9},{9,8},{10,11... | collective-permute-start | bytes 393224 | tf_op jit(solution)/shard_map/ppermute | solution.py:221
  37.5 2.9 %collective-permute-start.15 = (bf16[8,8192]{1,0:T(8,128)(2,1)S(1)}, bf16[8,8192]{1,0:T(8,128)(2,1)S(1)}, u32[]{:S(2)}, u32[]{:S(2)}) collective-permute-start(bf16[8,8192]{1,0:T(8,128)(2,1)S(1)} %collective-permute-done.10.refs_4_), channel_id=1, source_target_pairs={{0,1},{1,0},{2,3},{3,2},{4,5},{5,4},{6,7},{7,6},{8,9},{9,8},{10,11... | collective-permute-start | bytes 393224 | tf_op jit(solution)/shard_map/ppermute | solution.py:221

commit v4 on v3

--- a/solution.py
+++ b/solution.py
@@ -226,12 +226,11 @@
     return both, offsets + [k ^ bit for k in offsets]
 
 
-def exchange_all(packed, tests, tests_offsets, devices):
+def exchange_all(packed, tests, offsets, devices):
     far = devices // 4
     packed, tests = lax.optimization_barrier((packed, tests))
     packed = packed + exchange(packed, 1, devices)
     packed = packed + exchange(packed, 2, devices)
-    offsets = tests_offsets
     while far > 4:
         tests, offsets = join(tests, offsets, far, devices)
         far //= 2
@@ -239,10 +238,8 @@
     half, rows = len(offsets) // 2, tests.shape[0] // 2
     a, a_off = exchange(tests, 2, devices), [k ^ 2 for k in offsets]
     b, b_off = exchange(tests, 4, devices), [k ^ 4 for k in offsets]
-    packed = packed + exchange(packed, 4, devices)
-    packed = packed + exchange(packed, 8, devices)
-    bit = 16
-    while bit < devices // 2:
+    bit = 8
+    while bit < devices:
         packed = packed + exchange(packed, bit, devices)
         bit *= 2
     packed, a, b = lax.optimization_barrier((packed, a, b))
@@ -254,7 +251,7 @@
         (exchange(a[rows:], 4, devices), [k ^ 4 for k in a_off[half:]]),
     ]
     pieces += [(exchange(t, 1, devices), [k ^ 1 for k in off]) for t, off in pieces]
-    there = exchange(packed, bit, devices)
+    there = exchange(packed, 4, devices)
     return packed, there, [t for t, _ in pieces], [off for _, off in pieces]
 
 

time: 42 us -> 40.1 us (0.955)
  waiting for transfers between devices: 11.1 us -> 9.68 us
    ppermute x16, waiting for transfers between devices: 11.1 us -> 9.68 us  [exchange(): return lax.ppermute(x, 'ex', [(i, i ^ bit) for i in range(devices)])]
  transfers between devices with their start and end apart: 16 -> 16, of which waited for: 5 -> 5; matrix products, arithmetic and copies ran while one was open for 0% -> 0% of each run, Pallas kernels for 20% -> 21%
where the time goes in v4:
time: 40.1 us; the launch traced here: 39.9 us
  starting transfers between devices  20.2 us (50%)
  Pallas kernels  9.8 us (24%)
  waiting for transfers between devices  9.68 us (24%)
    ppermute x16, starting transfers between devices, exchange(): return lax.ppermute(x, 'ex', [(i, i ^ bit) for i in range(devices)])  20.2 us
    ppermute x16, waiting for transfers between devices, exchange(): return lax.ppermute(x, 'ex', [(i, i ^ bit) for i in range(devices)])  9.68 us
    pallas_call x1, Pallas kernels, project(): pl.pallas_call(project_kernel, out_shape=[pltpu.VMEM((wide, wide), jnp.fl...  5.98 us
    pallas_call x1, Pallas kernels, precondition(): pl.pallas_call(functools.partial(precond_kernel, float(tokens)), out_shap...  2.54 us
    pallas_call x1, Pallas kernels, score(): pl.pallas_call(functools.partial(score_kernel, sources, scale), out_shape...  1.28 us
  transfers between devices with their start and end apart: 16, of which 5 were waited for; matrix products, arithmetic and copies ran while one was open for 0% of the time, Pallas kernels for 21%

profile of v4, /device:TPU:1, one launch (start us, length us, event | category | flops | bytes accessed | tf_op | source)
XLA Modules:
  0.0 39.9 jit_solution(9534122282747567877)
XLA Ops:
  0.0 0.0 copy-start
  0.0 3.1 %collective-permute-start = (bf16[4,8192]{1,0:T(4,128)(2,1)}, bf16[4,8192]{1,0:T(4,128)(2,1)S(1)}, u32[]{:S(2)}, u32[]{:S(2)}) collective-permute-start(bf16[4,8192]{1,0:T(4,128)(2,1)} %param.9), channel_id=1, source_target_pairs={{0,16},{1,17},{2,18},{3,19},{4,20},{5,21},{6,22},{7,23},{8,24},{9,... | collective-permute-start | bytes 196616 | tf_op jit(solution)/shard_map/ppermute | solution.py:221
  3.1 6.0 %project.1 = (f32[128,128]{1,0:T(8,128)S(1)}, f32[1,64,128]{2,1,0:T(8,128)S(1)}) custom-call(bf16[1,1024,4096]{2,1,0:T(8,128)(2,1)} %x_hbm.1, bf16[1,1024,1024]{2,1,0:T(8,128)(2,1)} %g_hbm.1, bf16[128,4096]{1,0:T(8,128)(2,1)} %pin_hbm.1, bf16[64,1024]{1,0:T(8,128)(2,1)} %pout_hbm.1), custom_call_target="tpu_custom_call" | custom-call | tf_op jit(solution)/shard_map/project/pallas_call | solution.py:95
  9.1 0.0 collective-permute-done
  9.1 0.0 copy-done
  9.2 0.1 pad_maximum_fusion.1
  9.2 1.0 %collective-permute-start.1 = (f32[128,128]{1,0:T(8,128)S(1)}, f32[128,128]{1,0:T(8,128)S(1)}, u32[]{:S(2)}, u32[]{:S(2)}) collective-permute-start(f32[128,128]{1,0:T(8,128)S(1)} %get-tuple-element.19), channel_id=1, source_target_pairs={{0,1},{1,0},{2,3},{3,2},{4,5},{5,4},{6,7},{7,6},{8,9},{9,8},{10,11... | collective-permute-start | bytes 196616 | tf_op jit(solution)/shard_map/ppermute | solution.py:221
  10.2 1.3 %collective-permute-start.3 = (bf16[8,8192]{1,0:T(8,128)(2,1)S(1)}, bf16[8,8192]{1,0:T(8,128)(2,1)S(1)}, u32[]{:S(2)}, u32[]{:S(2)}) collective-permute-start(bf16[8,8192]{1,0:T(8,128)(2,1)S(1)} %pad_maximum_fusion.1), channel_id=1, source_target_pairs={{0,8},{1,9},{2,10},{3,11},{4,12},{5,13},{6,14},{7,15},{8,0},{9,1},... | collective-permute-start | bytes 393224 | tf_op jit(solution)/shard_map/ppermute | solution.py:221
  11.6 0.0 collective-permute-done.1
  11.6 1.3 %collective-permute-start.2 = (f32[128,128]{1,0:T(8,128)S(1)}, f32[128,128]{1,0:T(8,128)S(1)}, u32[]{:S(2)}, u32[]{:S(2)}) collective-permute-start(f32[128,128]{1,0:T(8,128)S(1)} %add.12), channel_id=1, source_target_pairs={{0,2},{1,3},{2,0},{3,1},{4,6},{5,7},{6,4},{7,5},{8,10},{9,11},{10,... | collective-permute-start | bytes 196616 | tf_op jit(solution)/shard_map/ppermute | solution.py:221
  12.8 2.2 %collective-permute-done.2 = f32[128,128]{1,0:T(8,128)S(1)} collective-permute-done((f32[128,128]{1,0:T(8,128)S(1)}, f32[128,128]{1,0:T(8,128)S(1)}, u32[]{:S(2)}, u32[]{:S(2)}) %collective-permute-start.2) | collective-permute-done | bytes 65568 | tf_op jit(solution)/shard_map/ppermute | solution.py:221
  15.1 0.3 collective-permute-done.3
  15.3 1.3 %collective-permute-start.6 = (bf16[16,8192]{1,0:T(8,128)(2,1)S(1)}, bf16[16,8192]{1,0:T(8,128)(2,1)S(1)}, u32[]{:S(2)}, u32[]{:S(2)}) collective-permute-start(bf16[16,8192]{1,0:T(8,128)(2,1)S(1)} %pad_maximum_fusion.refs_0_), channel_id=1, source_target_pairs={{0,2},{1,3},{2,0},{3,1},{4,6},{5,7},{6,4},{7,5},{8,10},{9,11},{10,... | collective-permute-start | bytes 786440 | tf_op jit(solution)/shard_map/ppermute | solution.py:221
  16.6 1.2 %collective-permute-start.7 = (bf16[16,8192]{1,0:T(8,128)(2,1)S(1)}, bf16[16,8192]{1,0:T(8,128)(2,1)S(1)}, u32[]{:S(2)}, u32[]{:S(2)}) collective-permute-start(bf16[16,8192]{1,0:T(8,128)(2,1)S(1)} %pad_maximum_fusion.refs_0_), channel_id=1, source_target_pairs={{0,4},{1,5},{2,6},{3,7},{4,0},{5,1},{6,2},{7,3},{8,12},{9,13},{10,... | collective-permute-start | bytes 786440 | tf_op jit(solution)/shard_map/ppermute | solution.py:221
  17.9 1.3 %collective-permute-start.4 = (f32[128,128]{1,0:T(8,128)S(1)}, f32[128,128]{1,0:T(8,128)S(1)}, u32[]{:S(2)}, u32[]{:S(2)}) collective-permute-start(f32[128,128]{1,0:T(8,128)S(1)} %add.13), channel_id=1, source_target_pairs={{0,8},{1,9},{2,10},{3,11},{4,12},{5,13},{6,14},{7,15},{8,0},{9,1},... | collective-permute-start | bytes 196616 | tf_op jit(solution)/shard_map/ppermute | solution.py:221
  19.2 2.1 %collective-permute-done.4 = f32[128,128]{1,0:T(8,128)S(1)} collective-permute-done((f32[128,128]{1,0:T(8,128)S(1)}, f32[128,128]{1,0:T(8,128)S(1)}, u32[]{:S(2)}, u32[]{:S(2)}) %collective-permute-start.4) | collective-permute-done | bytes 65568 | tf_op jit(solution)/shard_map/ppermute | solution.py:221
  21.3 0.1 collective-permute-start.5
  21.4 4.0 %collective-permute-done.5 = f32[128,128]{1,0:T(8,128)S(1)} collective-permute-done((f32[128,128]{1,0:T(8,128)S(1)}, f32[128,128]{1,0:T(8,128)S(1)}, u32[]{:S(2)}, u32[]{:S(2)}) %collective-permute-start.5) | collective-permute-done | bytes 65568 | tf_op jit(solution)/shard_map/ppermute | solution.py:221
  25.4 0.0 collective-permute-done.6.refs_1_
  25.4 0.0 collective-permute-done.7.refs_2_
  25.4 0.3 collective-permute-start.8
  25.7 3.8 %collective-permute-start.11 = (bf16[16,8192]{1,0:T(8,128)(2,1)S(1)}, bf16[16,8192]{1,0:T(8,128)(2,1)S(1)}, u32[]{:S(2)}, u32[]{:S(2)}) collective-permute-start(bf16[16,8192]{1,0:T(8,128)(2,1)S(1)} %pad_maximum_fusion.refs_0_), channel_id=1, source_target_pairs={{0,1},{1,0},{2,3},{3,2},{4,5},{5,4},{6,7},{7,6},{8,9},{9,8},{10,11... | collective-permute-start | bytes 786440 | tf_op jit(solution)/shard_map/ppermute | solution.py:221
  29.5 0.3 collective-permute-start.9
  29.8 1.3 %collective-permute-start.10 = (bf16[8,8192]{1,0:T(8,128)(2,1)S(1)}, bf16[8,8192]{1,0:T(8,128)(2,1)S(1)}, u32[]{:S(2)}, u32[]{:S(2)}) collective-permute-start(bf16[8,8192]{1,0:T(8,128)(2,1)S(1)} %slice.7), channel_id=1, source_target_pairs={{0,4},{1,5},{2,6},{3,7},{4,0},{5,1},{6,2},{7,3},{8,12},{9,13},{10,... | collective-permute-start | bytes 393224 | tf_op jit(solution)/shard_map/ppermute | solution.py:221
  31.1 0.6 %collective-permute-start.12 = (bf16[16,8192]{1,0:T(8,128)(2,1)S(1)}, bf16[16,8192]{1,0:T(8,128)(2,1)S(1)}, u32[]{:S(2)}, u32[]{:S(2)}) collective-permute-start(bf16[16,8192]{1,0:T(8,128)(2,1)S(1)} %collective-permute-done.6.refs_1_), channel_id=1, source_target_pairs={{0,1},{1,0},{2,3},{3,2},{4,5},{5,4},{6,7},{7,6},{8,9},{9,8},{10,11... | collective-permute-start | bytes 786440 | tf_op jit(solution)/shard_map/ppermute | solution.py:221
  31.7 0.0 collective-permute-done.8.there_ref
  31.7 1.9 %collective-permute-start.13 = (bf16[16,8192]{1,0:T(8,128)(2,1)S(1)}, bf16[16,8192]{1,0:T(8,128)(2,1)S(1)}, u32[]{:S(2)}, u32[]{:S(2)}) collective-permute-start(bf16[16,8192]{1,0:T(8,128)(2,1)S(1)} %collective-permute-done.7.refs_2_), channel_id=1, source_target_pairs={{0,1},{1,0},{2,3},{3,2},{4,5},{5,4},{6,7},{7,6},{8,9},{9,8},{10,11... | collective-permute-start | bytes 786440 | tf_op jit(solution)/shard_map/ppermute | solution.py:221
  33.6 1.1 %collective-permute-done.9.refs_3_ = bf16[8,8192]{1,0:T(8,128)(2,1)S(1)} collective-permute-done((bf16[8,8192]{1,0:T(8,128)(2,1)S(1)}, bf16[8,8192]{1,0:T(8,128)(2,1)S(1)}, u32[]{:S(2)}, u32[]{:S(2)}) %collective-permute-start.9) | collective-permute-done | bytes 131104 | tf_op jit(solution)/shard_map/ppermute | solution.py:221
  34.7 0.8 %collective-permute-start.14 = (bf16[8,8192]{1,0:T(8,128)(2,1)S(1)}, bf16[8,8192]{1,0:T(8,128)(2,1)S(1)}, u32[]{:S(2)}, u32[]{:S(2)}) collective-permute-start(bf16[8,8192]{1,0:T(8,128)(2,1)S(1)} %collective-permute-done.9.refs_3_), channel_id=1, source_target_pairs={{0,1},{1,0},{2,3},{3,2},{4,5},{5,4},{6,7},{7,6},{8,9},{9,8},{10,11... | collective-permute-start | bytes 393224 | tf_op jit(solution)/shard_map/ppermute | solution.py:221
  35.5 0.0 collective-permute-done.10.refs_4_
  35.5 0.6 %collective-permute-start.15 = (bf16[8,8192]{1,0:T(8,128)(2,1)S(1)}, bf16[8,8192]{1,0:T(8,128)(2,1)S(1)}, u32[]{:S(2)}, u32[]{:S(2)}) collective-permute-start(bf16[8,8192]{1,0:T(8,128)(2,1)S(1)} %collective-permute-done.10.refs_4_), channel_id=1, source_target_pairs={{0,1},{1,0},{2,3},{3,2},{4,5},{5,4},{6,7},{7,6},{8,9},{9,8},{10,11... | collective-permute-start | bytes 393224 | tf_op jit(solution)/shard_map/ppermute | solution.py:221
  36.1 2.5 %precondition.1.p_ref = f32[1,64,128]{2,1,0:T(8,128)S(1)} custom-call(f32[128,128]{1,0:T(8,128)S(1)} %add.15.here_ref, f32[128,128]{1,0:T(8,128)S(1)} %collective-permute-done.8.there_ref, f32[1,64,128]{2,1,0:T(8,128)S(1)} %get-tuple-element.24.grads_ref), custom_call_target="tpu_custom_call" | custom-call | tf_op jit(solution)/shard_map/precondition/pallas_call | solution.py:170
  38.6 0.0 collective-permute-done.11.refs_5_
  38.6 0.0 collective-permute-done.14.refs_8_
  38.6 0.0 collective-permute-done.15.refs_9_
  38.6 0.0 collective-permute-done.12.refs_6_
  38.6 0.0 collective-permute-done.13.refs_7_
  38.7 1.3 %score.1 = f32[1,128]{1,0:T(1,128)} custom-call(s32[1]{0:T(128)} %bitcast.me_ref, f32[1,64,128]{2,1,0:T(8,128)S(1)} %precondition.1.p_ref, bf16[16,8192]{1,0:T(8,128)(2,1)S(1)} %pad_maximum_fusion.refs_0_, bf16[16,8192]{1,0:T(8,128)(2,1)S(1)} %collective-permute-done.6.refs_1_, bf16[16,8192]{1,0:T(8,128)(2,1)S(1)} %collective-permute-done.7.refs_2_, ...), custom_call_target="tpu_custom_call" | custom-call | tf_op jit(solution)/shard_map/score/pallas_call | solution.py:210
  (7 shorter events, 0.1 us)
Async XLA Ops:
  0.0 9.1 %copy-start = (bf16[4,8192]{1,0:T(4,128)(2,1)S(1)}, bf16[4,8192]{1,0:T(4,128)(2,1)}, u32[]{:S(2)}) copy-start(bf16[4,8192]{1,0:T(4,128)(2,1)} %param.9) | copy-start | bytes 196612
  0.0 9.1 %collective-permute-start = (bf16[4,8192]{1,0:T(4,128)(2,1)}, bf16[4,8192]{1,0:T(4,128)(2,1)S(1)}, u32[]{:S(2)}, u32[]{:S(2)}) collective-permute-start(bf16[4,8192]{1,0:T(4,128)(2,1)} %param.9), channel_id=1, source_target_pairs={{0,16},{1,17},{2,18},{3,19},{4,20},{5,21},{6,22},{7,23},{8,24},{9,... | collective-permute-start | bytes 196616 | tf_op jit(solution)/shard_map/ppermute | solution.py:221
  9.2 2.3 %collective-permute-start.1 = (f32[128,128]{1,0:T(8,128)S(1)}, f32[128,128]{1,0:T(8,128)S(1)}, u32[]{:S(2)}, u32[]{:S(2)}) collective-permute-start(f32[128,128]{1,0:T(8,128)S(1)} %get-tuple-element.19), channel_id=1, source_target_pairs={{0,1},{1,0},{2,3},{3,2},{4,5},{5,4},{6,7},{7,6},{8,9},{9,8},{10,11... | collective-permute-start | bytes 196616 | tf_op jit(solution)/shard_map/ppermute | solution.py:221
  10.2 5.1 %collective-permute-start.3 = (bf16[8,8192]{1,0:T(8,128)(2,1)S(1)}, bf16[8,8192]{1,0:T(8,128)(2,1)S(1)}, u32[]{:S(2)}, u32[]{:S(2)}) collective-permute-start(bf16[8,8192]{1,0:T(8,128)(2,1)S(1)} %pad_maximum_fusion.1), channel_id=1, source_target_pairs={{0,8},{1,9},{2,10},{3,11},{4,12},{5,13},{6,14},{7,15},{8,0},{9,1},... | collective-permute-start | bytes 393224 | tf_op jit(solution)/shard_map/ppermute | solution.py:221
  11.6 3.5 %collective-permute-start.2 = (f32[128,128]{1,0:T(8,128)S(1)}, f32[128,128]{1,0:T(8,128)S(1)}, u32[]{:S(2)}, u32[]{:S(2)}) collective-permute-start(f32[128,128]{1,0:T(8,128)S(1)} %add.12), channel_id=1, source_target_pairs={{0,2},{1,3},{2,0},{3,1},{4,6},{5,7},{6,4},{7,5},{8,10},{9,11},{10,... | collective-permute-start | bytes 196616 | tf_op jit(solution)/shard_map/ppermute | solution.py:221
  15.3 10.0 %collective-permute-start.6 = (bf16[16,8192]{1,0:T(8,128)(2,1)S(1)}, bf16[16,8192]{1,0:T(8,128)(2,1)S(1)}, u32[]{:S(2)}, u32[]{:S(2)}) collective-permute-start(bf16[16,8192]{1,0:T(8,128)(2,1)S(1)} %pad_maximum_fusion.refs_0_), channel_id=1, source_target_pairs={{0,2},{1,3},{2,0},{3,1},{4,6},{5,7},{6,4},{7,5},{8,10},{9,11},{10,... | collective-permute-start | bytes 786440 | tf_op jit(solution)/shard_map/ppermute | solution.py:221
  16.6 8.8 %collective-permute-start.7 = (bf16[16,8192]{1,0:T(8,128)(2,1)S(1)}, bf16[16,8192]{1,0:T(8,128)(2,1)S(1)}, u32[]{:S(2)}, u32[]{:S(2)}) collective-permute-start(bf16[16,8192]{1,0:T(8,128)(2,1)S(1)} %pad_maximum_fusion.refs_0_), channel_id=1, source_target_pairs={{0,4},{1,5},{2,6},{3,7},{4,0},{5,1},{6,2},{7,3},{8,12},{9,13},{10,... | collective-permute-start | bytes 786440 | tf_op jit(solution)/shard_map/ppermute | solution.py:221
  17.9 3.4 %collective-permute-start.4 = (f32[128,128]{1,0:T(8,128)S(1)}, f32[128,128]{1,0:T(8,128)S(1)}, u32[]{:S(2)}, u32[]{:S(2)}) collective-permute-start(f32[128,128]{1,0:T(8,128)S(1)} %add.13), channel_id=1, source_target_pairs={{0,8},{1,9},{2,10},{3,11},{4,12},{5,13},{6,14},{7,15},{8,0},{9,1},... | collective-permute-start | bytes 196616 | tf_op jit(solution)/shard_map/ppermute | solution.py:221
  21.3 4.1 %collective-permute-start.5 = (f32[128,128]{1,0:T(8,128)S(1)}, f32[128,128]{1,0:T(8,128)S(1)}, u32[]{:S(2)}, u32[]{:S(2)}) collective-permute-start(f32[128,128]{1,0:T(8,128)S(1)} %add.14), channel_id=1, source_target_pairs={{0,16},{1,17},{2,18},{3,19},{4,20},{5,21},{6,22},{7,23},{8,24},{9,... | collective-permute-start | bytes 196616 | tf_op jit(solution)/shard_map/ppermute | solution.py:221
  25.4 6.3 %collective-permute-start.8 = (f32[128,128]{1,0:T(8,128)S(1)}, f32[128,128]{1,0:T(8,128)S(1)}, u32[]{:S(2)}, u32[]{:S(2)}) collective-permute-start(f32[128,128]{1,0:T(8,128)S(1)} %add.15.here_ref), channel_id=1, source_target_pairs={{0,4},{1,5},{2,6},{3,7},{4,0},{5,1},{6,2},{7,3},{8,12},{9,13},{10,... | collective-permute-start | bytes 196616 | tf_op jit(solution)/shard_map/ppermute | solution.py:221
  25.7 12.9 %collective-permute-start.11 = (bf16[16,8192]{1,0:T(8,128)(2,1)S(1)}, bf16[16,8192]{1,0:T(8,128)(2,1)S(1)}, u32[]{:S(2)}, u32[]{:S(2)}) collective-permute-start(bf16[16,8192]{1,0:T(8,128)(2,1)S(1)} %pad_maximum_fusion.refs_0_), channel_id=1, source_target_pairs={{0,1},{1,0},{2,3},{3,2},{4,5},{5,4},{6,7},{7,6},{8,9},{9,8},{10,11... | collective-permute-start | bytes 786440 | tf_op jit(solution)/shard_map/ppermute | solution.py:221
  29.5 5.2 %collective-permute-start.9 = (bf16[8,8192]{1,0:T(8,128)(2,1)S(1)}, bf16[8,8192]{1,0:T(8,128)(2,1)S(1)}, u32[]{:S(2)}, u32[]{:S(2)}) collective-permute-start(bf16[8,8192]{1,0:T(8,128)(2,1)S(1)} %slice.6), channel_id=1, source_target_pairs={{0,2},{1,3},{2,0},{3,1},{4,6},{5,7},{6,4},{7,5},{8,10},{9,11},{10,... | collective-permute-start | bytes 393224 | tf_op jit(solution)/shard_map/ppermute | solution.py:221
  29.8 5.6 %collective-permute-start.10 = (bf16[8,8192]{1,0:T(8,128)(2,1)S(1)}, bf16[8,8192]{1,0:T(8,128)(2,1)S(1)}, u32[]{:S(2)}, u32[]{:S(2)}) collective-permute-start(bf16[8,8192]{1,0:T(8,128)(2,1)S(1)} %slice.7), channel_id=1, source_target_pairs={{0,4},{1,5},{2,6},{3,7},{4,0},{5,1},{6,2},{7,3},{8,12},{9,13},{10,... | collective-permute-start | bytes 393224 | tf_op jit(solution)/shard_map/ppermute | solution.py:221
  31.1 7.5 %collective-permute-start.12 = (bf16[16,8192]{1,0:T(8,128)(2,1)S(1)}, bf16[16,8192]{1,0:T(8,128)(2,1)S(1)}, u32[]{:S(2)}, u32[]{:S(2)}) collective-permute-start(bf16[16,8192]{1,0:T(8,128)(2,1)S(1)} %collective-permute-done.6.refs_1_), channel_id=1, source_target_pairs={{0,1},{1,0},{2,3},{3,2},{4,5},{5,4},{6,7},{7,6},{8,9},{9,8},{10,11... | collective-permute-start | bytes 786440 | tf_op jit(solution)/shard_map/ppermute | solution.py:221
  31.7 6.9 %collective-permute-start.13 = (bf16[16,8192]{1,0:T(8,128)(2,1)S(1)}, bf16[16,8192]{1,0:T(8,128)(2,1)S(1)}, u32[]{:S(2)}, u32[]{:S(2)}) collective-permute-start(bf16[16,8192]{1,0:T(8,128)(2,1)S(1)} %collective-permute-done.7.refs_2_), channel_id=1, source_target_pairs={{0,1},{1,0},{2,3},{3,2},{4,5},{5,4},{6,7},{7,6},{8,9},{9,8},{10,11... | collective-permute-start | bytes 786440 | tf_op jit(solution)/shard_map/ppermute | solution.py:221
  34.7 3.9 %collective-permute-start.14 = (bf16[8,8192]{1,0:T(8,128)(2,1)S(1)}, bf16[8,8192]{1,0:T(8,128)(2,1)S(1)}, u32[]{:S(2)}, u32[]{:S(2)}) collective-permute-start(bf16[8,8192]{1,0:T(8,128)(2,1)S(1)} %collective-permute-done.9.refs_3_), channel_id=1, source_target_pairs={{0,1},{1,0},{2,3},{3,2},{4,5},{5,4},{6,7},{7,6},{8,9},{9,8},{10,11... | collective-permute-start | bytes 393224 | tf_op jit(solution)/shard_map/ppermute | solution.py:221
  35.5 3.1 %collective-permute-start.15 = (bf16[8,8192]{1,0:T(8,128)(2,1)S(1)}, bf16[8,8192]{1,0:T(8,128)(2,1)S(1)}, u32[]{:S(2)}, u32[]{:S(2)}) collective-permute-start(bf16[8,8192]{1,0:T(8,128)(2,1)S(1)} %collective-permute-done.10.refs_4_), channel_id=1, source_target_pairs={{0,1},{1,0},{2,3},{3,2},{4,5},{5,4},{6,7},{7,6},{8,9},{9,8},{10,11... | collective-permute-start | bytes 393224 | tf_op jit(solution)/shard_map/ppermute | solution.py:221

commit v5 on v4

--- a/solution.py
+++ b/solution.py
@@ -10,6 +10,7 @@
 HIGHEST = lax.Precision.HIGHEST
 DAMP = 0.1
 DEPTH = 2
+LONG = 10**10
 VMEM = pltpu.MemorySpace.VMEM
 SMEM = pltpu.MemorySpace.SMEM
 
@@ -134,10 +135,10 @@
     return (s / mean + jnp.where(eye, DAMP, 0.0)) * first, first / mean, eye
 
 
-def precond_kernel(tokens, here_ref, there_ref, grads_ref, out_ref):
-    wide = here_ref.shape[0]
+def precond_kernel(tokens, packed_ref, grads_ref, out_ref):
+    wide = packed_ref.shape[0]
     examples, narrow, _ = grads_ref.shape
-    packed = here_ref[...] + there_ref[...]
+    packed = packed_ref[...]
     upper = packed[:narrow]
     lower = jnp.concatenate([upper[:, narrow:].T, packed[narrow:, narrow:]], axis=1)
     yi, scale_in, _ = normalised(jnp.concatenate([upper, lower], axis=0))
@@ -166,14 +167,14 @@
         out_ref[e] = both.astype(jnp.bfloat16).astype(jnp.float32)
 
 
-def precondition(here, there, grads, tokens):
+def precondition(packed, grads, tokens):
     return pl.pallas_call(
         functools.partial(precond_kernel, float(tokens)),
         out_shape=pltpu.VMEM(grads.shape, jnp.float32),
-        in_specs=[pl.BlockSpec(memory_space=VMEM)] * 3,
+        in_specs=[pl.BlockSpec(memory_space=VMEM)] * 2,
         out_specs=pl.BlockSpec(memory_space=VMEM),
         name="precondition",
-    )(*[pltpu.with_memory_space_constraint(a, VMEM) for a in (here, there, grads)])
+    )(*[pltpu.with_memory_space_constraint(a, VMEM) for a in (packed, grads)])
 
 
 def score_kernel(sources, scale, me_ref, p_ref, *refs):
@@ -226,6 +227,21 @@
     return both, offsets + [k ^ bit for k in offsets]
 
 
+def add_kernel(a_ref, b_ref, out_ref):
+    out_ref[...] = a_ref[...] + b_ref[...]
+
+
+def add_late(a, b):
+    return pl.pallas_call(
+        add_kernel,
+        out_shape=pltpu.VMEM(a.shape, a.dtype),
+        in_specs=[pl.BlockSpec(memory_space=VMEM)] * 2,
+        out_specs=pl.BlockSpec(memory_space=VMEM),
+        cost_estimate=pl.CostEstimate(flops=LONG, bytes_accessed=3 * a.size * 4, transcendentals=0),
+        name="add",
+    )(*[pltpu.with_memory_space_constraint(t, VMEM) for t in (a, b)])
+
+
 def exchange_all(packed, tests, offsets, devices):
     far = devices // 4
     packed, tests = lax.optimization_barrier((packed, tests))
@@ -238,21 +254,20 @@
     half, rows = len(offsets) // 2, tests.shape[0] // 2
     a, a_off = exchange(tests, 2, devices), [k ^ 2 for k in offsets]
     b, b_off = exchange(tests, 4, devices), [k ^ 4 for k in offsets]
-    bit = 8
+    packed = add_late(packed, exchange(packed, 8, devices))
+    bit = 16
     while bit < devices:
         packed = packed + exchange(packed, bit, devices)
         bit *= 2
     packed, a, b = lax.optimization_barrier((packed, a, b))
-    pieces = [
-        (tests, offsets),
-        (a, a_off),
-        (b, b_off),
-        (exchange(b[:rows], 2, devices), [k ^ 2 for k in b_off[:half]]),
-        (exchange(a[rows:], 4, devices), [k ^ 4 for k in a_off[half:]]),
-    ]
-    pieces += [(exchange(t, 1, devices), [k ^ 1 for k in off]) for t, off in pieces]
-    there = exchange(packed, 4, devices)
-    return packed, there, [t for t, _ in pieces], [off for _, off in pieces]
+    c, c_off = exchange(b[:rows], 2, devices), [k ^ 2 for k in b_off[:half]]
+    d, d_off = exchange(a[rows:], 4, devices), [k ^ 4 for k in a_off[half:]]
+    packed = add_late(packed, exchange(packed, 4, devices))
+    packed, c, d, tests, a, b = lax.optimization_barrier((packed, c, d, tests, a, b))
+    everyone = jnp.concatenate([tests, a, b, c, d], axis=0)
+    offsets = offsets + a_off + b_off + c_off + d_off
+    pieces = [(everyone, offsets), (exchange(everyone, 1, devices), [k ^ 1 for k in offsets])]
+    return packed, [t for t, _ in pieces], [off for _, off in pieces]
 
 
 def on_device(example_inputs, output_grads, proj_in, proj_out, test_grads):
@@ -265,15 +280,15 @@
         far = exchange(test_grads, devices // 2, devices)
     packed, grads = project(example_inputs, output_grads, proj_in, proj_out)
     if simple:
-        here, there = lax.psum(packed, "ex"), jnp.zeros_like(packed)
+        packed = lax.psum(packed, "ex")
         pieces = [lax.all_gather(test_grads, "ex", axis=0, tiled=True)]
         sources = [list(range(devices))]
         me = me * 0
     else:
         packed, far = lax.optimization_barrier((packed, far))
         tests = jnp.concatenate([test_grads, far], axis=0)
-        here, there, pieces, sources = exchange_all(packed, tests, [0, devices // 2], devices)
-    precond = precondition(here, there, grads, examples * tokens * devices)
+        packed, pieces, sources = exchange_all(packed, tests, [0, devices // 2], devices)
+    precond = precondition(packed, grads, examples * tokens * devices)
     scale = 4.0 / (wide * narrow * tokens) ** 0.5
     return score(me[None], precond, pieces, sources, scale)
 

time: 40.1 us -> 38 us (0.948)
  starting transfers between devices: 20.2 us -> 17.2 us
  waiting for transfers between devices: 9.68 us -> 10.4 us
    ppermute x16 -> x12, starting transfers between devices: 20.2 us -> 17.2 us  [exchange(): return lax.ppermute(x, 'ex', [(i, i ^ bit) for i in range(devices)])]
    ppermute x16 -> x12, waiting for transfers between devices: 9.68 us -> 10.4 us  [exchange(): return lax.ppermute(x, 'ex', [(i, i ^ bit) for i in range(devices)])]
  transfers between devices with their start and end apart: 16 -> 12, of which waited for: 5 -> 7; matrix products, arithmetic and copies ran while one was open for 0% -> 0% of each run, Pallas kernels for 21% -> 23%
where the time goes in v5:
time: 38 us; the launch traced here: 37.8 us
  starting transfers between devices  17.2 us (45%)
  waiting for transfers between devices  10.4 us (27%)
  Pallas kernels  9.83 us (26%)
    ppermute x12, starting transfers between devices, exchange(): return lax.ppermute(x, 'ex', [(i, i ^ bit) for i in range(devices)])  17.2 us
    ppermute x12, waiting for transfers between devices, exchange(): return lax.ppermute(x, 'ex', [(i, i ^ bit) for i in range(devices)])  10.4 us
    pallas_call x1, Pallas kernels, project(): pl.pallas_call(project_kernel, out_shape=[pltpu.VMEM((wide, wide), jnp.fl...  5.98 us
    pallas_call x1, Pallas kernels, precondition(): pl.pallas_call(functools.partial(precond_kernel, float(tokens)), out_shap...  2.55 us
    pallas_call x1, Pallas kernels, score(): pl.pallas_call(functools.partial(score_kernel, sources, scale), out_shape...  1.28 us
  transfers between devices with their start and end apart: 12, of which 7 were waited for; matrix products, arithmetic and copies ran while one was open for 0% of the time, Pallas kernels for 23%

profile of v5, /device:TPU:1, one launch (start us, length us, event | category | flops | bytes accessed | tf_op | source)
XLA Modules:
  0.0 37.8 jit_solution(7392890687012095735)
XLA Ops:
  0.0 0.0 copy-start
  0.0 3.1 %collective-permute-start = (bf16[4,8192]{1,0:T(4,128)(2,1)}, bf16[4,8192]{1,0:T(4,128)(2,1)S(1)}, u32[]{:S(2)}, u32[]{:S(2)}) collective-permute-start(bf16[4,8192]{1,0:T(4,128)(2,1)} %param.9), channel_id=1, source_target_pairs={{0,16},{1,17},{2,18},{3,19},{4,20},{5,21},{6,22},{7,23},{8,24},{9,... | collective-permute-start | bytes 196616 | tf_op jit(solution)/shard_map/ppermute | solution.py:222
  3.1 6.0 %project.1 = (f32[128,128]{1,0:T(8,128)S(1)}, f32[1,64,128]{2,1,0:T(8,128)S(1)}) custom-call(bf16[1,1024,4096]{2,1,0:T(8,128)(2,1)} %x_hbm.1, bf16[1,1024,1024]{2,1,0:T(8,128)(2,1)} %g_hbm.1, bf16[128,4096]{1,0:T(8,128)(2,1)} %pin_hbm.1, bf16[64,1024]{1,0:T(8,128)(2,1)} %pout_hbm.1), custom_call_target="tpu_custom_call" | custom-call | tf_op jit(solution)/shard_map/project/pallas_call | solution.py:96
  9.1 0.0 collective-permute-done
  9.1 0.0 copy-done
  9.2 0.1 pad_maximum_fusion.1
  9.2 1.0 %collective-permute-start.1 = (f32[128,128]{1,0:T(8,128)S(1)}, f32[128,128]{1,0:T(8,128)S(1)}, u32[]{:S(2)}, u32[]{:S(2)}) collective-permute-start(f32[128,128]{1,0:T(8,128)S(1)} %get-tuple-element.25), channel_id=1, source_target_pairs={{0,1},{1,0},{2,3},{3,2},{4,5},{5,4},{6,7},{7,6},{8,9},{9,8},{10,11... | collective-permute-start | bytes 196616 | tf_op jit(solution)/shard_map/ppermute | solution.py:222
  10.2 1.3 %collective-permute-start.3 = (bf16[8,8192]{1,0:T(8,128)(2,1)S(1)}, bf16[8,8192]{1,0:T(8,128)(2,1)S(1)}, u32[]{:S(2)}, u32[]{:S(2)}) collective-permute-start(bf16[8,8192]{1,0:T(8,128)(2,1)S(1)} %pad_maximum_fusion.1), channel_id=1, source_target_pairs={{0,8},{1,9},{2,10},{3,11},{4,12},{5,13},{6,14},{7,15},{8,0},{9,1},... | collective-permute-start | bytes 393224 | tf_op jit(solution)/shard_map/ppermute | solution.py:222
  11.6 0.0 collective-permute-done.1
  11.6 1.3 %collective-permute-start.2 = (f32[128,128]{1,0:T(8,128)S(1)}, f32[128,128]{1,0:T(8,128)S(1)}, u32[]{:S(2)}, u32[]{:S(2)}) collective-permute-start(f32[128,128]{1,0:T(8,128)S(1)} %add.11), channel_id=1, source_target_pairs={{0,2},{1,3},{2,0},{3,1},{4,6},{5,7},{6,4},{7,5},{8,10},{9,11},{10,... | collective-permute-start | bytes 196616 | tf_op jit(solution)/shard_map/ppermute | solution.py:222
  12.8 2.2 %collective-permute-done.2 = f32[128,128]{1,0:T(8,128)S(1)} collective-permute-done((f32[128,128]{1,0:T(8,128)S(1)}, f32[128,128]{1,0:T(8,128)S(1)}, u32[]{:S(2)}, u32[]{:S(2)}) %collective-permute-start.2) | collective-permute-done | bytes 65568 | tf_op jit(solution)/shard_map/ppermute | solution.py:222
  15.1 0.3 collective-permute-done.3
  15.3 1.4 %collective-permute-start.4 = (f32[128,128]{1,0:T(8,128)S(1)}, f32[128,128]{1,0:T(8,128)S(1)}, u32[]{:S(2)}, u32[]{:S(2)}) collective-permute-start(f32[128,128]{1,0:T(8,128)S(1)} %add.12.a_ref), channel_id=1, source_target_pairs={{0,8},{1,9},{2,10},{3,11},{4,12},{5,13},{6,14},{7,15},{8,0},{9,1},... | collective-permute-start | bytes 196616 | tf_op jit(solution)/shard_map/ppermute | solution.py:222
  16.7 1.2 %collective-permute-start.7 = (bf16[16,8192]{1,0:T(8,128)(2,1)S(1)}, bf16[16,8192]{1,0:T(8,128)(2,1)S(1)}, u32[]{:S(2)}, u32[]{:S(2)}) collective-permute-start(bf16[16,8192]{1,0:T(8,128)(2,1)S(1)} %pad_maximum_fusion), channel_id=1, source_target_pairs={{0,4},{1,5},{2,6},{3,7},{4,0},{5,1},{6,2},{7,3},{8,12},{9,13},{10,... | collective-permute-start | bytes 786440 | tf_op jit(solution)/shard_map/ppermute | solution.py:222
  17.9 1.2 %collective-permute-start.6 = (bf16[16,8192]{1,0:T(8,128)(2,1)S(1)}, bf16[16,8192]{1,0:T(8,128)(2,1)S(1)}, u32[]{:S(2)}, u32[]{:S(2)}) collective-permute-start(bf16[16,8192]{1,0:T(8,128)(2,1)S(1)} %pad_maximum_fusion), channel_id=1, source_target_pairs={{0,2},{1,3},{2,0},{3,1},{4,6},{5,7},{6,4},{7,5},{8,10},{9,11},{10,... | collective-permute-start | bytes 786440 | tf_op jit(solution)/shard_map/ppermute | solution.py:222
  19.2 0.0 collective-permute-done.4.b_ref
  19.2 0.1 collective-permute-start.5
  19.3 4.7 %collective-permute-done.5 = f32[128,128]{1,0:T(8,128)S(1)} collective-permute-done((f32[128,128]{1,0:T(8,128)S(1)}, f32[128,128]{1,0:T(8,128)S(1)}, u32[]{:S(2)}, u32[]{:S(2)}) %collective-permute-start.5) | collective-permute-done | bytes 65568 | tf_op jit(solution)/shard_map/ppermute | solution.py:222
  24.0 0.0 collective-permute-done.7
  24.0 0.4 collective-permute-done.6
  24.3 0.3 collective-permute-start.8
  24.6 1.2 %collective-permute-start.10 = (bf16[8,8192]{1,0:T(8,128)(2,1)S(1)}, bf16[8,8192]{1,0:T(8,128)(2,1)S(1)}, u32[]{:S(2)}, u32[]{:S(2)}) collective-permute-start(bf16[8,8192]{1,0:T(8,128)(2,1)S(1)} %slice.7), channel_id=1, source_target_pairs={{0,4},{1,5},{2,6},{3,7},{4,0},{5,1},{6,2},{7,3},{8,12},{9,13},{10,... | collective-permute-start | bytes 393224 | tf_op jit(solution)/shard_map/ppermute | solution.py:222
  25.9 1.2 %collective-permute-start.9 = (bf16[8,8192]{1,0:T(8,128)(2,1)S(1)}, bf16[8,8192]{1,0:T(8,128)(2,1)S(1)}, u32[]{:S(2)}, u32[]{:S(2)}) collective-permute-start(bf16[8,8192]{1,0:T(8,128)(2,1)S(1)} %slice.6), channel_id=1, source_target_pairs={{0,2},{1,3},{2,0},{3,1},{4,6},{5,7},{6,4},{7,5},{8,10},{9,11},{10,... | collective-permute-start | bytes 393224 | tf_op jit(solution)/shard_map/ppermute | solution.py:222
  27.1 0.3 collective-permute-done.8.b_ref
  27.5 1.4 %collective-permute-done.10 = bf16[8,8192]{1,0:T(8,128)(2,1)S(1)} collective-permute-done((bf16[8,8192]{1,0:T(8,128)(2,1)S(1)}, bf16[8,8192]{1,0:T(8,128)(2,1)S(1)}, u32[]{:S(2)}, u32[]{:S(2)}) %collective-permute-start.10) | collective-permute-done | bytes 131104 | tf_op jit(solution)/shard_map/ppermute | solution.py:222
  28.9 1.2 %collective-permute-done.9 = bf16[8,8192]{1,0:T(8,128)(2,1)S(1)} collective-permute-done((bf16[8,8192]{1,0:T(8,128)(2,1)S(1)}, bf16[8,8192]{1,0:T(8,128)(2,1)S(1)}, u32[]{:S(2)}, u32[]{:S(2)}) %collective-permute-start.9) | collective-permute-done | bytes 131104 | tf_op jit(solution)/shard_map/ppermute | solution.py:222
  30.1 3.8 %collective-permute-start.11 = (bf16[64,8192]{1,0:T(8,128)(2,1)S(1)}, bf16[64,8192]{1,0:T(8,128)(2,1)S(1)}, u32[]{:S(2)}, u32[]{:S(2)}) collective-permute-start(bf16[64,8192]{1,0:T(8,128)(2,1)S(1)} %constant_dynamic-update-slice_fusion.refs_0_), channel_id=1, source_target_pairs={{0,1},{1,0},{2,3},{3,2},{4,5},{5,4},{6,7},{7,6},{8,9},{9,8},{10,11... | collective-permute-start | bytes 3145736 | tf_op jit(solution)/shard_map/ppermute | solution.py:222
  33.9 2.6 %precondition.1.p_ref = f32[1,64,128]{2,1,0:T(8,128)S(1)} custom-call(f32[128,128]{1,0:T(8,128)S(1)} %add.15.packed_ref, f32[1,64,128]{2,1,0:T(8,128)S(1)} %get-tuple-element.33.grads_ref), custom_call_target="tpu_custom_call" | custom-call | tf_op jit(solution)/shard_map/precondition/pallas_call | solution.py:171
  36.5 0.0 collective-permute-done.11.refs_1_
  36.5 1.3 %score.1 = f32[1,128]{1,0:T(1,128)} custom-call(s32[1]{0:T(128)} %bitcast.me_ref, f32[1,64,128]{2,1,0:T(8,128)S(1)} %precondition.1.p_ref, bf16[64,8192]{1,0:T(8,128)(2,1)S(1)} %constant_dynamic-update-slice_fusion.refs_0_, bf16[64,8192]{1,0:T(8,128)(2,1)S(1)} %collective-permute-done.11.refs_1_), custom_call_target="tpu_custom_call" | custom-call | tf_op jit(solution)/shard_map/score/pallas_call | solution.py:211
  (13 shorter events, 0.2 us)
Async XLA Ops:
  0.0 9.1 %copy-start = (bf16[4,8192]{1,0:T(4,128)(2,1)S(1)}, bf16[4,8192]{1,0:T(4,128)(2,1)}, u32[]{:S(2)}) copy-start(bf16[4,8192]{1,0:T(4,128)(2,1)} %param.9) | copy-start | bytes 196612
  0.0 9.1 %collective-permute-start = (bf16[4,8192]{1,0:T(4,128)(2,1)}, bf16[4,8192]{1,0:T(4,128)(2,1)S(1)}, u32[]{:S(2)}, u32[]{:S(2)}) collective-permute-start(bf16[4,8192]{1,0:T(4,128)(2,1)} %param.9), channel_id=1, source_target_pairs={{0,16},{1,17},{2,18},{3,19},{4,20},{5,21},{6,22},{7,23},{8,24},{9,... | collective-permute-start | bytes 196616 | tf_op jit(solution)/shard_map/ppermute | solution.py:222
  9.2 2.3 %collective-permute-start.1 = (f32[128,128]{1,0:T(8,128)S(1)}, f32[128,128]{1,0:T(8,128)S(1)}, u32[]{:S(2)}, u32[]{:S(2)}) collective-permute-start(f32[128,128]{1,0:T(8,128)S(1)} %get-tuple-element.25), channel_id=1, source_target_pairs={{0,1},{1,0},{2,3},{3,2},{4,5},{5,4},{6,7},{7,6},{8,9},{9,8},{10,11... | collective-permute-start | bytes 196616 | tf_op jit(solution)/shard_map/ppermute | solution.py:222
  10.2 5.1 %collective-permute-start.3 = (bf16[8,8192]{1,0:T(8,128)(2,1)S(1)}, bf16[8,8192]{1,0:T(8,128)(2,1)S(1)}, u32[]{:S(2)}, u32[]{:S(2)}) collective-permute-start(bf16[8,8192]{1,0:T(8,128)(2,1)S(1)} %pad_maximum_fusion.1), channel_id=1, source_target_pairs={{0,8},{1,9},{2,10},{3,11},{4,12},{5,13},{6,14},{7,15},{8,0},{9,1},... | collective-permute-start | bytes 393224 | tf_op jit(solution)/shard_map/ppermute | solution.py:222
  11.6 3.5 %collective-permute-start.2 = (f32[128,128]{1,0:T(8,128)S(1)}, f32[128,128]{1,0:T(8,128)S(1)}, u32[]{:S(2)}, u32[]{:S(2)}) collective-permute-start(f32[128,128]{1,0:T(8,128)S(1)} %add.11), channel_id=1, source_target_pairs={{0,2},{1,3},{2,0},{3,1},{4,6},{5,7},{6,4},{7,5},{8,10},{9,11},{10,... | collective-permute-start | bytes 196616 | tf_op jit(solution)/shard_map/ppermute | solution.py:222
  15.3 3.8 %collective-permute-start.4 = (f32[128,128]{1,0:T(8,128)S(1)}, f32[128,128]{1,0:T(8,128)S(1)}, u32[]{:S(2)}, u32[]{:S(2)}) collective-permute-start(f32[128,128]{1,0:T(8,128)S(1)} %add.12.a_ref), channel_id=1, source_target_pairs={{0,8},{1,9},{2,10},{3,11},{4,12},{5,13},{6,14},{7,15},{8,0},{9,1},... | collective-permute-start | bytes 196616 | tf_op jit(solution)/shard_map/ppermute | solution.py:222
  16.7 7.3 %collective-permute-start.7 = (bf16[16,8192]{1,0:T(8,128)(2,1)S(1)}, bf16[16,8192]{1,0:T(8,128)(2,1)S(1)}, u32[]{:S(2)}, u32[]{:S(2)}) collective-permute-start(bf16[16,8192]{1,0:T(8,128)(2,1)S(1)} %pad_maximum_fusion), channel_id=1, source_target_pairs={{0,4},{1,5},{2,6},{3,7},{4,0},{5,1},{6,2},{7,3},{8,12},{9,13},{10,... | collective-permute-start | bytes 786440 | tf_op jit(solution)/shard_map/ppermute | solution.py:222
  17.9 6.4 %collective-permute-start.6 = (bf16[16,8192]{1,0:T(8,128)(2,1)S(1)}, bf16[16,8192]{1,0:T(8,128)(2,1)S(1)}, u32[]{:S(2)}, u32[]{:S(2)}) collective-permute-start(bf16[16,8192]{1,0:T(8,128)(2,1)S(1)} %pad_maximum_fusion), channel_id=1, source_target_pairs={{0,2},{1,3},{2,0},{3,1},{4,6},{5,7},{6,4},{7,5},{8,10},{9,11},{10,... | collective-permute-start | bytes 786440 | tf_op jit(solution)/shard_map/ppermute | solution.py:222
  19.2 4.8 %collective-permute-start.5 = (f32[128,128]{1,0:T(8,128)S(1)}, f32[128,128]{1,0:T(8,128)S(1)}, u32[]{:S(2)}, u32[]{:S(2)}) collective-permute-start(f32[128,128]{1,0:T(8,128)S(1)} %add.14), channel_id=1, source_target_pairs={{0,16},{1,17},{2,18},{3,19},{4,20},{5,21},{6,22},{7,23},{8,24},{9,... | collective-permute-start | bytes 196616 | tf_op jit(solution)/shard_map/ppermute | solution.py:222
  24.3 3.1 %collective-permute-start.8 = (f32[128,128]{1,0:T(8,128)S(1)}, f32[128,128]{1,0:T(8,128)S(1)}, u32[]{:S(2)}, u32[]{:S(2)}) collective-permute-start(f32[128,128]{1,0:T(8,128)S(1)} %add.13.a_ref), channel_id=1, source_target_pairs={{0,4},{1,5},{2,6},{3,7},{4,0},{5,1},{6,2},{7,3},{8,12},{9,13},{10,... | collective-permute-start | bytes 196616 | tf_op jit(solution)/shard_map/ppermute | solution.py:222
  24.6 4.2 %collective-permute-start.10 = (bf16[8,8192]{1,0:T(8,128)(2,1)S(1)}, bf16[8,8192]{1,0:T(8,128)(2,1)S(1)}, u32[]{:S(2)}, u32[]{:S(2)}) collective-permute-start(bf16[8,8192]{1,0:T(8,128)(2,1)S(1)} %slice.7), channel_id=1, source_target_pairs={{0,4},{1,5},{2,6},{3,7},{4,0},{5,1},{6,2},{7,3},{8,12},{9,13},{10,... | collective-permute-start | bytes 393224 | tf_op jit(solution)/shard_map/ppermute | solution.py:222
  25.9 4.1 %collective-permute-start.9 = (bf16[8,8192]{1,0:T(8,128)(2,1)S(1)}, bf16[8,8192]{1,0:T(8,128)(2,1)S(1)}, u32[]{:S(2)}, u32[]{:S(2)}) collective-permute-start(bf16[8,8192]{1,0:T(8,128)(2,1)S(1)} %slice.6), channel_id=1, source_target_pairs={{0,2},{1,3},{2,0},{3,1},{4,6},{5,7},{6,4},{7,5},{8,10},{9,11},{10,... | collective-permute-start | bytes 393224 | tf_op jit(solution)/shard_map/ppermute | solution.py:222
  30.1 6.4 %collective-permute-start.11 = (bf16[64,8192]{1,0:T(8,128)(2,1)S(1)}, bf16[64,8192]{1,0:T(8,128)(2,1)S(1)}, u32[]{:S(2)}, u32[]{:S(2)}) collective-permute-start(bf16[64,8192]{1,0:T(8,128)(2,1)S(1)} %constant_dynamic-update-slice_fusion.refs_0_), channel_id=1, source_target_pairs={{0,1},{1,0},{2,3},{3,2},{4,5},{5,4},{6,7},{7,6},{8,9},{9,8},{10,11... | collective-permute-start | bytes 3145736 | tf_op jit(solution)/shard_map/ppermute | solution.py:222

commit v6 on v5

--- a/solution.py
+++ b/solution.py
@@ -231,13 +231,13 @@
     out_ref[...] = a_ref[...] + b_ref[...]
 
 
-def add_late(a, b):
+def add_late(a, b, flops=LONG):
     return pl.pallas_call(
         add_kernel,
         out_shape=pltpu.VMEM(a.shape, a.dtype),
         in_specs=[pl.BlockSpec(memory_space=VMEM)] * 2,
         out_specs=pl.BlockSpec(memory_space=VMEM),
-        cost_estimate=pl.CostEstimate(flops=LONG, bytes_accessed=3 * a.size * 4, transcendentals=0),
+        cost_estimate=pl.CostEstimate(flops=flops, bytes_accessed=3 * a.size * 4, transcendentals=0),
         name="add",
     )(*[pltpu.with_memory_space_constraint(t, VMEM) for t in (a, b)])
 
@@ -259,10 +259,9 @@
     while bit < devices:
         packed = packed + exchange(packed, bit, devices)
         bit *= 2
-    packed, a, b = lax.optimization_barrier((packed, a, b))
     c, c_off = exchange(b[:rows], 2, devices), [k ^ 2 for k in b_off[:half]]
     d, d_off = exchange(a[rows:], 4, devices), [k ^ 4 for k in a_off[half:]]
-    packed = add_late(packed, exchange(packed, 4, devices))
+    packed = packed + exchange(packed, 4, devices)
     packed, c, d, tests, a, b = lax.optimization_barrier((packed, c, d, tests, a, b))
     everyone = jnp.concatenate([tests, a, b, c, d], axis=0)
     offsets = offsets + a_off + b_off + c_off + d_off

time: 38 us -> 37.2 us (0.979)
  starting transfers between devices: 17.2 us -> 16.4 us
    ppermute x12, starting transfers between devices: 17.2 us -> 16.4 us  [exchange(): return lax.ppermute(x, 'ex', [(i, i ^ bit) for i in range(devices)])]
  transfers between devices with their start and end apart: 12 -> 12, of which waited for: 7 -> 4; matrix products, arithmetic and copies ran while one was open for 0% -> 0% of each run, Pallas kernels for 23% -> 23%
where the time goes in v6:
time: 37.2 us; the launch traced here: 37 us
  starting transfers between devices  16.4 us (44%)
  waiting for transfers between devices  10.5 us (28%)
  Pallas kernels  9.81 us (26%)
    ppermute x12, starting transfers between devices, exchange(): return lax.ppermute(x, 'ex', [(i, i ^ bit) for i in range(devices)])  16.4 us
    ppermute x12, waiting for transfers between devices, exchange(): return lax.ppermute(x, 'ex', [(i, i ^ bit) for i in range(devices)])  10.5 us
    pallas_call x1, Pallas kernels, project(): pl.pallas_call(project_kernel, out_shape=[pltpu.VMEM((wide, wide), jnp.fl...  5.98 us
    pallas_call x1, Pallas kernels, precondition(): pl.pallas_call(functools.partial(precond_kernel, float(tokens)), out_shap...  2.55 us
    pallas_call x1, Pallas kernels, score(): pl.pallas_call(functools.partial(score_kernel, sources, scale), out_shape...  1.28 us
  transfers between devices with their start and end apart: 12, of which 4 were waited for; matrix products, arithmetic and copies ran while one was open for 0% of the time, Pallas kernels for 23%

profile of v6, /device:TPU:1, one launch (start us, length us, event | category | flops | bytes accessed | tf_op | source)
XLA Modules:
  0.0 37.0 jit_solution(16914467546884471215)
XLA Ops:
  0.0 0.0 copy-start
  0.0 3.1 %collective-permute-start = (bf16[4,8192]{1,0:T(4,128)(2,1)}, bf16[4,8192]{1,0:T(4,128)(2,1)S(1)}, u32[]{:S(2)}, u32[]{:S(2)}) collective-permute-start(bf16[4,8192]{1,0:T(4,128)(2,1)} %param.9), channel_id=1, source_target_pairs={{0,16},{1,17},{2,18},{3,19},{4,20},{5,21},{6,22},{7,23},{8,24},{9,... | collective-permute-start | bytes 196616 | tf_op jit(solution)/shard_map/ppermute | solution.py:222
  3.1 6.0 %project.1 = (f32[128,128]{1,0:T(8,128)S(1)}, f32[1,64,128]{2,1,0:T(8,128)S(1)}) custom-call(bf16[1,1024,4096]{2,1,0:T(8,128)(2,1)} %x_hbm.1, bf16[1,1024,1024]{2,1,0:T(8,128)(2,1)} %g_hbm.1, bf16[128,4096]{1,0:T(8,128)(2,1)} %pin_hbm.1, bf16[64,1024]{1,0:T(8,128)(2,1)} %pout_hbm.1), custom_call_target="tpu_custom_call" | custom-call | tf_op jit(solution)/shard_map/project/pallas_call | solution.py:96
  9.1 0.0 collective-permute-done
  9.1 0.0 copy-done
  9.2 0.1 pad_maximum_fusion.1
  9.2 1.0 %collective-permute-start.1 = (f32[128,128]{1,0:T(8,128)S(1)}, f32[128,128]{1,0:T(8,128)S(1)}, u32[]{:S(2)}, u32[]{:S(2)}) collective-permute-start(f32[128,128]{1,0:T(8,128)S(1)} %get-tuple-element.22), channel_id=1, source_target_pairs={{0,1},{1,0},{2,3},{3,2},{4,5},{5,4},{6,7},{7,6},{8,9},{9,8},{10,11... | collective-permute-start | bytes 196616 | tf_op jit(solution)/shard_map/ppermute | solution.py:222
  10.2 1.3 %collective-permute-start.3 = (bf16[8,8192]{1,0:T(8,128)(2,1)S(1)}, bf16[8,8192]{1,0:T(8,128)(2,1)S(1)}, u32[]{:S(2)}, u32[]{:S(2)}) collective-permute-start(bf16[8,8192]{1,0:T(8,128)(2,1)S(1)} %pad_maximum_fusion.1), channel_id=1, source_target_pairs={{0,8},{1,9},{2,10},{3,11},{4,12},{5,13},{6,14},{7,15},{8,0},{9,1},... | collective-permute-start | bytes 393224 | tf_op jit(solution)/shard_map/ppermute | solution.py:222
  11.6 0.0 collective-permute-done.1
  11.6 1.3 %collective-permute-start.2 = (f32[128,128]{1,0:T(8,128)S(1)}, f32[128,128]{1,0:T(8,128)S(1)}, u32[]{:S(2)}, u32[]{:S(2)}) collective-permute-start(f32[128,128]{1,0:T(8,128)S(1)} %add.13), channel_id=1, source_target_pairs={{0,2},{1,3},{2,0},{3,1},{4,6},{5,7},{6,4},{7,5},{8,10},{9,11},{10,... | collective-permute-start | bytes 196616 | tf_op jit(solution)/shard_map/ppermute | solution.py:222
  12.8 2.2 %collective-permute-done.2 = f32[128,128]{1,0:T(8,128)S(1)} collective-permute-done((f32[128,128]{1,0:T(8,128)S(1)}, f32[128,128]{1,0:T(8,128)S(1)}, u32[]{:S(2)}, u32[]{:S(2)}) %collective-permute-start.2) | collective-permute-done | bytes 65568 | tf_op jit(solution)/shard_map/ppermute | solution.py:222
  15.1 0.3 collective-permute-done.3
  15.3 1.4 %collective-permute-start.4 = (f32[128,128]{1,0:T(8,128)S(1)}, f32[128,128]{1,0:T(8,128)S(1)}, u32[]{:S(2)}, u32[]{:S(2)}) collective-permute-start(f32[128,128]{1,0:T(8,128)S(1)} %add.14.a_ref), channel_id=1, source_target_pairs={{0,8},{1,9},{2,10},{3,11},{4,12},{5,13},{6,14},{7,15},{8,0},{9,1},... | collective-permute-start | bytes 196616 | tf_op jit(solution)/shard_map/ppermute | solution.py:222
  16.7 1.2 %collective-permute-start.9 = (bf16[16,8192]{1,0:T(8,128)(2,1)S(1)}, bf16[16,8192]{1,0:T(8,128)(2,1)S(1)}, u32[]{:S(2)}, u32[]{:S(2)}) collective-permute-start(bf16[16,8192]{1,0:T(8,128)(2,1)S(1)} %pad_maximum_fusion), channel_id=1, source_target_pairs={{0,2},{1,3},{2,0},{3,1},{4,6},{5,7},{6,4},{7,5},{8,10},{9,11},{10,... | collective-permute-start | bytes 786440 | tf_op jit(solution)/shard_map/ppermute | solution.py:222
  17.9 1.2 %collective-permute-start.7 = (bf16[16,8192]{1,0:T(8,128)(2,1)S(1)}, bf16[16,8192]{1,0:T(8,128)(2,1)S(1)}, u32[]{:S(2)}, u32[]{:S(2)}) collective-permute-start(bf16[16,8192]{1,0:T(8,128)(2,1)S(1)} %pad_maximum_fusion), channel_id=1, source_target_pairs={{0,4},{1,5},{2,6},{3,7},{4,0},{5,1},{6,2},{7,3},{8,12},{9,13},{10,... | collective-permute-start | bytes 786440 | tf_op jit(solution)/shard_map/ppermute | solution.py:222
  19.2 0.0 collective-permute-done.4.b_ref
  19.2 0.1 collective-permute-start.5
  19.3 4.1 %collective-permute-done.9 = bf16[16,8192]{1,0:T(8,128)(2,1)S(1)} collective-permute-done((bf16[16,8192]{1,0:T(8,128)(2,1)S(1)}, bf16[16,8192]{1,0:T(8,128)(2,1)S(1)}, u32[]{:S(2)}, u32[]{:S(2)}) %collective-permute-start.9) | collective-permute-done | bytes 262176 | tf_op jit(solution)/shard_map/ppermute | solution.py:222
  23.4 1.3 %collective-permute-start.10 = (bf16[8,8192]{1,0:T(8,128)(2,1)S(1)}, bf16[8,8192]{1,0:T(8,128)(2,1)S(1)}, u32[]{:S(2)}, u32[]{:S(2)}) collective-permute-start(bf16[8,8192]{1,0:T(8,128)(2,1)S(1)} %slice.9), channel_id=1, source_target_pairs={{0,4},{1,5},{2,6},{3,7},{4,0},{5,1},{6,2},{7,3},{8,12},{9,13},{10,... | collective-permute-start | bytes 393224 | tf_op jit(solution)/shard_map/ppermute | solution.py:222
  24.7 0.0 collective-permute-done.7
  24.7 1.3 %collective-permute-start.8 = (bf16[8,8192]{1,0:T(8,128)(2,1)S(1)}, bf16[8,8192]{1,0:T(8,128)(2,1)S(1)}, u32[]{:S(2)}, u32[]{:S(2)}) collective-permute-start(bf16[8,8192]{1,0:T(8,128)(2,1)S(1)} %slice.8), channel_id=1, source_target_pairs={{0,2},{1,3},{2,0},{3,1},{4,6},{5,7},{6,4},{7,5},{8,10},{9,11},{10,... | collective-permute-start | bytes 393224 | tf_op jit(solution)/shard_map/ppermute | solution.py:222
  26.0 0.0 collective-permute-done.5
  26.0 0.3 collective-permute-start.6
  26.3 3.9 %collective-permute-done.6 = f32[128,128]{1,0:T(8,128)S(1)} collective-permute-done((f32[128,128]{1,0:T(8,128)S(1)}, f32[128,128]{1,0:T(8,128)S(1)}, u32[]{:S(2)}, u32[]{:S(2)}) %collective-permute-start.6) | collective-permute-done | bytes 65568 | tf_op jit(solution)/shard_map/ppermute | solution.py:222
  30.2 0.0 collective-permute-done.10
  30.2 0.0 collective-permute-done.8
  30.3 2.8 %collective-permute-start.11 = (bf16[64,8192]{1,0:T(8,128)(2,1)S(1)}, bf16[64,8192]{1,0:T(8,128)(2,1)S(1)}, u32[]{:S(2)}, u32[]{:S(2)}) collective-permute-start(bf16[64,8192]{1,0:T(8,128)(2,1)S(1)} %constant_dynamic-update-slice_fusion.refs_0_), channel_id=1, source_target_pairs={{0,1},{1,0},{2,3},{3,2},{4,5},{5,4},{6,7},{7,6},{8,9},{9,8},{10,11... | collective-permute-start | bytes 3145736 | tf_op jit(solution)/shard_map/ppermute | solution.py:222
  33.2 2.5 %precondition.1.p_ref = f32[1,64,128]{2,1,0:T(8,128)S(1)} custom-call(f32[128,128]{1,0:T(8,128)S(1)} %add.16.packed_ref, f32[1,64,128]{2,1,0:T(8,128)S(1)} %get-tuple-element.27.grads_ref), custom_call_target="tpu_custom_call" | custom-call | tf_op jit(solution)/shard_map/precondition/pallas_call | solution.py:171
  35.7 0.0 collective-permute-done.11.refs_1_
  35.7 1.3 %score.1 = f32[1,128]{1,0:T(1,128)} custom-call(s32[1]{0:T(128)} %bitcast.me_ref, f32[1,64,128]{2,1,0:T(8,128)S(1)} %precondition.1.p_ref, bf16[64,8192]{1,0:T(8,128)(2,1)S(1)} %constant_dynamic-update-slice_fusion.refs_0_, bf16[64,8192]{1,0:T(8,128)(2,1)S(1)} %collective-permute-done.11.refs_1_), custom_call_target="tpu_custom_call" | custom-call | tf_op jit(solution)/shard_map/score/pallas_call | solution.py:211
  (13 shorter events, 0.2 us)
Async XLA Ops:
  0.0 9.1 %copy-start = (bf16[4,8192]{1,0:T(4,128)(2,1)S(1)}, bf16[4,8192]{1,0:T(4,128)(2,1)}, u32[]{:S(2)}) copy-start(bf16[4,8192]{1,0:T(4,128)(2,1)} %param.9) | copy-start | bytes 196612
  0.0 9.1 %collective-permute-start = (bf16[4,8192]{1,0:T(4,128)(2,1)}, bf16[4,8192]{1,0:T(4,128)(2,1)S(1)}, u32[]{:S(2)}, u32[]{:S(2)}) collective-permute-start(bf16[4,8192]{1,0:T(4,128)(2,1)} %param.9), channel_id=1, source_target_pairs={{0,16},{1,17},{2,18},{3,19},{4,20},{5,21},{6,22},{7,23},{8,24},{9,... | collective-permute-start | bytes 196616 | tf_op jit(solution)/shard_map/ppermute | solution.py:222
  9.2 2.3 %collective-permute-start.1 = (f32[128,128]{1,0:T(8,128)S(1)}, f32[128,128]{1,0:T(8,128)S(1)}, u32[]{:S(2)}, u32[]{:S(2)}) collective-permute-start(f32[128,128]{1,0:T(8,128)S(1)} %get-tuple-element.22), channel_id=1, source_target_pairs={{0,1},{1,0},{2,3},{3,2},{4,5},{5,4},{6,7},{7,6},{8,9},{9,8},{10,11... | collective-permute-start | bytes 196616 | tf_op jit(solution)/shard_map/ppermute | solution.py:222
  10.2 5.1 %collective-permute-start.3 = (bf16[8,8192]{1,0:T(8,128)(2,1)S(1)}, bf16[8,8192]{1,0:T(8,128)(2,1)S(1)}, u32[]{:S(2)}, u32[]{:S(2)}) collective-permute-start(bf16[8,8192]{1,0:T(8,128)(2,1)S(1)} %pad_maximum_fusion.1), channel_id=1, source_target_pairs={{0,8},{1,9},{2,10},{3,11},{4,12},{5,13},{6,14},{7,15},{8,0},{9,1},... | collective-permute-start | bytes 393224 | tf_op jit(solution)/shard_map/ppermute | solution.py:222
  11.6 3.5 %collective-permute-start.2 = (f32[128,128]{1,0:T(8,128)S(1)}, f32[128,128]{1,0:T(8,128)S(1)}, u32[]{:S(2)}, u32[]{:S(2)}) collective-permute-start(f32[128,128]{1,0:T(8,128)S(1)} %add.13), channel_id=1, source_target_pairs={{0,2},{1,3},{2,0},{3,1},{4,6},{5,7},{6,4},{7,5},{8,10},{9,11},{10,... | collective-permute-start | bytes 196616 | tf_op jit(solution)/shard_map/ppermute | solution.py:222
  15.3 3.8 %collective-permute-start.4 = (f32[128,128]{1,0:T(8,128)S(1)}, f32[128,128]{1,0:T(8,128)S(1)}, u32[]{:S(2)}, u32[]{:S(2)}) collective-permute-start(f32[128,128]{1,0:T(8,128)S(1)} %add.14.a_ref), channel_id=1, source_target_pairs={{0,8},{1,9},{2,10},{3,11},{4,12},{5,13},{6,14},{7,15},{8,0},{9,1},... | collective-permute-start | bytes 196616 | tf_op jit(solution)/shard_map/ppermute | solution.py:222
  16.7 6.7 %collective-permute-start.9 = (bf16[16,8192]{1,0:T(8,128)(2,1)S(1)}, bf16[16,8192]{1,0:T(8,128)(2,1)S(1)}, u32[]{:S(2)}, u32[]{:S(2)}) collective-permute-start(bf16[16,8192]{1,0:T(8,128)(2,1)S(1)} %pad_maximum_fusion), channel_id=1, source_target_pairs={{0,2},{1,3},{2,0},{3,1},{4,6},{5,7},{6,4},{7,5},{8,10},{9,11},{10,... | collective-permute-start | bytes 786440 | tf_op jit(solution)/shard_map/ppermute | solution.py:222
  17.9 6.8 %collective-permute-start.7 = (bf16[16,8192]{1,0:T(8,128)(2,1)S(1)}, bf16[16,8192]{1,0:T(8,128)(2,1)S(1)}, u32[]{:S(2)}, u32[]{:S(2)}) collective-permute-start(bf16[16,8192]{1,0:T(8,128)(2,1)S(1)} %pad_maximum_fusion), channel_id=1, source_target_pairs={{0,4},{1,5},{2,6},{3,7},{4,0},{5,1},{6,2},{7,3},{8,12},{9,13},{10,... | collective-permute-start | bytes 786440 | tf_op jit(solution)/shard_map/ppermute | solution.py:222
  19.2 6.8 %collective-permute-start.5 = (f32[128,128]{1,0:T(8,128)S(1)}, f32[128,128]{1,0:T(8,128)S(1)}, u32[]{:S(2)}, u32[]{:S(2)}) collective-permute-start(f32[128,128]{1,0:T(8,128)S(1)} %add.17), channel_id=1, source_target_pairs={{0,16},{1,17},{2,18},{3,19},{4,20},{5,21},{6,22},{7,23},{8,24},{9,... | collective-permute-start | bytes 196616 | tf_op jit(solution)/shard_map/ppermute | solution.py:222
  23.4 6.8 %collective-permute-start.10 = (bf16[8,8192]{1,0:T(8,128)(2,1)S(1)}, bf16[8,8192]{1,0:T(8,128)(2,1)S(1)}, u32[]{:S(2)}, u32[]{:S(2)}) collective-permute-start(bf16[8,8192]{1,0:T(8,128)(2,1)S(1)} %slice.9), channel_id=1, source_target_pairs={{0,4},{1,5},{2,6},{3,7},{4,0},{5,1},{6,2},{7,3},{8,12},{9,13},{10,... | collective-permute-start | bytes 393224 | tf_op jit(solution)/shard_map/ppermute | solution.py:222
  24.7 5.5 %collective-permute-start.8 = (bf16[8,8192]{1,0:T(8,128)(2,1)S(1)}, bf16[8,8192]{1,0:T(8,128)(2,1)S(1)}, u32[]{:S(2)}, u32[]{:S(2)}) collective-permute-start(bf16[8,8192]{1,0:T(8,128)(2,1)S(1)} %slice.8), channel_id=1, source_target_pairs={{0,2},{1,3},{2,0},{3,1},{4,6},{5,7},{6,4},{7,5},{8,10},{9,11},{10,... | collective-permute-start | bytes 393224 | tf_op jit(solution)/shard_map/ppermute | solution.py:222
  26.0 4.2 %collective-permute-start.6 = (f32[128,128]{1,0:T(8,128)S(1)}, f32[128,128]{1,0:T(8,128)S(1)}, u32[]{:S(2)}, u32[]{:S(2)}) collective-permute-start(f32[128,128]{1,0:T(8,128)S(1)} %add.15), channel_id=1, source_target_pairs={{0,4},{1,5},{2,6},{3,7},{4,0},{5,1},{6,2},{7,3},{8,12},{9,13},{10,... | collective-permute-start | bytes 196616 | tf_op jit(solution)/shard_map/ppermute | solution.py:222
  30.3 5.4 %collective-permute-start.11 = (bf16[64,8192]{1,0:T(8,128)(2,1)S(1)}, bf16[64,8192]{1,0:T(8,128)(2,1)S(1)}, u32[]{:S(2)}, u32[]{:S(2)}) collective-permute-start(bf16[64,8192]{1,0:T(8,128)(2,1)S(1)} %constant_dynamic-update-slice_fusion.refs_0_), channel_id=1, source_target_pairs={{0,1},{1,0},{2,3},{3,2},{4,5},{5,4},{6,7},{7,6},{8,9},{9,8},{10,11... | collective-permute-start | bytes 3145736 | tf_op jit(solution)/shard_map/ppermute | solution.py:222

commit v7 on v6

--- a/solution.py
+++ b/solution.py
@@ -75,16 +75,20 @@
         both[e, tokens, :wide] = dot(x[i], pin_t[...]).astype(jnp.bfloat16)
         both[e, tokens, wide:] = over_last(g[i], pout[...]).astype(jnp.bfloat16)
 
+    total = jnp.zeros((wide + narrow, wide + narrow), jnp.float32)
     for e in range(examples):
         sums = over_first(both[e], both[e])
         grads_ref[e] = sums[wide:, :wide]
-        low = jnp.concatenate([sums[wide:, wide:], sums[narrow:wide, narrow:wide]], axis=1)
-        if e == 0:
-            packed_ref[:narrow] = sums[:narrow, :wide]
-            packed_ref[narrow:] = low
-        else:
-            packed_ref[:narrow] += sums[:narrow, :wide]
-            packed_ref[narrow:] += low
+        total = total + sums
+    row = lax.broadcasted_iota(jnp.int32, (narrow, narrow), 0)
+    col = lax.broadcasted_iota(jnp.int32, (narrow, narrow), 1)
+    small = total[wide:, wide:]
+    diagonal = jnp.sum(jnp.where(row == col, small, 0.0), axis=0, keepdims=True)
+    spare = jnp.where(row == narrow - 1, diagonal, diagonal[:, narrow - 1 :])
+    packed_ref[:narrow, :narrow] = jnp.where(col < row, small, total[:narrow, :narrow])
+    packed_ref[:narrow, narrow:] = jnp.where(col < row, spare, total[narrow:wide, narrow:wide])
+    packed_ref[narrow:, :narrow] = total[: narrow // 2, narrow:wide]
+    packed_ref[narrow:, narrow:] = total[narrow // 2 : narrow, narrow:wide]
 
 
 def project(x, g, pin, pout):
@@ -96,7 +100,7 @@
     return pl.pallas_call(
         project_kernel,
         out_shape=[
-            pltpu.VMEM((wide, wide), jnp.float32),
+            pltpu.VMEM((narrow + narrow // 2, wide), jnp.float32),
             pltpu.VMEM((examples, narrow, wide), jnp.float32),
         ],
         in_specs=[pl.BlockSpec(memory_space=pl.ANY)] * 4,
@@ -136,13 +140,32 @@
 
 
 def precond_kernel(tokens, packed_ref, grads_ref, out_ref):
-    wide = packed_ref.shape[0]
+    wide = packed_ref.shape[1]
     examples, narrow, _ = grads_ref.shape
     packed = packed_ref[...]
-    upper = packed[:narrow]
-    lower = jnp.concatenate([upper[:, narrow:].T, packed[narrow:, narrow:]], axis=1)
-    yi, scale_in, _ = normalised(jnp.concatenate([upper, lower], axis=0))
-    yo, scale_out, eye = normalised(packed[narrow:, :narrow])
+    row = lax.broadcasted_iota(jnp.int32, (narrow, narrow), 0)
+    col = lax.broadcasted_iota(jnp.int32, (narrow, narrow), 1)
+    left, right = packed[:narrow, :narrow], packed[:narrow, narrow:]
+    corner = jnp.concatenate([packed[narrow:, :narrow], packed[narrow:, narrow:]], axis=0)
+    zero = jnp.zeros((narrow, narrow), jnp.float32)
+    above = jnp.concatenate(
+        [
+            jnp.concatenate([jnp.where(col > row, left, 0.0), corner], axis=1),
+            jnp.concatenate([zero, jnp.where(col > row, right, 0.0)], axis=1),
+        ],
+        axis=0,
+    )
+    middle = jnp.concatenate(
+        [
+            jnp.concatenate([jnp.where(col == row, left, 0.0), zero], axis=1),
+            jnp.concatenate([zero, jnp.where(col == row, right, 0.0)], axis=1),
+        ],
+        axis=0,
+    )
+    yi, scale_in, _ = normalised(above + above.T + middle)
+    below = jnp.where(col < row, left, 0.0)
+    diagonal = jnp.where(col[:1] < narrow - 1, right[narrow - 1 :], right[narrow - 2 : narrow - 1, :1])
+    yo, scale_out, eye = normalised(below + below.T + jnp.where(col == row, diagonal, 0.0))
     w = grads_ref[...].reshape(examples * narrow, wide)
     xo = jnp.where(eye, 1.0, 0.0)
     wides, narrows = factors(wide), factors(narrow)
@@ -257,7 +280,7 @@
     packed = add_late(packed, exchange(packed, 8, devices))
     bit = 16
     while bit < devices:
-        packed = packed + exchange(packed, bit, devices)
+        packed = add_late(packed, exchange(packed, bit, devices), LONG // 5)
         bit *= 2
     c, c_off = exchange(b[:rows], 2, devices), [k ^ 2 for k in b_off[:half]]
     d, d_off = exchange(a[rows:], 4, devices), [k ^ 4 for k in a_off[half:]]

time: 37.2 us -> 36.7 us (0.987)
  waiting for transfers between devices: 10.5 us -> 9.53 us
    ppermute x12, waiting for transfers between devices: 10.5 us -> 9.53 us  [exchange(): return lax.ppermute(x, 'ex', [(i, i ^ bit) for i in range(devices)])]
  transfers between devices with their start and end apart: 12 -> 12, of which waited for: 4 -> 4; matrix products, arithmetic and copies ran while one was open for 0% -> 0% of each run, Pallas kernels for 23% -> 24%
where the time goes in v7:
time: 36.7 us; the launch traced here: 36.6 us
  starting transfers between devices  16.6 us (45%)
  Pallas kernels  10 us (27%)
  waiting for transfers between devices  9.53 us (26%)
    ppermute x12, starting transfers between devices, exchange(): return lax.ppermute(x, 'ex', [(i, i ^ bit) for i in range(devices)])  16.6 us
    ppermute x12, waiting for transfers between devices, exchange(): return lax.ppermute(x, 'ex', [(i, i ^ bit) for i in range(devices)])  9.53 us
    pallas_call x1, Pallas kernels, project(): pl.pallas_call(project_kernel, out_shape=[pltpu.VMEM((narrow + narrow //...  6.13 us
    pallas_call x1, Pallas kernels, precondition(): pl.pallas_call(functools.partial(precond_kernel, float(tokens)), out_shap...  2.62 us
    pallas_call x1, Pallas kernels, score(): pl.pallas_call(functools.partial(score_kernel, sources, scale), out_shape...  1.28 us
  transfers between devices with their start and end apart: 12, of which 4 were waited for; matrix products, arithmetic and copies ran while one was open for 0% of the time, Pallas kernels for 24%

profile of v7, /device:TPU:1, one launch (start us, length us, event | category | flops | bytes accessed | tf_op | source)
XLA Modules:
  0.0 36.6 jit_solution(935235539204356702)
XLA Ops:
  0.0 0.0 copy-start
  0.0 3.1 %collective-permute-start = (bf16[4,8192]{1,0:T(4,128)(2,1)}, bf16[4,8192]{1,0:T(4,128)(2,1)S(1)}, u32[]{:S(2)}, u32[]{:S(2)}) collective-permute-start(bf16[4,8192]{1,0:T(4,128)(2,1)} %param.9), channel_id=1, source_target_pairs={{0,16},{1,17},{2,18},{3,19},{4,20},{5,21},{6,22},{7,23},{8,24},{9,... | collective-permute-start | bytes 196616 | tf_op jit(solution)/shard_map/ppermute | solution.py:245
  3.1 6.1 %project.1 = (f32[96,128]{1,0:T(8,128)S(1)}, f32[1,64,128]{2,1,0:T(8,128)S(1)}) custom-call(bf16[1,1024,4096]{2,1,0:T(8,128)(2,1)} %x_hbm.1, bf16[1,1024,1024]{2,1,0:T(8,128)(2,1)} %g_hbm.1, bf16[128,4096]{1,0:T(8,128)(2,1)} %pin_hbm.1, bf16[64,1024]{1,0:T(8,128)(2,1)} %pout_hbm.1), custom_call_target="tpu_custom_call" | custom-call | tf_op jit(solution)/shard_map/project/pallas_call | solution.py:100
  9.3 0.0 collective-permute-done
  9.3 0.0 copy-done
  9.3 0.1 pad_maximum_fusion.1
  9.4 1.4 %collective-permute-start.3 = (bf16[8,8192]{1,0:T(8,128)(2,1)S(1)}, bf16[8,8192]{1,0:T(8,128)(2,1)S(1)}, u32[]{:S(2)}, u32[]{:S(2)}) collective-permute-start(bf16[8,8192]{1,0:T(8,128)(2,1)S(1)} %pad_maximum_fusion.1), channel_id=1, source_target_pairs={{0,8},{1,9},{2,10},{3,11},{4,12},{5,13},{6,14},{7,15},{8,0},{9,1},... | collective-permute-start | bytes 393224 | tf_op jit(solution)/shard_map/ppermute | solution.py:245
  10.7 1.2 %collective-permute-start.1 = (f32[96,128]{1,0:T(8,128)S(1)}, f32[96,128]{1,0:T(8,128)S(1)}, u32[]{:S(2)}, u32[]{:S(2)}) collective-permute-start(f32[96,128]{1,0:T(8,128)S(1)} %get-tuple-element.22), channel_id=1, source_target_pairs={{0,1},{1,0},{2,3},{3,2},{4,5},{5,4},{6,7},{7,6},{8,9},{9,8},{10,11... | collective-permute-start | bytes 147464 | tf_op jit(solution)/shard_map/ppermute | solution.py:245
  12.0 0.9 %collective-permute-done.1 = f32[96,128]{1,0:T(8,128)S(1)} collective-permute-done((f32[96,128]{1,0:T(8,128)S(1)}, f32[96,128]{1,0:T(8,128)S(1)}, u32[]{:S(2)}, u32[]{:S(2)}) %collective-permute-start.1) | collective-permute-done | bytes 49184 | tf_op jit(solution)/shard_map/ppermute | solution.py:245
  12.9 1.2 %collective-permute-start.2 = (f32[96,128]{1,0:T(8,128)S(1)}, f32[96,128]{1,0:T(8,128)S(1)}, u32[]{:S(2)}, u32[]{:S(2)}) collective-permute-start(f32[96,128]{1,0:T(8,128)S(1)} %add.11), channel_id=1, source_target_pairs={{0,2},{1,3},{2,0},{3,1},{4,6},{5,7},{6,4},{7,5},{8,10},{9,11},{10,... | collective-permute-start | bytes 147464 | tf_op jit(solution)/shard_map/ppermute | solution.py:245
  14.1 1.7 %collective-permute-done.2 = f32[96,128]{1,0:T(8,128)S(1)} collective-permute-done((f32[96,128]{1,0:T(8,128)S(1)}, f32[96,128]{1,0:T(8,128)S(1)}, u32[]{:S(2)}, u32[]{:S(2)}) %collective-permute-start.2) | collective-permute-done | bytes 49184 | tf_op jit(solution)/shard_map/ppermute | solution.py:245
  15.8 0.0 collective-permute-done.3
  15.8 0.5 %collective-permute-start.4 = (f32[96,128]{1,0:T(8,128)S(1)}, f32[96,128]{1,0:T(8,128)S(1)}, u32[]{:S(2)}, u32[]{:S(2)}) collective-permute-start(f32[96,128]{1,0:T(8,128)S(1)} %add.12.a_ref), channel_id=1, source_target_pairs={{0,8},{1,9},{2,10},{3,11},{4,12},{5,13},{6,14},{7,15},{8,0},{9,1},... | collective-permute-start | bytes 147464 | tf_op jit(solution)/shard_map/ppermute | solution.py:245
  16.4 1.2 %collective-permute-start.9 = (bf16[16,8192]{1,0:T(8,128)(2,1)S(1)}, bf16[16,8192]{1,0:T(8,128)(2,1)S(1)}, u32[]{:S(2)}, u32[]{:S(2)}) collective-permute-start(bf16[16,8192]{1,0:T(8,128)(2,1)S(1)} %pad_maximum_fusion), channel_id=1, source_target_pairs={{0,2},{1,3},{2,0},{3,1},{4,6},{5,7},{6,4},{7,5},{8,10},{9,11},{10,... | collective-permute-start | bytes 786440 | tf_op jit(solution)/shard_map/ppermute | solution.py:245
  17.6 1.2 %collective-permute-start.7 = (bf16[16,8192]{1,0:T(8,128)(2,1)S(1)}, bf16[16,8192]{1,0:T(8,128)(2,1)S(1)}, u32[]{:S(2)}, u32[]{:S(2)}) collective-permute-start(bf16[16,8192]{1,0:T(8,128)(2,1)S(1)} %pad_maximum_fusion), channel_id=1, source_target_pairs={{0,4},{1,5},{2,6},{3,7},{4,0},{5,1},{6,2},{7,3},{8,12},{9,13},{10,... | collective-permute-start | bytes 786440 | tf_op jit(solution)/shard_map/ppermute | solution.py:245
  18.8 0.0 collective-permute-done.4.b_ref
  18.9 0.1 collective-permute-start.5
  19.0 3.7 %collective-permute-done.9 = bf16[16,8192]{1,0:T(8,128)(2,1)S(1)} collective-permute-done((bf16[16,8192]{1,0:T(8,128)(2,1)S(1)}, bf16[16,8192]{1,0:T(8,128)(2,1)S(1)}, u32[]{:S(2)}, u32[]{:S(2)}) %collective-permute-start.9) | collective-permute-done | bytes 262176 | tf_op jit(solution)/shard_map/ppermute | solution.py:245
  22.6 1.3 %collective-permute-start.10 = (bf16[8,8192]{1,0:T(8,128)(2,1)S(1)}, bf16[8,8192]{1,0:T(8,128)(2,1)S(1)}, u32[]{:S(2)}, u32[]{:S(2)}) collective-permute-start(bf16[8,8192]{1,0:T(8,128)(2,1)S(1)} %slice.9), channel_id=1, source_target_pairs={{0,4},{1,5},{2,6},{3,7},{4,0},{5,1},{6,2},{7,3},{8,12},{9,13},{10,... | collective-permute-start | bytes 393224 | tf_op jit(solution)/shard_map/ppermute | solution.py:245
  23.9 0.0 collective-permute-done.7
  24.0 1.3 %collective-permute-start.8 = (bf16[8,8192]{1,0:T(8,128)(2,1)S(1)}, bf16[8,8192]{1,0:T(8,128)(2,1)S(1)}, u32[]{:S(2)}, u32[]{:S(2)}) collective-permute-start(bf16[8,8192]{1,0:T(8,128)(2,1)S(1)} %slice.8), channel_id=1, source_target_pairs={{0,2},{1,3},{2,0},{3,1},{4,6},{5,7},{6,4},{7,5},{8,10},{9,11},{10,... | collective-permute-start | bytes 393224 | tf_op jit(solution)/shard_map/ppermute | solution.py:245
  25.2 0.0 collective-permute-done.5.b_ref
  25.2 0.3 collective-permute-start.6
  25.5 3.2 %collective-permute-done.6 = f32[96,128]{1,0:T(8,128)S(1)} collective-permute-done((f32[96,128]{1,0:T(8,128)S(1)}, f32[96,128]{1,0:T(8,128)S(1)}, u32[]{:S(2)}, u32[]{:S(2)}) %collective-permute-start.6) | collective-permute-done | bytes 49184 | tf_op jit(solution)/shard_map/ppermute | solution.py:245
  28.8 0.0 collective-permute-done.10
  28.8 0.0 collective-permute-done.8
  28.9 3.7 %collective-permute-start.11 = (bf16[64,8192]{1,0:T(8,128)(2,1)S(1)}, bf16[64,8192]{1,0:T(8,128)(2,1)S(1)}, u32[]{:S(2)}, u32[]{:S(2)}) collective-permute-start(bf16[64,8192]{1,0:T(8,128)(2,1)S(1)} %constant_dynamic-update-slice_fusion.refs_0_), channel_id=1, source_target_pairs={{0,1},{1,0},{2,3},{3,2},{4,5},{5,4},{6,7},{7,6},{8,9},{9,8},{10,11... | collective-permute-start | bytes 3145736 | tf_op jit(solution)/shard_map/ppermute | solution.py:245
  32.6 2.6 %precondition.1.p_ref = f32[1,64,128]{2,1,0:T(8,128)S(1)} custom-call(f32[96,128]{1,0:T(8,128)S(1)} %add.13.packed_ref, f32[1,64,128]{2,1,0:T(8,128)S(1)} %get-tuple-element.27.grads_ref), custom_call_target="tpu_custom_call" | custom-call | tf_op jit(solution)/shard_map/precondition/pallas_call | solution.py:194
  35.3 0.0 collective-permute-done.11.refs_1_
  35.3 1.3 %score.1 = f32[1,128]{1,0:T(1,128)} custom-call(s32[1]{0:T(128)} %bitcast.me_ref, f32[1,64,128]{2,1,0:T(8,128)S(1)} %precondition.1.p_ref, bf16[64,8192]{1,0:T(8,128)(2,1)S(1)} %constant_dynamic-update-slice_fusion.refs_0_, bf16[64,8192]{1,0:T(8,128)(2,1)S(1)} %collective-permute-done.11.refs_1_), custom_call_target="tpu_custom_call" | custom-call | tf_op jit(solution)/shard_map/score/pallas_call | solution.py:234
  (13 shorter events, 0.2 us)
Async XLA Ops:
  0.0 9.3 %copy-start = (bf16[4,8192]{1,0:T(4,128)(2,1)S(1)}, bf16[4,8192]{1,0:T(4,128)(2,1)}, u32[]{:S(2)}) copy-start(bf16[4,8192]{1,0:T(4,128)(2,1)} %param.9) | copy-start | bytes 196612
  0.0 9.3 %collective-permute-start = (bf16[4,8192]{1,0:T(4,128)(2,1)}, bf16[4,8192]{1,0:T(4,128)(2,1)S(1)}, u32[]{:S(2)}, u32[]{:S(2)}) collective-permute-start(bf16[4,8192]{1,0:T(4,128)(2,1)} %param.9), channel_id=1, source_target_pairs={{0,16},{1,17},{2,18},{3,19},{4,20},{5,21},{6,22},{7,23},{8,24},{9,... | collective-permute-start | bytes 196616 | tf_op jit(solution)/shard_map/ppermute | solution.py:245
  9.4 6.4 %collective-permute-start.3 = (bf16[8,8192]{1,0:T(8,128)(2,1)S(1)}, bf16[8,8192]{1,0:T(8,128)(2,1)S(1)}, u32[]{:S(2)}, u32[]{:S(2)}) collective-permute-start(bf16[8,8192]{1,0:T(8,128)(2,1)S(1)} %pad_maximum_fusion.1), channel_id=1, source_target_pairs={{0,8},{1,9},{2,10},{3,11},{4,12},{5,13},{6,14},{7,15},{8,0},{9,1},... | collective-permute-start | bytes 393224 | tf_op jit(solution)/shard_map/ppermute | solution.py:245
  10.7 2.1 %collective-permute-start.1 = (f32[96,128]{1,0:T(8,128)S(1)}, f32[96,128]{1,0:T(8,128)S(1)}, u32[]{:S(2)}, u32[]{:S(2)}) collective-permute-start(f32[96,128]{1,0:T(8,128)S(1)} %get-tuple-element.22), channel_id=1, source_target_pairs={{0,1},{1,0},{2,3},{3,2},{4,5},{5,4},{6,7},{7,6},{8,9},{9,8},{10,11... | collective-permute-start | bytes 147464 | tf_op jit(solution)/shard_map/ppermute | solution.py:245
  12.9 2.9 %collective-permute-start.2 = (f32[96,128]{1,0:T(8,128)S(1)}, f32[96,128]{1,0:T(8,128)S(1)}, u32[]{:S(2)}, u32[]{:S(2)}) collective-permute-start(f32[96,128]{1,0:T(8,128)S(1)} %add.11), channel_id=1, source_target_pairs={{0,2},{1,3},{2,0},{3,1},{4,6},{5,7},{6,4},{7,5},{8,10},{9,11},{10,... | collective-permute-start | bytes 147464 | tf_op jit(solution)/shard_map/ppermute | solution.py:245
  15.8 3.0 %collective-permute-start.4 = (f32[96,128]{1,0:T(8,128)S(1)}, f32[96,128]{1,0:T(8,128)S(1)}, u32[]{:S(2)}, u32[]{:S(2)}) collective-permute-start(f32[96,128]{1,0:T(8,128)S(1)} %add.12.a_ref), channel_id=1, source_target_pairs={{0,8},{1,9},{2,10},{3,11},{4,12},{5,13},{6,14},{7,15},{8,0},{9,1},... | collective-permute-start | bytes 147464 | tf_op jit(solution)/shard_map/ppermute | solution.py:245
  16.4 6.3 %collective-permute-start.9 = (bf16[16,8192]{1,0:T(8,128)(2,1)S(1)}, bf16[16,8192]{1,0:T(8,128)(2,1)S(1)}, u32[]{:S(2)}, u32[]{:S(2)}) collective-permute-start(bf16[16,8192]{1,0:T(8,128)(2,1)S(1)} %pad_maximum_fusion), channel_id=1, source_target_pairs={{0,2},{1,3},{2,0},{3,1},{4,6},{5,7},{6,4},{7,5},{8,10},{9,11},{10,... | collective-permute-start | bytes 786440 | tf_op jit(solution)/shard_map/ppermute | solution.py:245
  17.6 6.4 %collective-permute-start.7 = (bf16[16,8192]{1,0:T(8,128)(2,1)S(1)}, bf16[16,8192]{1,0:T(8,128)(2,1)S(1)}, u32[]{:S(2)}, u32[]{:S(2)}) collective-permute-start(bf16[16,8192]{1,0:T(8,128)(2,1)S(1)} %pad_maximum_fusion), channel_id=1, source_target_pairs={{0,4},{1,5},{2,6},{3,7},{4,0},{5,1},{6,2},{7,3},{8,12},{9,13},{10,... | collective-permute-start | bytes 786440 | tf_op jit(solution)/shard_map/ppermute | solution.py:245
  18.9 6.4 %collective-permute-start.5 = (f32[96,128]{1,0:T(8,128)S(1)}, f32[96,128]{1,0:T(8,128)S(1)}, u32[]{:S(2)}, u32[]{:S(2)}) collective-permute-start(f32[96,128]{1,0:T(8,128)S(1)} %add.14.a_ref), channel_id=1, source_target_pairs={{0,16},{1,17},{2,18},{3,19},{4,20},{5,21},{6,22},{7,23},{8,24},{9,... | collective-permute-start | bytes 147464 | tf_op jit(solution)/shard_map/ppermute | solution.py:245
  22.6 6.1 %collective-permute-start.10 = (bf16[8,8192]{1,0:T(8,128)(2,1)S(1)}, bf16[8,8192]{1,0:T(8,128)(2,1)S(1)}, u32[]{:S(2)}, u32[]{:S(2)}) collective-permute-start(bf16[8,8192]{1,0:T(8,128)(2,1)S(1)} %slice.9), channel_id=1, source_target_pairs={{0,4},{1,5},{2,6},{3,7},{4,0},{5,1},{6,2},{7,3},{8,12},{9,13},{10,... | collective-permute-start | bytes 393224 | tf_op jit(solution)/shard_map/ppermute | solution.py:245
  24.0 4.8 %collective-permute-start.8 = (bf16[8,8192]{1,0:T(8,128)(2,1)S(1)}, bf16[8,8192]{1,0:T(8,128)(2,1)S(1)}, u32[]{:S(2)}, u32[]{:S(2)}) collective-permute-start(bf16[8,8192]{1,0:T(8,128)(2,1)S(1)} %slice.8), channel_id=1, source_target_pairs={{0,2},{1,3},{2,0},{3,1},{4,6},{5,7},{6,4},{7,5},{8,10},{9,11},{10,... | collective-permute-start | bytes 393224 | tf_op jit(solution)/shard_map/ppermute | solution.py:245
  25.2 3.5 %collective-permute-start.6 = (f32[96,128]{1,0:T(8,128)S(1)}, f32[96,128]{1,0:T(8,128)S(1)}, u32[]{:S(2)}, u32[]{:S(2)}) collective-permute-start(f32[96,128]{1,0:T(8,128)S(1)} %add.15), channel_id=1, source_target_pairs={{0,4},{1,5},{2,6},{3,7},{4,0},{5,1},{6,2},{7,3},{8,12},{9,13},{10,... | collective-permute-start | bytes 147464 | tf_op jit(solution)/shard_map/ppermute | solution.py:245
  28.9 6.4 %collective-permute-start.11 = (bf16[64,8192]{1,0:T(8,128)(2,1)S(1)}, bf16[64,8192]{1,0:T(8,128)(2,1)S(1)}, u32[]{:S(2)}, u32[]{:S(2)}) collective-permute-start(bf16[64,8192]{1,0:T(8,128)(2,1)S(1)} %constant_dynamic-update-slice_fusion.refs_0_), channel_id=1, source_target_pairs={{0,1},{1,0},{2,3},{3,2},{4,5},{5,4},{6,7},{7,6},{8,9},{9,8},{10,11... | collective-permute-start | bytes 3145736 | tf_op jit(solution)/shard_map/ppermute | solution.py:245

commit v8 on v7

--- a/solution.py
+++ b/solution.py
@@ -46,7 +46,7 @@
     pout_copy.start()
 
     def place(i):
-        return i // per, pl.ds(pl.multiple_of((i % per) * rows, rows), rows)
+        return i // per, pl.ds((i % per) * rows, rows)
 
     def copies(i):
         return (
@@ -58,17 +58,18 @@
         for copy in copies(i):
             copy.start()
     pin_copy.wait()
+    if DEPTH < chunks:
+        for copy in copies(DEPTH):
+            copy.start()
     pin_t[...] = pin[...].T
     pout_copy.wait()
 
-    @pl.loop(0, chunks)
-    def _(i):
+    for i in range(chunks):
         for copy in copies(i):
             copy.wait()
 
-        @pl.when(i + DEPTH < chunks)
-        def _():
-            for copy in copies(i + DEPTH):
+        if i + DEPTH + 1 < chunks:
+            for copy in copies(i + DEPTH + 1):
                 copy.start()
 
         e, tokens = place(i)
@@ -207,14 +208,11 @@
     me = me_ref[0]
     lane = lax.broadcasted_iota(jnp.int32, (1, tests), 1)
     for e in range(examples):
-
-        def add(o, sums):
-            p = p_ref[e, pl.ds(o, 1), :]
-            here = pl.ds(pl.multiple_of(o * wide, wide), wide)
-            return tuple(s + t[:, here].astype(jnp.float32) * p for s, t in zip(sums, pieces))
-
-        zeros = tuple(jnp.zeros((t.shape[0], wide), jnp.float32) for t in pieces)
-        sums = lax.fori_loop(0, narrow, add, zeros, unroll=4)
+        sums = [jnp.zeros((t.shape[0], wide), jnp.float32) for t in pieces]
+        for o in range(narrow):
+            p = p_ref[e, o : o + 1, :]
+            here = slice(o * wide, (o + 1) * wide)
+            sums = [s + t[:, here].astype(jnp.float32) * p for s, t in zip(sums, pieces)]
         total = jnp.zeros((1, tests), jnp.float32)
         for s, offsets in zip(sums, sources):
             rows = s.shape[0]

time: 36.7 us -> 36.2 us (0.986)
  Pallas kernels: 10 us -> 9.59 us
where the time goes in v8:
time: 36.2 us; the launch traced here: 36.1 us
  starting transfers between devices  16.7 us (46%)
  Pallas kernels  9.59 us (26%)
  waiting for transfers between devices  9.52 us (26%)
    ppermute x12, starting transfers between devices, exchange(): return lax.ppermute(x, 'ex', [(i, i ^ bit) for i in range(devices)])  16.7 us
    ppermute x12, waiting for transfers between devices, exchange(): return lax.ppermute(x, 'ex', [(i, i ^ bit) for i in range(devices)])  9.52 us
    pallas_call x1, Pallas kernels, project(): pl.pallas_call(project_kernel, out_shape=[pltpu.VMEM((narrow + narrow //...  5.92 us
    pallas_call x1, Pallas kernels, precondition(): pl.pallas_call(functools.partial(precond_kernel, float(tokens)), out_shap...  2.61 us
    pallas_call x1, Pallas kernels, score(): pl.pallas_call(functools.partial(score_kernel, sources, scale), out_shape...  1.04 us
  transfers between devices with their start and end apart: 12, of which 4 were waited for; matrix products, arithmetic and copies ran while one was open for 0% of the time, Pallas kernels for 24%

profile of v8, /device:TPU:1, one launch (start us, length us, event | category | flops | bytes accessed | tf_op | source)
XLA Modules:
  0.0 36.1 jit_solution(18429640724857422145)
XLA Ops:
  0.0 0.0 copy-start
  0.0 3.1 %collective-permute-start = (bf16[4,8192]{1,0:T(4,128)(2,1)}, bf16[4,8192]{1,0:T(4,128)(2,1)S(1)}, u32[]{:S(2)}, u32[]{:S(2)}) collective-permute-start(bf16[4,8192]{1,0:T(4,128)(2,1)} %param.9), channel_id=1, source_target_pairs={{0,16},{1,17},{2,18},{3,19},{4,20},{5,21},{6,22},{7,23},{8,24},{9,... | collective-permute-start | bytes 196616 | tf_op jit(solution)/shard_map/ppermute | solution.py:243
  3.1 5.9 %project.1 = (f32[96,128]{1,0:T(8,128)S(1)}, f32[1,64,128]{2,1,0:T(8,128)S(1)}) custom-call(bf16[1,1024,4096]{2,1,0:T(8,128)(2,1)} %x_hbm.1, bf16[1,1024,1024]{2,1,0:T(8,128)(2,1)} %g_hbm.1, bf16[128,4096]{1,0:T(8,128)(2,1)} %pin_hbm.1, bf16[64,1024]{1,0:T(8,128)(2,1)} %pout_hbm.1), custom_call_target="tpu_custom_call" | custom-call | tf_op jit(solution)/shard_map/project/pallas_call | solution.py:101
  9.1 0.0 collective-permute-done
  9.1 0.0 copy-done
  9.1 0.1 pad_maximum_fusion.1
  9.2 1.4 %collective-permute-start.3 = (bf16[8,8192]{1,0:T(8,128)(2,1)S(1)}, bf16[8,8192]{1,0:T(8,128)(2,1)S(1)}, u32[]{:S(2)}, u32[]{:S(2)}) collective-permute-start(bf16[8,8192]{1,0:T(8,128)(2,1)S(1)} %pad_maximum_fusion.1), channel_id=1, source_target_pairs={{0,8},{1,9},{2,10},{3,11},{4,12},{5,13},{6,14},{7,15},{8,0},{9,1},... | collective-permute-start | bytes 393224 | tf_op jit(solution)/shard_map/ppermute | solution.py:243
  10.5 1.2 %collective-permute-start.1 = (f32[96,128]{1,0:T(8,128)S(1)}, f32[96,128]{1,0:T(8,128)S(1)}, u32[]{:S(2)}, u32[]{:S(2)}) collective-permute-start(f32[96,128]{1,0:T(8,128)S(1)} %get-tuple-element.22), channel_id=1, source_target_pairs={{0,1},{1,0},{2,3},{3,2},{4,5},{5,4},{6,7},{7,6},{8,9},{9,8},{10,11... | collective-permute-start | bytes 147464 | tf_op jit(solution)/shard_map/ppermute | solution.py:243
  11.8 0.9 %collective-permute-done.1 = f32[96,128]{1,0:T(8,128)S(1)} collective-permute-done((f32[96,128]{1,0:T(8,128)S(1)}, f32[96,128]{1,0:T(8,128)S(1)}, u32[]{:S(2)}, u32[]{:S(2)}) %collective-permute-start.1) | collective-permute-done | bytes 49184 | tf_op jit(solution)/shard_map/ppermute | solution.py:243
  12.6 1.2 %collective-permute-start.2 = (f32[96,128]{1,0:T(8,128)S(1)}, f32[96,128]{1,0:T(8,128)S(1)}, u32[]{:S(2)}, u32[]{:S(2)}) collective-permute-start(f32[96,128]{1,0:T(8,128)S(1)} %add.11), channel_id=1, source_target_pairs={{0,2},{1,3},{2,0},{3,1},{4,6},{5,7},{6,4},{7,5},{8,10},{9,11},{10,... | collective-permute-start | bytes 147464 | tf_op jit(solution)/shard_map/ppermute | solution.py:243
  13.9 1.7 %collective-permute-done.2 = f32[96,128]{1,0:T(8,128)S(1)} collective-permute-done((f32[96,128]{1,0:T(8,128)S(1)}, f32[96,128]{1,0:T(8,128)S(1)}, u32[]{:S(2)}, u32[]{:S(2)}) %collective-permute-start.2) | collective-permute-done | bytes 49184 | tf_op jit(solution)/shard_map/ppermute | solution.py:243
  15.6 0.0 collective-permute-done.3
  15.6 0.5 %collective-permute-start.4 = (f32[96,128]{1,0:T(8,128)S(1)}, f32[96,128]{1,0:T(8,128)S(1)}, u32[]{:S(2)}, u32[]{:S(2)}) collective-permute-start(f32[96,128]{1,0:T(8,128)S(1)} %add.12.a_ref), channel_id=1, source_target_pairs={{0,8},{1,9},{2,10},{3,11},{4,12},{5,13},{6,14},{7,15},{8,0},{9,1},... | collective-permute-start | bytes 147464 | tf_op jit(solution)/shard_map/ppermute | solution.py:243
  16.2 1.2 %collective-permute-start.9 = (bf16[16,8192]{1,0:T(8,128)(2,1)S(1)}, bf16[16,8192]{1,0:T(8,128)(2,1)S(1)}, u32[]{:S(2)}, u32[]{:S(2)}) collective-permute-start(bf16[16,8192]{1,0:T(8,128)(2,1)S(1)} %pad_maximum_fusion), channel_id=1, source_target_pairs={{0,2},{1,3},{2,0},{3,1},{4,6},{5,7},{6,4},{7,5},{8,10},{9,11},{10,... | collective-permute-start | bytes 786440 | tf_op jit(solution)/shard_map/ppermute | solution.py:243
  17.4 1.2 %collective-permute-start.7 = (bf16[16,8192]{1,0:T(8,128)(2,1)S(1)}, bf16[16,8192]{1,0:T(8,128)(2,1)S(1)}, u32[]{:S(2)}, u32[]{:S(2)}) collective-permute-start(bf16[16,8192]{1,0:T(8,128)(2,1)S(1)} %pad_maximum_fusion), channel_id=1, source_target_pairs={{0,4},{1,5},{2,6},{3,7},{4,0},{5,1},{6,2},{7,3},{8,12},{9,13},{10,... | collective-permute-start | bytes 786440 | tf_op jit(solution)/shard_map/ppermute | solution.py:243
  18.6 0.0 collective-permute-done.4.b_ref
  18.6 0.1 collective-permute-start.5
  18.8 3.7 %collective-permute-done.9 = bf16[16,8192]{1,0:T(8,128)(2,1)S(1)} collective-permute-done((bf16[16,8192]{1,0:T(8,128)(2,1)S(1)}, bf16[16,8192]{1,0:T(8,128)(2,1)S(1)}, u32[]{:S(2)}, u32[]{:S(2)}) %collective-permute-start.9) | collective-permute-done | bytes 262176 | tf_op jit(solution)/shard_map/ppermute | solution.py:243
  22.4 1.3 %collective-permute-start.10 = (bf16[8,8192]{1,0:T(8,128)(2,1)S(1)}, bf16[8,8192]{1,0:T(8,128)(2,1)S(1)}, u32[]{:S(2)}, u32[]{:S(2)}) collective-permute-start(bf16[8,8192]{1,0:T(8,128)(2,1)S(1)} %slice.9), channel_id=1, source_target_pairs={{0,4},{1,5},{2,6},{3,7},{4,0},{5,1},{6,2},{7,3},{8,12},{9,13},{10,... | collective-permute-start | bytes 393224 | tf_op jit(solution)/shard_map/ppermute | solution.py:243
  23.7 0.0 collective-permute-done.7
  23.7 1.3 %collective-permute-start.8 = (bf16[8,8192]{1,0:T(8,128)(2,1)S(1)}, bf16[8,8192]{1,0:T(8,128)(2,1)S(1)}, u32[]{:S(2)}, u32[]{:S(2)}) collective-permute-start(bf16[8,8192]{1,0:T(8,128)(2,1)S(1)} %slice.8), channel_id=1, source_target_pairs={{0,2},{1,3},{2,0},{3,1},{4,6},{5,7},{6,4},{7,5},{8,10},{9,11},{10,... | collective-permute-start | bytes 393224 | tf_op jit(solution)/shard_map/ppermute | solution.py:243
  25.0 0.0 collective-permute-done.5.b_ref
  25.0 0.3 collective-permute-start.6
  25.3 3.2 %collective-permute-done.6 = f32[96,128]{1,0:T(8,128)S(1)} collective-permute-done((f32[96,128]{1,0:T(8,128)S(1)}, f32[96,128]{1,0:T(8,128)S(1)}, u32[]{:S(2)}, u32[]{:S(2)}) %collective-permute-start.6) | collective-permute-done | bytes 49184 | tf_op jit(solution)/shard_map/ppermute | solution.py:243
  28.5 0.0 collective-permute-done.10
  28.6 0.0 collective-permute-done.8
  28.7 3.7 %collective-permute-start.11 = (bf16[64,8192]{1,0:T(8,128)(2,1)S(1)}, bf16[64,8192]{1,0:T(8,128)(2,1)S(1)}, u32[]{:S(2)}, u32[]{:S(2)}) collective-permute-start(bf16[64,8192]{1,0:T(8,128)(2,1)S(1)} %constant_dynamic-update-slice_fusion.refs_0_), channel_id=1, source_target_pairs={{0,1},{1,0},{2,3},{3,2},{4,5},{5,4},{6,7},{7,6},{8,9},{9,8},{10,11... | collective-permute-start | bytes 3145736 | tf_op jit(solution)/shard_map/ppermute | solution.py:243
  32.4 2.6 %precondition.1.p_ref = f32[1,64,128]{2,1,0:T(8,128)S(1)} custom-call(f32[96,128]{1,0:T(8,128)S(1)} %add.13.packed_ref, f32[1,64,128]{2,1,0:T(8,128)S(1)} %get-tuple-element.27.grads_ref), custom_call_target="tpu_custom_call" | custom-call | tf_op jit(solution)/shard_map/precondition/pallas_call | solution.py:195
  35.0 0.0 collective-permute-done.11.refs_1_
  35.1 1.0 %score.1 = f32[1,128]{1,0:T(1,128)} custom-call(s32[1]{0:T(128)} %bitcast.me_ref, f32[1,64,128]{2,1,0:T(8,128)S(1)} %precondition.1.p_ref, bf16[64,8192]{1,0:T(8,128)(2,1)S(1)} %constant_dynamic-update-slice_fusion.refs_0_, bf16[64,8192]{1,0:T(8,128)(2,1)S(1)} %collective-permute-done.11.refs_1_), custom_call_target="tpu_custom_call" | custom-call | tf_op jit(solution)/shard_map/score/pallas_call | solution.py:232
  (13 shorter events, 0.2 us)
Async XLA Ops:
  0.0 9.1 %copy-start = (bf16[4,8192]{1,0:T(4,128)(2,1)S(1)}, bf16[4,8192]{1,0:T(4,128)(2,1)}, u32[]{:S(2)}) copy-start(bf16[4,8192]{1,0:T(4,128)(2,1)} %param.9) | copy-start | bytes 196612
  0.0 9.1 %collective-permute-start = (bf16[4,8192]{1,0:T(4,128)(2,1)}, bf16[4,8192]{1,0:T(4,128)(2,1)S(1)}, u32[]{:S(2)}, u32[]{:S(2)}) collective-permute-start(bf16[4,8192]{1,0:T(4,128)(2,1)} %param.9), channel_id=1, source_target_pairs={{0,16},{1,17},{2,18},{3,19},{4,20},{5,21},{6,22},{7,23},{8,24},{9,... | collective-permute-start | bytes 196616 | tf_op jit(solution)/shard_map/ppermute | solution.py:243
  9.2 6.4 %collective-permute-start.3 = (bf16[8,8192]{1,0:T(8,128)(2,1)S(1)}, bf16[8,8192]{1,0:T(8,128)(2,1)S(1)}, u32[]{:S(2)}, u32[]{:S(2)}) collective-permute-start(bf16[8,8192]{1,0:T(8,128)(2,1)S(1)} %pad_maximum_fusion.1), channel_id=1, source_target_pairs={{0,8},{1,9},{2,10},{3,11},{4,12},{5,13},{6,14},{7,15},{8,0},{9,1},... | collective-permute-start | bytes 393224 | tf_op jit(solution)/shard_map/ppermute | solution.py:243
  10.5 2.1 %collective-permute-start.1 = (f32[96,128]{1,0:T(8,128)S(1)}, f32[96,128]{1,0:T(8,128)S(1)}, u32[]{:S(2)}, u32[]{:S(2)}) collective-permute-start(f32[96,128]{1,0:T(8,128)S(1)} %get-tuple-element.22), channel_id=1, source_target_pairs={{0,1},{1,0},{2,3},{3,2},{4,5},{5,4},{6,7},{7,6},{8,9},{9,8},{10,11... | collective-permute-start | bytes 147464 | tf_op jit(solution)/shard_map/ppermute | solution.py:243
  12.6 2.9 %collective-permute-start.2 = (f32[96,128]{1,0:T(8,128)S(1)}, f32[96,128]{1,0:T(8,128)S(1)}, u32[]{:S(2)}, u32[]{:S(2)}) collective-permute-start(f32[96,128]{1,0:T(8,128)S(1)} %add.11), channel_id=1, source_target_pairs={{0,2},{1,3},{2,0},{3,1},{4,6},{5,7},{6,4},{7,5},{8,10},{9,11},{10,... | collective-permute-start | bytes 147464 | tf_op jit(solution)/shard_map/ppermute | solution.py:243
  15.6 3.0 %collective-permute-start.4 = (f32[96,128]{1,0:T(8,128)S(1)}, f32[96,128]{1,0:T(8,128)S(1)}, u32[]{:S(2)}, u32[]{:S(2)}) collective-permute-start(f32[96,128]{1,0:T(8,128)S(1)} %add.12.a_ref), channel_id=1, source_target_pairs={{0,8},{1,9},{2,10},{3,11},{4,12},{5,13},{6,14},{7,15},{8,0},{9,1},... | collective-permute-start | bytes 147464 | tf_op jit(solution)/shard_map/ppermute | solution.py:243
  16.2 6.3 %collective-permute-start.9 = (bf16[16,8192]{1,0:T(8,128)(2,1)S(1)}, bf16[16,8192]{1,0:T(8,128)(2,1)S(1)}, u32[]{:S(2)}, u32[]{:S(2)}) collective-permute-start(bf16[16,8192]{1,0:T(8,128)(2,1)S(1)} %pad_maximum_fusion), channel_id=1, source_target_pairs={{0,2},{1,3},{2,0},{3,1},{4,6},{5,7},{6,4},{7,5},{8,10},{9,11},{10,... | collective-permute-start | bytes 786440 | tf_op jit(solution)/shard_map/ppermute | solution.py:243
  17.4 6.4 %collective-permute-start.7 = (bf16[16,8192]{1,0:T(8,128)(2,1)S(1)}, bf16[16,8192]{1,0:T(8,128)(2,1)S(1)}, u32[]{:S(2)}, u32[]{:S(2)}) collective-permute-start(bf16[16,8192]{1,0:T(8,128)(2,1)S(1)} %pad_maximum_fusion), channel_id=1, source_target_pairs={{0,4},{1,5},{2,6},{3,7},{4,0},{5,1},{6,2},{7,3},{8,12},{9,13},{10,... | collective-permute-start | bytes 786440 | tf_op jit(solution)/shard_map/ppermute | solution.py:243
  18.6 6.4 %collective-permute-start.5 = (f32[96,128]{1,0:T(8,128)S(1)}, f32[96,128]{1,0:T(8,128)S(1)}, u32[]{:S(2)}, u32[]{:S(2)}) collective-permute-start(f32[96,128]{1,0:T(8,128)S(1)} %add.14.a_ref), channel_id=1, source_target_pairs={{0,16},{1,17},{2,18},{3,19},{4,20},{5,21},{6,22},{7,23},{8,24},{9,... | collective-permute-start | bytes 147464 | tf_op jit(solution)/shard_map/ppermute | solution.py:243
  22.4 6.1 %collective-permute-start.10 = (bf16[8,8192]{1,0:T(8,128)(2,1)S(1)}, bf16[8,8192]{1,0:T(8,128)(2,1)S(1)}, u32[]{:S(2)}, u32[]{:S(2)}) collective-permute-start(bf16[8,8192]{1,0:T(8,128)(2,1)S(1)} %slice.9), channel_id=1, source_target_pairs={{0,4},{1,5},{2,6},{3,7},{4,0},{5,1},{6,2},{7,3},{8,12},{9,13},{10,... | collective-permute-start | bytes 393224 | tf_op jit(solution)/shard_map/ppermute | solution.py:243
  23.7 4.8 %collective-permute-start.8 = (bf16[8,8192]{1,0:T(8,128)(2,1)S(1)}, bf16[8,8192]{1,0:T(8,128)(2,1)S(1)}, u32[]{:S(2)}, u32[]{:S(2)}) collective-permute-start(bf16[8,8192]{1,0:T(8,128)(2,1)S(1)} %slice.8), channel_id=1, source_target_pairs={{0,2},{1,3},{2,0},{3,1},{4,6},{5,7},{6,4},{7,5},{8,10},{9,11},{10,... | collective-permute-start | bytes 393224 | tf_op jit(solution)/shard_map/ppermute | solution.py:243
  25.0 3.5 %collective-permute-start.6 = (f32[96,128]{1,0:T(8,128)S(1)}, f32[96,128]{1,0:T(8,128)S(1)}, u32[]{:S(2)}, u32[]{:S(2)}) collective-permute-start(f32[96,128]{1,0:T(8,128)S(1)} %add.15), channel_id=1, source_target_pairs={{0,4},{1,5},{2,6},{3,7},{4,0},{5,1},{6,2},{7,3},{8,12},{9,13},{10,... | collective-permute-start | bytes 147464 | tf_op jit(solution)/shard_map/ppermute | solution.py:243
  28.7 6.4 %collective-permute-start.11 = (bf16[64,8192]{1,0:T(8,128)(2,1)S(1)}, bf16[64,8192]{1,0:T(8,128)(2,1)S(1)}, u32[]{:S(2)}, u32[]{:S(2)}) collective-permute-start(bf16[64,8192]{1,0:T(8,128)(2,1)S(1)} %constant_dynamic-update-slice_fusion.refs_0_), channel_id=1, source_target_pairs={{0,1},{1,0},{2,3},{3,2},{4,5},{5,4},{6,7},{7,6},{8,9},{9,8},{10,11... | collective-permute-start | bytes 3145736 | tf_op jit(solution)/shard_map/ppermute | solution.py:243

commit v9 on v8

--- a/solution.py
+++ b/solution.py
@@ -21,6 +21,16 @@
 
 def exact(a, b):
     return jnp.dot(a, b, precision=HIGHEST, preferred_element_type=jnp.float32)
+
+
+def halves(a):
+    high = a.astype(jnp.bfloat16)
+    return high, (a - high.astype(jnp.float32)).astype(jnp.bfloat16)
+
+
+def near_exact(a, b):
+    (a_high, a_low), (b_high, b_low) = halves(a), halves(b)
+    return dot(a_high, b_high) + (dot(a_low, b_high) + dot(a_high, b_low))
 
 
 def over_last(a, b):
@@ -171,23 +181,24 @@
     xo = jnp.where(eye, 1.0, 0.0)
     wides, narrows = factors(wide), factors(narrow)
     for k in range(max(len(wides), len(narrows))):
+        times = exact if k < 5 else near_exact
         if k < len(wides):
             if k < len(wides) - 1:
                 both = jnp.concatenate([yi, w], axis=0)
-                both = wides[k] * (2 * both - exact(both, yi))
+                both = wides[k] * (2 * both - times(both, yi))
                 yi, w = both[:wide], both[wide:]
             else:
-                w = wides[k] * (2 * w - exact(w, yi))
+                w = wides[k] * (2 * w - times(w, yi))
         if k < len(narrows):
             if k < len(narrows) - 1:
                 both = jnp.concatenate([yo, xo], axis=0)
-                both = narrows[k] * (2 * both - exact(both, yo))
+                both = narrows[k] * (2 * both - times(both, yo))
                 yo, xo = both[:narrow], both[narrow:]
             else:
-                xo = narrows[k] * (2 * xo - exact(xo, yo))
+                xo = narrows[k] * (2 * xo - times(xo, yo))
     scale = (scale_in * tokens) * (scale_out * tokens)
     for e in range(examples):
-        both = exact(xo, w[e * narrow : (e + 1) * narrow]) * scale
+        both = near_exact(xo, w[e * narrow : (e + 1) * narrow]) * scale
         out_ref[e] = both.astype(jnp.bfloat16).astype(jnp.float32)
 
 

time: 36.2 us -> 36.2 us (level)
  transfers between devices with their start and end apart: 12 -> 12, of which waited for: 4 -> 4; matrix products, arithmetic and copies ran while one was open for 0% -> 0% of each run, Pallas kernels for 24% -> 23%
where the time goes in v9:
time: 36.2 us; the launch traced here: 35.8 us
  starting transfers between devices  16.7 us (46%)
  waiting for transfers between devices  9.52 us (26%)
  Pallas kernels  9.33 us (26%)
    ppermute x12, starting transfers between devices, exchange(): return lax.ppermute(x, 'ex', [(i, i ^ bit) for i in range(devices)])  16.7 us
    ppermute x12, waiting for transfers between devices, exchange(): return lax.ppermute(x, 'ex', [(i, i ^ bit) for i in range(devices)])  9.52 us
    pallas_call x1, Pallas kernels, project(): pl.pallas_call(project_kernel, out_shape=[pltpu.VMEM((narrow + narrow //...  5.92 us
    pallas_call x1, Pallas kernels, precondition(): pl.pallas_call(functools.partial(precond_kernel, float(tokens)), out_shap...  2.35 us
    pallas_call x1, Pallas kernels, score(): pl.pallas_call(functools.partial(score_kernel, sources, scale), out_shape...  1.04 us
  transfers between devices with their start and end apart: 12, of which 4 were waited for; matrix products, arithmetic and copies ran while one was open for 0% of the time, Pallas kernels for 23%

profile of v9, /device:TPU:1, one launch (start us, length us, event | category | flops | bytes accessed | tf_op | source)
XLA Modules:
  0.0 35.8 jit_solution(12165394664690564330)
XLA Ops:
  0.0 0.0 copy-start
  0.0 3.1 %collective-permute-start = (bf16[4,8192]{1,0:T(4,128)(2,1)}, bf16[4,8192]{1,0:T(4,128)(2,1)S(1)}, u32[]{:S(2)}, u32[]{:S(2)}) collective-permute-start(bf16[4,8192]{1,0:T(4,128)(2,1)} %param.9), channel_id=1, source_target_pairs={{0,16},{1,17},{2,18},{3,19},{4,20},{5,21},{6,22},{7,23},{8,24},{9,... | collective-permute-start | bytes 196616 | tf_op jit(solution)/shard_map/ppermute | solution.py:254
  3.1 5.9 %project.1 = (f32[96,128]{1,0:T(8,128)S(1)}, f32[1,64,128]{2,1,0:T(8,128)S(1)}) custom-call(bf16[1,1024,4096]{2,1,0:T(8,128)(2,1)} %x_hbm.1, bf16[1,1024,1024]{2,1,0:T(8,128)(2,1)} %g_hbm.1, bf16[128,4096]{1,0:T(8,128)(2,1)} %pin_hbm.1, bf16[64,1024]{1,0:T(8,128)(2,1)} %pout_hbm.1), custom_call_target="tpu_custom_call" | custom-call | tf_op jit(solution)/shard_map/project/pallas_call | solution.py:111
  9.1 0.0 collective-permute-done
  9.1 0.0 copy-done
  9.1 0.1 pad_maximum_fusion.1
  9.2 1.4 %collective-permute-start.3 = (bf16[8,8192]{1,0:T(8,128)(2,1)S(1)}, bf16[8,8192]{1,0:T(8,128)(2,1)S(1)}, u32[]{:S(2)}, u32[]{:S(2)}) collective-permute-start(bf16[8,8192]{1,0:T(8,128)(2,1)S(1)} %pad_maximum_fusion.1), channel_id=1, source_target_pairs={{0,8},{1,9},{2,10},{3,11},{4,12},{5,13},{6,14},{7,15},{8,0},{9,1},... | collective-permute-start | bytes 393224 | tf_op jit(solution)/shard_map/ppermute | solution.py:254
  10.5 1.2 %collective-permute-start.1 = (f32[96,128]{1,0:T(8,128)S(1)}, f32[96,128]{1,0:T(8,128)S(1)}, u32[]{:S(2)}, u32[]{:S(2)}) collective-permute-start(f32[96,128]{1,0:T(8,128)S(1)} %get-tuple-element.22), channel_id=1, source_target_pairs={{0,1},{1,0},{2,3},{3,2},{4,5},{5,4},{6,7},{7,6},{8,9},{9,8},{10,11... | collective-permute-start | bytes 147464 | tf_op jit(solution)/shard_map/ppermute | solution.py:254
  11.8 0.9 %collective-permute-done.1 = f32[96,128]{1,0:T(8,128)S(1)} collective-permute-done((f32[96,128]{1,0:T(8,128)S(1)}, f32[96,128]{1,0:T(8,128)S(1)}, u32[]{:S(2)}, u32[]{:S(2)}) %collective-permute-start.1) | collective-permute-done | bytes 49184 | tf_op jit(solution)/shard_map/ppermute | solution.py:254
  12.6 1.2 %collective-permute-start.2 = (f32[96,128]{1,0:T(8,128)S(1)}, f32[96,128]{1,0:T(8,128)S(1)}, u32[]{:S(2)}, u32[]{:S(2)}) collective-permute-start(f32[96,128]{1,0:T(8,128)S(1)} %add.11), channel_id=1, source_target_pairs={{0,2},{1,3},{2,0},{3,1},{4,6},{5,7},{6,4},{7,5},{8,10},{9,11},{10,... | collective-permute-start | bytes 147464 | tf_op jit(solution)/shard_map/ppermute | solution.py:254
  13.9 1.7 %collective-permute-done.2 = f32[96,128]{1,0:T(8,128)S(1)} collective-permute-done((f32[96,128]{1,0:T(8,128)S(1)}, f32[96,128]{1,0:T(8,128)S(1)}, u32[]{:S(2)}, u32[]{:S(2)}) %collective-permute-start.2) | collective-permute-done | bytes 49184 | tf_op jit(solution)/shard_map/ppermute | solution.py:254
  15.6 0.0 collective-permute-done.3
  15.6 0.5 %collective-permute-start.4 = (f32[96,128]{1,0:T(8,128)S(1)}, f32[96,128]{1,0:T(8,128)S(1)}, u32[]{:S(2)}, u32[]{:S(2)}) collective-permute-start(f32[96,128]{1,0:T(8,128)S(1)} %add.12.a_ref), channel_id=1, source_target_pairs={{0,8},{1,9},{2,10},{3,11},{4,12},{5,13},{6,14},{7,15},{8,0},{9,1},... | collective-permute-start | bytes 147464 | tf_op jit(solution)/shard_map/ppermute | solution.py:254
  16.2 1.2 %collective-permute-start.9 = (bf16[16,8192]{1,0:T(8,128)(2,1)S(1)}, bf16[16,8192]{1,0:T(8,128)(2,1)S(1)}, u32[]{:S(2)}, u32[]{:S(2)}) collective-permute-start(bf16[16,8192]{1,0:T(8,128)(2,1)S(1)} %pad_maximum_fusion), channel_id=1, source_target_pairs={{0,2},{1,3},{2,0},{3,1},{4,6},{5,7},{6,4},{7,5},{8,10},{9,11},{10,... | collective-permute-start | bytes 786440 | tf_op jit(solution)/shard_map/ppermute | solution.py:254
  17.4 1.2 %collective-permute-start.7 = (bf16[16,8192]{1,0:T(8,128)(2,1)S(1)}, bf16[16,8192]{1,0:T(8,128)(2,1)S(1)}, u32[]{:S(2)}, u32[]{:S(2)}) collective-permute-start(bf16[16,8192]{1,0:T(8,128)(2,1)S(1)} %pad_maximum_fusion), channel_id=1, source_target_pairs={{0,4},{1,5},{2,6},{3,7},{4,0},{5,1},{6,2},{7,3},{8,12},{9,13},{10,... | collective-permute-start | bytes 786440 | tf_op jit(solution)/shard_map/ppermute | solution.py:254
  18.6 0.0 collective-permute-done.4.b_ref
  18.6 0.1 collective-permute-start.5
  18.8 3.7 %collective-permute-done.9 = bf16[16,8192]{1,0:T(8,128)(2,1)S(1)} collective-permute-done((bf16[16,8192]{1,0:T(8,128)(2,1)S(1)}, bf16[16,8192]{1,0:T(8,128)(2,1)S(1)}, u32[]{:S(2)}, u32[]{:S(2)}) %collective-permute-start.9) | collective-permute-done | bytes 262176 | tf_op jit(solution)/shard_map/ppermute | solution.py:254
  22.4 1.3 %collective-permute-start.10 = (bf16[8,8192]{1,0:T(8,128)(2,1)S(1)}, bf16[8,8192]{1,0:T(8,128)(2,1)S(1)}, u32[]{:S(2)}, u32[]{:S(2)}) collective-permute-start(bf16[8,8192]{1,0:T(8,128)(2,1)S(1)} %slice.9), channel_id=1, source_target_pairs={{0,4},{1,5},{2,6},{3,7},{4,0},{5,1},{6,2},{7,3},{8,12},{9,13},{10,... | collective-permute-start | bytes 393224 | tf_op jit(solution)/shard_map/ppermute | solution.py:254
  23.7 0.0 collective-permute-done.7
  23.7 1.3 %collective-permute-start.8 = (bf16[8,8192]{1,0:T(8,128)(2,1)S(1)}, bf16[8,8192]{1,0:T(8,128)(2,1)S(1)}, u32[]{:S(2)}, u32[]{:S(2)}) collective-permute-start(bf16[8,8192]{1,0:T(8,128)(2,1)S(1)} %slice.8), channel_id=1, source_target_pairs={{0,2},{1,3},{2,0},{3,1},{4,6},{5,7},{6,4},{7,5},{8,10},{9,11},{10,... | collective-permute-start | bytes 393224 | tf_op jit(solution)/shard_map/ppermute | solution.py:254
  25.0 0.0 collective-permute-done.5.b_ref
  25.0 0.3 collective-permute-start.6
  25.3 3.2 %collective-permute-done.6 = f32[96,128]{1,0:T(8,128)S(1)} collective-permute-done((f32[96,128]{1,0:T(8,128)S(1)}, f32[96,128]{1,0:T(8,128)S(1)}, u32[]{:S(2)}, u32[]{:S(2)}) %collective-permute-start.6) | collective-permute-done | bytes 49184 | tf_op jit(solution)/shard_map/ppermute | solution.py:254
  28.5 0.0 collective-permute-done.10
  28.6 0.0 collective-permute-done.8
  28.7 3.7 %collective-permute-start.11 = (bf16[64,8192]{1,0:T(8,128)(2,1)S(1)}, bf16[64,8192]{1,0:T(8,128)(2,1)S(1)}, u32[]{:S(2)}, u32[]{:S(2)}) collective-permute-start(bf16[64,8192]{1,0:T(8,128)(2,1)S(1)} %constant_dynamic-update-slice_fusion.refs_0_), channel_id=1, source_target_pairs={{0,1},{1,0},{2,3},{3,2},{4,5},{5,4},{6,7},{7,6},{8,9},{9,8},{10,11... | collective-permute-start | bytes 3145736 | tf_op jit(solution)/shard_map/ppermute | solution.py:254
  32.4 2.4 %precondition.1.p_ref = f32[1,64,128]{2,1,0:T(8,128)S(1)} custom-call(f32[96,128]{1,0:T(8,128)S(1)} %add.13.packed_ref, f32[1,64,128]{2,1,0:T(8,128)S(1)} %get-tuple-element.27.grads_ref), custom_call_target="tpu_custom_call" | custom-call | tf_op jit(solution)/shard_map/precondition/pallas_call | solution.py:206
  34.8 0.0 collective-permute-done.11.refs_1_
  34.8 1.0 %score.1 = f32[1,128]{1,0:T(1,128)} custom-call(s32[1]{0:T(128)} %bitcast.me_ref, f32[1,64,128]{2,1,0:T(8,128)S(1)} %precondition.1.p_ref, bf16[64,8192]{1,0:T(8,128)(2,1)S(1)} %constant_dynamic-update-slice_fusion.refs_0_, bf16[64,8192]{1,0:T(8,128)(2,1)S(1)} %collective-permute-done.11.refs_1_), custom_call_target="tpu_custom_call" | custom-call | tf_op jit(solution)/shard_map/score/pallas_call | solution.py:243
  (13 shorter events, 0.2 us)
Async XLA Ops:
  0.0 9.1 %copy-start = (bf16[4,8192]{1,0:T(4,128)(2,1)S(1)}, bf16[4,8192]{1,0:T(4,128)(2,1)}, u32[]{:S(2)}) copy-start(bf16[4,8192]{1,0:T(4,128)(2,1)} %param.9) | copy-start | bytes 196612
  0.0 9.1 %collective-permute-start = (bf16[4,8192]{1,0:T(4,128)(2,1)}, bf16[4,8192]{1,0:T(4,128)(2,1)S(1)}, u32[]{:S(2)}, u32[]{:S(2)}) collective-permute-start(bf16[4,8192]{1,0:T(4,128)(2,1)} %param.9), channel_id=1, source_target_pairs={{0,16},{1,17},{2,18},{3,19},{4,20},{5,21},{6,22},{7,23},{8,24},{9,... | collective-permute-start | bytes 196616 | tf_op jit(solution)/shard_map/ppermute | solution.py:254
  9.2 6.4 %collective-permute-start.3 = (bf16[8,8192]{1,0:T(8,128)(2,1)S(1)}, bf16[8,8192]{1,0:T(8,128)(2,1)S(1)}, u32[]{:S(2)}, u32[]{:S(2)}) collective-permute-start(bf16[8,8192]{1,0:T(8,128)(2,1)S(1)} %pad_maximum_fusion.1), channel_id=1, source_target_pairs={{0,8},{1,9},{2,10},{3,11},{4,12},{5,13},{6,14},{7,15},{8,0},{9,1},... | collective-permute-start | bytes 393224 | tf_op jit(solution)/shard_map/ppermute | solution.py:254
  10.5 2.1 %collective-permute-start.1 = (f32[96,128]{1,0:T(8,128)S(1)}, f32[96,128]{1,0:T(8,128)S(1)}, u32[]{:S(2)}, u32[]{:S(2)}) collective-permute-start(f32[96,128]{1,0:T(8,128)S(1)} %get-tuple-element.22), channel_id=1, source_target_pairs={{0,1},{1,0},{2,3},{3,2},{4,5},{5,4},{6,7},{7,6},{8,9},{9,8},{10,11... | collective-permute-start | bytes 147464 | tf_op jit(solution)/shard_map/ppermute | solution.py:254
  12.6 2.9 %collective-permute-start.2 = (f32[96,128]{1,0:T(8,128)S(1)}, f32[96,128]{1,0:T(8,128)S(1)}, u32[]{:S(2)}, u32[]{:S(2)}) collective-permute-start(f32[96,128]{1,0:T(8,128)S(1)} %add.11), channel_id=1, source_target_pairs={{0,2},{1,3},{2,0},{3,1},{4,6},{5,7},{6,4},{7,5},{8,10},{9,11},{10,... | collective-permute-start | bytes 147464 | tf_op jit(solution)/shard_map/ppermute | solution.py:254
  15.6 3.0 %collective-permute-start.4 = (f32[96,128]{1,0:T(8,128)S(1)}, f32[96,128]{1,0:T(8,128)S(1)}, u32[]{:S(2)}, u32[]{:S(2)}) collective-permute-start(f32[96,128]{1,0:T(8,128)S(1)} %add.12.a_ref), channel_id=1, source_target_pairs={{0,8},{1,9},{2,10},{3,11},{4,12},{5,13},{6,14},{7,15},{8,0},{9,1},... | collective-permute-start | bytes 147464 | tf_op jit(solution)/shard_map/ppermute | solution.py:254
  16.2 6.3 %collective-permute-start.9 = (bf16[16,8192]{1,0:T(8,128)(2,1)S(1)}, bf16[16,8192]{1,0:T(8,128)(2,1)S(1)}, u32[]{:S(2)}, u32[]{:S(2)}) collective-permute-start(bf16[16,8192]{1,0:T(8,128)(2,1)S(1)} %pad_maximum_fusion), channel_id=1, source_target_pairs={{0,2},{1,3},{2,0},{3,1},{4,6},{5,7},{6,4},{7,5},{8,10},{9,11},{10,... | collective-permute-start | bytes 786440 | tf_op jit(solution)/shard_map/ppermute | solution.py:254
  17.4 6.4 %collective-permute-start.7 = (bf16[16,8192]{1,0:T(8,128)(2,1)S(1)}, bf16[16,8192]{1,0:T(8,128)(2,1)S(1)}, u32[]{:S(2)}, u32[]{:S(2)}) collective-permute-start(bf16[16,8192]{1,0:T(8,128)(2,1)S(1)} %pad_maximum_fusion), channel_id=1, source_target_pairs={{0,4},{1,5},{2,6},{3,7},{4,0},{5,1},{6,2},{7,3},{8,12},{9,13},{10,... | collective-permute-start | bytes 786440 | tf_op jit(solution)/shard_map/ppermute | solution.py:254
  18.6 6.4 %collective-permute-start.5 = (f32[96,128]{1,0:T(8,128)S(1)}, f32[96,128]{1,0:T(8,128)S(1)}, u32[]{:S(2)}, u32[]{:S(2)}) collective-permute-start(f32[96,128]{1,0:T(8,128)S(1)} %add.14.a_ref), channel_id=1, source_target_pairs={{0,16},{1,17},{2,18},{3,19},{4,20},{5,21},{6,22},{7,23},{8,24},{9,... | collective-permute-start | bytes 147464 | tf_op jit(solution)/shard_map/ppermute | solution.py:254
  22.4 6.1 %collective-permute-start.10 = (bf16[8,8192]{1,0:T(8,128)(2,1)S(1)}, bf16[8,8192]{1,0:T(8,128)(2,1)S(1)}, u32[]{:S(2)}, u32[]{:S(2)}) collective-permute-start(bf16[8,8192]{1,0:T(8,128)(2,1)S(1)} %slice.9), channel_id=1, source_target_pairs={{0,4},{1,5},{2,6},{3,7},{4,0},{5,1},{6,2},{7,3},{8,12},{9,13},{10,... | collective-permute-start | bytes 393224 | tf_op jit(solution)/shard_map/ppermute | solution.py:254
  23.7 4.8 %collective-permute-start.8 = (bf16[8,8192]{1,0:T(8,128)(2,1)S(1)}, bf16[8,8192]{1,0:T(8,128)(2,1)S(1)}, u32[]{:S(2)}, u32[]{:S(2)}) collective-permute-start(bf16[8,8192]{1,0:T(8,128)(2,1)S(1)} %slice.8), channel_id=1, source_target_pairs={{0,2},{1,3},{2,0},{3,1},{4,6},{5,7},{6,4},{7,5},{8,10},{9,11},{10,... | collective-permute-start | bytes 393224 | tf_op jit(solution)/shard_map/ppermute | solution.py:254
  25.0 3.5 %collective-permute-start.6 = (f32[96,128]{1,0:T(8,128)S(1)}, f32[96,128]{1,0:T(8,128)S(1)}, u32[]{:S(2)}, u32[]{:S(2)}) collective-permute-start(f32[96,128]{1,0:T(8,128)S(1)} %add.15), channel_id=1, source_target_pairs={{0,4},{1,5},{2,6},{3,7},{4,0},{5,1},{6,2},{7,3},{8,12},{9,13},{10,... | collective-permute-start | bytes 147464 | tf_op jit(solution)/shard_map/ppermute | solution.py:254
  28.7 6.1 %collective-permute-start.11 = (bf16[64,8192]{1,0:T(8,128)(2,1)S(1)}, bf16[64,8192]{1,0:T(8,128)(2,1)S(1)}, u32[]{:S(2)}, u32[]{:S(2)}) collective-permute-start(bf16[64,8192]{1,0:T(8,128)(2,1)S(1)} %constant_dynamic-update-slice_fusion.refs_0_), channel_id=1, source_target_pairs={{0,1},{1,0},{2,3},{3,2},{4,5},{5,4},{6,7},{7,6},{8,9},{9,8},{10,11... | collective-permute-start | bytes 3145736 | tf_op jit(solution)/shard_map/ppermute | solution.py:254

commit v10 on v9

--- a/solution.py
+++ b/solution.py
@@ -150,7 +150,24 @@
     return (s / mean + jnp.where(eye, DAMP, 0.0)) * first, first / mean, eye
 
 
-def precond_kernel(tokens, packed_ref, grads_ref, out_ref):
+def score_rows(me, p_ref, e, tests, offsets, count):
+    _, narrow, wide = p_ref.shape
+    rows = tests.shape[0]
+    per = rows // len(offsets)
+    sums = jnp.zeros((rows, wide), jnp.float32)
+    for o in range(narrow):
+        sums = sums + tests[:, o * wide : (o + 1) * wide].astype(jnp.float32) * p_ref[e, o : o + 1, :]
+    row = lax.broadcasted_iota(jnp.int32, (rows, 1), 0)
+    target = jnp.zeros((rows, 1), jnp.int32)
+    for i, offset in enumerate(offsets):
+        inside = (row >= i * per) & (row < (i + 1) * per)
+        target = jnp.where(inside, (me ^ offset) * per + row - i * per, target)
+    lane = lax.broadcasted_iota(jnp.int32, (1, count), 1)
+    by_row = jnp.sum(sums, axis=1, keepdims=True)
+    return jnp.sum(jnp.where(target == lane, by_row, 0.0), axis=0, keepdims=True)
+
+
+def precond_kernel(tokens, offsets, me_ref, packed_ref, grads_ref, tests_ref, out_ref, part_ref):
     wide = packed_ref.shape[1]
     examples, narrow, _ = grads_ref.shape
     packed = packed_ref[...]
@@ -200,54 +217,38 @@
     for e in range(examples):
         both = near_exact(xo, w[e * narrow : (e + 1) * narrow]) * scale
         out_ref[e] = both.astype(jnp.bfloat16).astype(jnp.float32)
-
-
-def precondition(packed, grads, tokens):
+        part_ref[e : e + 1, :] = score_rows(me_ref[0], out_ref, e, tests_ref, offsets, part_ref.shape[1])
+
+
+def precondition(me, packed, grads, tests, offsets, tokens, count):
     return pl.pallas_call(
-        functools.partial(precond_kernel, float(tokens)),
-        out_shape=pltpu.VMEM(grads.shape, jnp.float32),
-        in_specs=[pl.BlockSpec(memory_space=VMEM)] * 2,
-        out_specs=pl.BlockSpec(memory_space=VMEM),
+        functools.partial(precond_kernel, float(tokens), offsets),
+        out_shape=[pltpu.VMEM(grads.shape, jnp.float32), pltpu.VMEM((grads.shape[0], count), jnp.float32)],
+        in_specs=[pl.BlockSpec(memory_space=SMEM)] + [pl.BlockSpec(memory_space=VMEM)] * 3,
+        out_specs=[pl.BlockSpec(memory_space=VMEM)] * 2,
+        compiler_params=pltpu.CompilerParams(vmem_limit_bytes=32 * 2**20),
         name="precondition",
-    )(*[pltpu.with_memory_space_constraint(a, VMEM) for a in (packed, grads)])
-
-
-def score_kernel(sources, scale, me_ref, p_ref, *refs):
+    )(me, *[pltpu.with_memory_space_constraint(a, VMEM) for a in (packed, grads, tests)])
+
+
+def score_kernel(sources, scale, me_ref, p_ref, part_ref, *refs):
     pieces, out_ref = refs[:-1], refs[-1]
-    examples, narrow, wide = p_ref.shape
-    tests = out_ref.shape[1]
-    me = me_ref[0]
-    lane = lax.broadcasted_iota(jnp.int32, (1, tests), 1)
-    for e in range(examples):
-        sums = [jnp.zeros((t.shape[0], wide), jnp.float32) for t in pieces]
-        for o in range(narrow):
-            p = p_ref[e, o : o + 1, :]
-            here = slice(o * wide, (o + 1) * wide)
-            sums = [s + t[:, here].astype(jnp.float32) * p for s, t in zip(sums, pieces)]
-        total = jnp.zeros((1, tests), jnp.float32)
-        for s, offsets in zip(sums, sources):
-            rows = s.shape[0]
-            per = rows // len(offsets)
-            row = lax.broadcasted_iota(jnp.int32, (rows, 1), 0)
-            target = jnp.zeros((rows, 1), jnp.int32)
-            for i, offset in enumerate(offsets):
-                inside = (row >= i * per) & (row < (i + 1) * per)
-                target = jnp.where(inside, (me ^ offset) * per + row - i * per, target)
-            by_row = jnp.sum(s, axis=1, keepdims=True)
-            total += jnp.sum(jnp.where(target == lane, by_row, 0.0), axis=0, keepdims=True)
-        out_ref[pl.ds(e, 1), :] = total * scale
-
-
-def score(me, precond, pieces, sources, scale):
-    tests = sum(t.shape[0] for t in pieces)
+    for e in range(p_ref.shape[0]):
+        total = part_ref[e : e + 1, :]
+        for t, offsets in zip(pieces, sources):
+            total = total + score_rows(me_ref[0], p_ref, e, t, offsets, out_ref.shape[1])
+        out_ref[e : e + 1, :] = total * scale
+
+
+def score(me, precond, part, pieces, sources, scale):
     return pl.pallas_call(
         functools.partial(score_kernel, sources, scale),
-        out_shape=jax.ShapeDtypeStruct((precond.shape[0], tests), jnp.float32),
-        in_specs=[pl.BlockSpec(memory_space=SMEM)] + [pl.BlockSpec(memory_space=VMEM)] * (1 + len(pieces)),
+        out_shape=jax.ShapeDtypeStruct(part.shape, jnp.float32),
+        in_specs=[pl.BlockSpec(memory_space=SMEM)] + [pl.BlockSpec(memory_space=VMEM)] * (2 + len(pieces)),
         out_specs=pl.BlockSpec(memory_space=VMEM),
         compiler_params=pltpu.CompilerParams(vmem_limit_bytes=32 * 2**20),
         name="score",
-    )(me, *[pltpu.with_memory_space_constraint(a, VMEM) for a in (precond, *pieces)])
+    )(me, *[pltpu.with_memory_space_constraint(a, VMEM) for a in (precond, part, *pieces)])
 
 
 def exchange(x, bit, devices):
@@ -319,9 +320,12 @@
         packed, far = lax.optimization_barrier((packed, far))
         tests = jnp.concatenate([test_grads, far], axis=0)
         packed, pieces, sources = exchange_all(packed, tests, [0, devices // 2], devices)
-    precond = precondition(packed, grads, examples * tokens * devices)
+    count = test_grads.shape[0] * devices
+    precond, part = precondition(
+        me[None], packed, grads, pieces[0], sources[0], examples * tokens * devices, count
+    )
     scale = 4.0 / (wide * narrow * tokens) ** 0.5
-    return score(me[None], precond, pieces, sources, scale)
+    return score(me[None], precond, part, pieces[1:], sources[1:], scale)
 
 
 def solution(mesh):

time: 36.2 us -> 36.1 us (level)
  transfers between devices with their start and end apart: 12 -> 12, of which waited for: 4 -> 4; matrix products, arithmetic and copies ran while one was open for 0% -> 0% of each run, Pallas kernels for 23% -> 24%
where the time goes in v10:
time: 36.1 us; the launch traced here: 36 us
  starting transfers between devices  16.7 us (46%)
  waiting for transfers between devices  9.52 us (26%)
  Pallas kernels  9.46 us (26%)
    ppermute x12, starting transfers between devices, exchange(): return lax.ppermute(x, 'ex', [(i, i ^ bit) for i in range(devices)])  16.7 us
    ppermute x12, waiting for transfers between devices, exchange(): return lax.ppermute(x, 'ex', [(i, i ^ bit) for i in range(devices)])  9.52 us
    pallas_call x1, Pallas kernels, project(): pl.pallas_call(project_kernel, out_shape=[pltpu.VMEM((narrow + narrow //...  5.92 us
    pallas_call x1, Pallas kernels, precondition(): pl.pallas_call(functools.partial(precond_kernel, float(tokens), offsets),...  2.67 us
    pallas_call x1, Pallas kernels, score(): pl.pallas_call(functools.partial(score_kernel, sources, scale), out_shape...  0.85 us
  transfers between devices with their start and end apart: 12, of which 4 were waited for; matrix products, arithmetic and copies ran while one was open for 0% of the time, Pallas kernels for 24%

profile of v10, /device:TPU:1, one launch (start us, length us, event | category | flops | bytes accessed | tf_op | source)
XLA Modules:
  0.0 36.0 jit_solution(5110683329435565527)
XLA Ops:
  0.0 0.0 copy-start
  0.0 3.1 %collective-permute-start = (bf16[4,8192]{1,0:T(4,128)(2,1)}, bf16[4,8192]{1,0:T(4,128)(2,1)S(1)}, u32[]{:S(2)}, u32[]{:S(2)}) collective-permute-start(bf16[4,8192]{1,0:T(4,128)(2,1)} %param.9), channel_id=1, source_target_pairs={{0,16},{1,17},{2,18},{3,19},{4,20},{5,21},{6,22},{7,23},{8,24},{9,... | collective-permute-start | bytes 196616 | tf_op jit(solution)/shard_map/ppermute | solution.py:255
  3.1 5.9 %project.1 = (f32[96,128]{1,0:T(8,128)S(1)}, f32[1,64,128]{2,1,0:T(8,128)S(1)}) custom-call(bf16[1,1024,4096]{2,1,0:T(8,128)(2,1)} %x_hbm.1, bf16[1,1024,1024]{2,1,0:T(8,128)(2,1)} %g_hbm.1, bf16[128,4096]{1,0:T(8,128)(2,1)} %pin_hbm.1, bf16[64,1024]{1,0:T(8,128)(2,1)} %pout_hbm.1), custom_call_target="tpu_custom_call" | custom-call | tf_op jit(solution)/shard_map/project/pallas_call | solution.py:111
  9.1 0.0 collective-permute-done
  9.1 0.0 copy-done
  9.1 0.1 pad_maximum_fusion.1
  9.2 1.4 %collective-permute-start.3 = (bf16[8,8192]{1,0:T(8,128)(2,1)S(1)}, bf16[8,8192]{1,0:T(8,128)(2,1)S(1)}, u32[]{:S(2)}, u32[]{:S(2)}) collective-permute-start(bf16[8,8192]{1,0:T(8,128)(2,1)S(1)} %pad_maximum_fusion.1), channel_id=1, source_target_pairs={{0,8},{1,9},{2,10},{3,11},{4,12},{5,13},{6,14},{7,15},{8,0},{9,1},... | collective-permute-start | bytes 393224 | tf_op jit(solution)/shard_map/ppermute | solution.py:255
  10.5 1.2 %collective-permute-start.1 = (f32[96,128]{1,0:T(8,128)S(1)}, f32[96,128]{1,0:T(8,128)S(1)}, u32[]{:S(2)}, u32[]{:S(2)}) collective-permute-start(f32[96,128]{1,0:T(8,128)S(1)} %get-tuple-element.24), channel_id=1, source_target_pairs={{0,1},{1,0},{2,3},{3,2},{4,5},{5,4},{6,7},{7,6},{8,9},{9,8},{10,11... | collective-permute-start | bytes 147464 | tf_op jit(solution)/shard_map/ppermute | solution.py:255
  11.8 0.9 %collective-permute-done.1 = f32[96,128]{1,0:T(8,128)S(1)} collective-permute-done((f32[96,128]{1,0:T(8,128)S(1)}, f32[96,128]{1,0:T(8,128)S(1)}, u32[]{:S(2)}, u32[]{:S(2)}) %collective-permute-start.1) | collective-permute-done | bytes 49184 | tf_op jit(solution)/shard_map/ppermute | solution.py:255
  12.6 1.2 %collective-permute-start.2 = (f32[96,128]{1,0:T(8,128)S(1)}, f32[96,128]{1,0:T(8,128)S(1)}, u32[]{:S(2)}, u32[]{:S(2)}) collective-permute-start(f32[96,128]{1,0:T(8,128)S(1)} %add.11), channel_id=1, source_target_pairs={{0,2},{1,3},{2,0},{3,1},{4,6},{5,7},{6,4},{7,5},{8,10},{9,11},{10,... | collective-permute-start | bytes 147464 | tf_op jit(solution)/shard_map/ppermute | solution.py:255
  13.9 1.7 %collective-permute-done.2 = f32[96,128]{1,0:T(8,128)S(1)} collective-permute-done((f32[96,128]{1,0:T(8,128)S(1)}, f32[96,128]{1,0:T(8,128)S(1)}, u32[]{:S(2)}, u32[]{:S(2)}) %collective-permute-start.2) | collective-permute-done | bytes 49184 | tf_op jit(solution)/shard_map/ppermute | solution.py:255
  15.6 0.0 collective-permute-done.3
  15.6 0.5 %collective-permute-start.4 = (f32[96,128]{1,0:T(8,128)S(1)}, f32[96,128]{1,0:T(8,128)S(1)}, u32[]{:S(2)}, u32[]{:S(2)}) collective-permute-start(f32[96,128]{1,0:T(8,128)S(1)} %add.12.a_ref), channel_id=1, source_target_pairs={{0,8},{1,9},{2,10},{3,11},{4,12},{5,13},{6,14},{7,15},{8,0},{9,1},... | collective-permute-start | bytes 147464 | tf_op jit(solution)/shard_map/ppermute | solution.py:255
  16.2 1.2 %collective-permute-start.9 = (bf16[16,8192]{1,0:T(8,128)(2,1)S(1)}, bf16[16,8192]{1,0:T(8,128)(2,1)S(1)}, u32[]{:S(2)}, u32[]{:S(2)}) collective-permute-start(bf16[16,8192]{1,0:T(8,128)(2,1)S(1)} %pad_maximum_fusion), channel_id=1, source_target_pairs={{0,2},{1,3},{2,0},{3,1},{4,6},{5,7},{6,4},{7,5},{8,10},{9,11},{10,... | collective-permute-start | bytes 786440 | tf_op jit(solution)/shard_map/ppermute | solution.py:255
  17.4 1.2 %collective-permute-start.7 = (bf16[16,8192]{1,0:T(8,128)(2,1)S(1)}, bf16[16,8192]{1,0:T(8,128)(2,1)S(1)}, u32[]{:S(2)}, u32[]{:S(2)}) collective-permute-start(bf16[16,8192]{1,0:T(8,128)(2,1)S(1)} %pad_maximum_fusion), channel_id=1, source_target_pairs={{0,4},{1,5},{2,6},{3,7},{4,0},{5,1},{6,2},{7,3},{8,12},{9,13},{10,... | collective-permute-start | bytes 786440 | tf_op jit(solution)/shard_map/ppermute | solution.py:255
  18.6 0.0 collective-permute-done.4.b_ref
  18.6 0.1 collective-permute-start.5
  18.8 3.7 %collective-permute-done.9 = bf16[16,8192]{1,0:T(8,128)(2,1)S(1)} collective-permute-done((bf16[16,8192]{1,0:T(8,128)(2,1)S(1)}, bf16[16,8192]{1,0:T(8,128)(2,1)S(1)}, u32[]{:S(2)}, u32[]{:S(2)}) %collective-permute-start.9) | collective-permute-done | bytes 262176 | tf_op jit(solution)/shard_map/ppermute | solution.py:255
  22.4 1.3 %collective-permute-start.10 = (bf16[8,8192]{1,0:T(8,128)(2,1)S(1)}, bf16[8,8192]{1,0:T(8,128)(2,1)S(1)}, u32[]{:S(2)}, u32[]{:S(2)}) collective-permute-start(bf16[8,8192]{1,0:T(8,128)(2,1)S(1)} %slice.9), channel_id=1, source_target_pairs={{0,4},{1,5},{2,6},{3,7},{4,0},{5,1},{6,2},{7,3},{8,12},{9,13},{10,... | collective-permute-start | bytes 393224 | tf_op jit(solution)/shard_map/ppermute | solution.py:255
  23.7 0.0 collective-permute-done.7
  23.7 1.3 %collective-permute-start.8 = (bf16[8,8192]{1,0:T(8,128)(2,1)S(1)}, bf16[8,8192]{1,0:T(8,128)(2,1)S(1)}, u32[]{:S(2)}, u32[]{:S(2)}) collective-permute-start(bf16[8,8192]{1,0:T(8,128)(2,1)S(1)} %slice.8), channel_id=1, source_target_pairs={{0,2},{1,3},{2,0},{3,1},{4,6},{5,7},{6,4},{7,5},{8,10},{9,11},{10,... | collective-permute-start | bytes 393224 | tf_op jit(solution)/shard_map/ppermute | solution.py:255
  25.0 0.0 collective-permute-done.5.b_ref
  25.0 0.3 collective-permute-start.6
  25.3 3.2 %collective-permute-done.6 = f32[96,128]{1,0:T(8,128)S(1)} collective-permute-done((f32[96,128]{1,0:T(8,128)S(1)}, f32[96,128]{1,0:T(8,128)S(1)}, u32[]{:S(2)}, u32[]{:S(2)}) %collective-permute-start.6) | collective-permute-done | bytes 49184 | tf_op jit(solution)/shard_map/ppermute | solution.py:255
  28.5 0.0 collective-permute-done.10
  28.6 0.0 collective-permute-done.8
  28.7 3.7 %collective-permute-start.11 = (bf16[64,8192]{1,0:T(8,128)(2,1)S(1)}, bf16[64,8192]{1,0:T(8,128)(2,1)S(1)}, u32[]{:S(2)}, u32[]{:S(2)}) collective-permute-start(bf16[64,8192]{1,0:T(8,128)(2,1)S(1)} %constant_dynamic-update-slice_fusion.tests_ref), channel_id=1, source_target_pairs={{0,1},{1,0},{2,3},{3,2},{4,5},{5,4},{6,7},{7,6},{8,9},{9,8},{10,11... | collective-permute-start | bytes 3145736 | tf_op jit(solution)/shard_map/ppermute | solution.py:255
  32.4 2.7 %precondition.1 = (f32[1,64,128]{2,1,0:T(8,128)S(1)}, f32[1,128]{1,0:T(1,128)S(1)}) custom-call(s32[1]{0:T(128)} %bitcast.me_ref, f32[96,128]{1,0:T(8,128)S(1)} %add.13.packed_ref, f32[1,64,128]{2,1,0:T(8,128)S(1)} %get-tuple-element.29.grads_ref, bf16[64,8192]{1,0:T(8,128)(2,1)S(1)} %constant_dynamic-update-slice_fusion.tests_ref), custom_call_target="tpu_custom_call" | custom-call | tf_op jit(solution)/shard_map/precondition/pallas_call | solution.py:224
  35.1 0.0 collective-permute-done.11.refs_0_
  35.1 0.9 %score.1 = f32[1,128]{1,0:T(1,128)} custom-call(s32[1]{0:T(128)} %bitcast.me_ref, f32[1,64,128]{2,1,0:T(8,128)S(1)} %get-tuple-element.35.p_ref, f32[1,128]{1,0:T(1,128)S(1)} %get-tuple-element.36.part_ref, bf16[64,8192]{1,0:T(8,128)(2,1)S(1)} %collective-permute-done.11.refs_0_), custom_call_target="tpu_custom_call" | custom-call | tf_op jit(solution)/shard_map/score/pallas_call | solution.py:244
  (13 shorter events, 0.2 us)
Async XLA Ops:
  0.0 9.1 %copy-start = (bf16[4,8192]{1,0:T(4,128)(2,1)S(1)}, bf16[4,8192]{1,0:T(4,128)(2,1)}, u32[]{:S(2)}) copy-start(bf16[4,8192]{1,0:T(4,128)(2,1)} %param.9) | copy-start | bytes 196612
  0.0 9.1 %collective-permute-start = (bf16[4,8192]{1,0:T(4,128)(2,1)}, bf16[4,8192]{1,0:T(4,128)(2,1)S(1)}, u32[]{:S(2)}, u32[]{:S(2)}) collective-permute-start(bf16[4,8192]{1,0:T(4,128)(2,1)} %param.9), channel_id=1, source_target_pairs={{0,16},{1,17},{2,18},{3,19},{4,20},{5,21},{6,22},{7,23},{8,24},{9,... | collective-permute-start | bytes 196616 | tf_op jit(solution)/shard_map/ppermute | solution.py:255
  9.2 6.4 %collective-permute-start.3 = (bf16[8,8192]{1,0:T(8,128)(2,1)S(1)}, bf16[8,8192]{1,0:T(8,128)(2,1)S(1)}, u32[]{:S(2)}, u32[]{:S(2)}) collective-permute-start(bf16[8,8192]{1,0:T(8,128)(2,1)S(1)} %pad_maximum_fusion.1), channel_id=1, source_target_pairs={{0,8},{1,9},{2,10},{3,11},{4,12},{5,13},{6,14},{7,15},{8,0},{9,1},... | collective-permute-start | bytes 393224 | tf_op jit(solution)/shard_map/ppermute | solution.py:255
  10.5 2.1 %collective-permute-start.1 = (f32[96,128]{1,0:T(8,128)S(1)}, f32[96,128]{1,0:T(8,128)S(1)}, u32[]{:S(2)}, u32[]{:S(2)}) collective-permute-start(f32[96,128]{1,0:T(8,128)S(1)} %get-tuple-element.24), channel_id=1, source_target_pairs={{0,1},{1,0},{2,3},{3,2},{4,5},{5,4},{6,7},{7,6},{8,9},{9,8},{10,11... | collective-permute-start | bytes 147464 | tf_op jit(solution)/shard_map/ppermute | solution.py:255
  12.6 2.9 %collective-permute-start.2 = (f32[96,128]{1,0:T(8,128)S(1)}, f32[96,128]{1,0:T(8,128)S(1)}, u32[]{:S(2)}, u32[]{:S(2)}) collective-permute-start(f32[96,128]{1,0:T(8,128)S(1)} %add.11), channel_id=1, source_target_pairs={{0,2},{1,3},{2,0},{3,1},{4,6},{5,7},{6,4},{7,5},{8,10},{9,11},{10,... | collective-permute-start | bytes 147464 | tf_op jit(solution)/shard_map/ppermute | solution.py:255
  15.6 3.0 %collective-permute-start.4 = (f32[96,128]{1,0:T(8,128)S(1)}, f32[96,128]{1,0:T(8,128)S(1)}, u32[]{:S(2)}, u32[]{:S(2)}) collective-permute-start(f32[96,128]{1,0:T(8,128)S(1)} %add.12.a_ref), channel_id=1, source_target_pairs={{0,8},{1,9},{2,10},{3,11},{4,12},{5,13},{6,14},{7,15},{8,0},{9,1},... | collective-permute-start | bytes 147464 | tf_op jit(solution)/shard_map/ppermute | solution.py:255
  16.2 6.3 %collective-permute-start.9 = (bf16[16,8192]{1,0:T(8,128)(2,1)S(1)}, bf16[16,8192]{1,0:T(8,128)(2,1)S(1)}, u32[]{:S(2)}, u32[]{:S(2)}) collective-permute-start(bf16[16,8192]{1,0:T(8,128)(2,1)S(1)} %pad_maximum_fusion), channel_id=1, source_target_pairs={{0,2},{1,3},{2,0},{3,1},{4,6},{5,7},{6,4},{7,5},{8,10},{9,11},{10,... | collective-permute-start | bytes 786440 | tf_op jit(solution)/shard_map/ppermute | solution.py:255
  17.4 6.4 %collective-permute-start.7 = (bf16[16,8192]{1,0:T(8,128)(2,1)S(1)}, bf16[16,8192]{1,0:T(8,128)(2,1)S(1)}, u32[]{:S(2)}, u32[]{:S(2)}) collective-permute-start(bf16[16,8192]{1,0:T(8,128)(2,1)S(1)} %pad_maximum_fusion), channel_id=1, source_target_pairs={{0,4},{1,5},{2,6},{3,7},{4,0},{5,1},{6,2},{7,3},{8,12},{9,13},{10,... | collective-permute-start | bytes 786440 | tf_op jit(solution)/shard_map/ppermute | solution.py:255
  18.6 6.4 %collective-permute-start.5 = (f32[96,128]{1,0:T(8,128)S(1)}, f32[96,128]{1,0:T(8,128)S(1)}, u32[]{:S(2)}, u32[]{:S(2)}) collective-permute-start(f32[96,128]{1,0:T(8,128)S(1)} %add.14.a_ref), channel_id=1, source_target_pairs={{0,16},{1,17},{2,18},{3,19},{4,20},{5,21},{6,22},{7,23},{8,24},{9,... | collective-permute-start | bytes 147464 | tf_op jit(solution)/shard_map/ppermute | solution.py:255
  22.4 6.1 %collective-permute-start.10 = (bf16[8,8192]{1,0:T(8,128)(2,1)S(1)}, bf16[8,8192]{1,0:T(8,128)(2,1)S(1)}, u32[]{:S(2)}, u32[]{:S(2)}) collective-permute-start(bf16[8,8192]{1,0:T(8,128)(2,1)S(1)} %slice.9), channel_id=1, source_target_pairs={{0,4},{1,5},{2,6},{3,7},{4,0},{5,1},{6,2},{7,3},{8,12},{9,13},{10,... | collective-permute-start | bytes 393224 | tf_op jit(solution)/shard_map/ppermute | solution.py:255
  23.7 4.8 %collective-permute-start.8 = (bf16[8,8192]{1,0:T(8,128)(2,1)S(1)}, bf16[8,8192]{1,0:T(8,128)(2,1)S(1)}, u32[]{:S(2)}, u32[]{:S(2)}) collective-permute-start(bf16[8,8192]{1,0:T(8,128)(2,1)S(1)} %slice.8), channel_id=1, source_target_pairs={{0,2},{1,3},{2,0},{3,1},{4,6},{5,7},{6,4},{7,5},{8,10},{9,11},{10,... | collective-permute-start | bytes 393224 | tf_op jit(solution)/shard_map/ppermute | solution.py:255
  25.0 3.5 %collective-permute-start.6 = (f32[96,128]{1,0:T(8,128)S(1)}, f32[96,128]{1,0:T(8,128)S(1)}, u32[]{:S(2)}, u32[]{:S(2)}) collective-permute-start(f32[96,128]{1,0:T(8,128)S(1)} %add.15), channel_id=1, source_target_pairs={{0,4},{1,5},{2,6},{3,7},{4,0},{5,1},{6,2},{7,3},{8,12},{9,13},{10,... | collective-permute-start | bytes 147464 | tf_op jit(solution)/shard_map/ppermute | solution.py:255
  28.7 6.4 %collective-permute-start.11 = (bf16[64,8192]{1,0:T(8,128)(2,1)S(1)}, bf16[64,8192]{1,0:T(8,128)(2,1)S(1)}, u32[]{:S(2)}, u32[]{:S(2)}) collective-permute-start(bf16[64,8192]{1,0:T(8,128)(2,1)S(1)} %constant_dynamic-update-slice_fusion.tests_ref), channel_id=1, source_target_pairs={{0,1},{1,0},{2,3},{3,2},{4,5},{5,4},{6,7},{7,6},{8,9},{9,8},{10,11... | collective-permute-start | bytes 3145736 | tf_op jit(solution)/shard_map/ppermute | solution.py:255

commit v11 on v10

--- a/solution.py
+++ b/solution.py
@@ -198,7 +198,7 @@
     xo = jnp.where(eye, 1.0, 0.0)
     wides, narrows = factors(wide), factors(narrow)
     for k in range(max(len(wides), len(narrows))):
-        times = exact if k < 5 else near_exact
+        times = exact if k < 4 else near_exact
         if k < len(wides):
             if k < len(wides) - 1:
                 both = jnp.concatenate([yi, w], axis=0)

time: 36.1 us -> 36 us (level)
  no operation moved by 1% of the time
where the time goes in v11:
time: 36 us; the launch traced here: 35.9 us
  starting transfers between devices  16.7 us (46%)
  waiting for transfers between devices  9.52 us (26%)
  Pallas kernels  9.39 us (26%)
    ppermute x12, starting transfers between devices, exchange(): return lax.ppermute(x, 'ex', [(i, i ^ bit) for i in range(devices)])  16.7 us
    ppermute x12, waiting for transfers between devices, exchange(): return lax.ppermute(x, 'ex', [(i, i ^ bit) for i in range(devices)])  9.52 us
    pallas_call x1, Pallas kernels, project(): pl.pallas_call(project_kernel, out_shape=[pltpu.VMEM((narrow + narrow //...  5.92 us
    pallas_call x1, Pallas kernels, precondition(): pl.pallas_call(functools.partial(precond_kernel, float(tokens), offsets),...  2.6 us
    pallas_call x1, Pallas kernels, score(): pl.pallas_call(functools.partial(score_kernel, sources, scale), out_shape...  0.85 us
  transfers between devices with their start and end apart: 12, of which 4 were waited for; matrix products, arithmetic and copies ran while one was open for 0% of the time, Pallas kernels for 24%

profile of v11, /device:TPU:1, one launch (start us, length us, event | category | flops | bytes accessed | tf_op | source)
XLA Modules:
  0.0 35.9 jit_solution(14028607778029416449)
XLA Ops:
  0.0 0.0 copy-start
  0.0 3.1 %collective-permute-start = (bf16[4,8192]{1,0:T(4,128)(2,1)}, bf16[4,8192]{1,0:T(4,128)(2,1)S(1)}, u32[]{:S(2)}, u32[]{:S(2)}) collective-permute-start(bf16[4,8192]{1,0:T(4,128)(2,1)} %param.9), channel_id=1, source_target_pairs={{0,16},{1,17},{2,18},{3,19},{4,20},{5,21},{6,22},{7,23},{8,24},{9,... | collective-permute-start | bytes 196616 | tf_op jit(solution)/shard_map/ppermute | solution.py:255
  3.1 5.9 %project.1 = (f32[96,128]{1,0:T(8,128)S(1)}, f32[1,64,128]{2,1,0:T(8,128)S(1)}) custom-call(bf16[1,1024,4096]{2,1,0:T(8,128)(2,1)} %x_hbm.1, bf16[1,1024,1024]{2,1,0:T(8,128)(2,1)} %g_hbm.1, bf16[128,4096]{1,0:T(8,128)(2,1)} %pin_hbm.1, bf16[64,1024]{1,0:T(8,128)(2,1)} %pout_hbm.1), custom_call_target="tpu_custom_call" | custom-call | tf_op jit(solution)/shard_map/project/pallas_call | solution.py:111
  9.1 0.0 collective-permute-done
  9.1 0.0 copy-done
  9.1 0.1 pad_maximum_fusion.1
  9.2 1.4 %collective-permute-start.3 = (bf16[8,8192]{1,0:T(8,128)(2,1)S(1)}, bf16[8,8192]{1,0:T(8,128)(2,1)S(1)}, u32[]{:S(2)}, u32[]{:S(2)}) collective-permute-start(bf16[8,8192]{1,0:T(8,128)(2,1)S(1)} %pad_maximum_fusion.1), channel_id=1, source_target_pairs={{0,8},{1,9},{2,10},{3,11},{4,12},{5,13},{6,14},{7,15},{8,0},{9,1},... | collective-permute-start | bytes 393224 | tf_op jit(solution)/shard_map/ppermute | solution.py:255
  10.5 1.2 %collective-permute-start.1 = (f32[96,128]{1,0:T(8,128)S(1)}, f32[96,128]{1,0:T(8,128)S(1)}, u32[]{:S(2)}, u32[]{:S(2)}) collective-permute-start(f32[96,128]{1,0:T(8,128)S(1)} %get-tuple-element.24), channel_id=1, source_target_pairs={{0,1},{1,0},{2,3},{3,2},{4,5},{5,4},{6,7},{7,6},{8,9},{9,8},{10,11... | collective-permute-start | bytes 147464 | tf_op jit(solution)/shard_map/ppermute | solution.py:255
  11.8 0.9 %collective-permute-done.1 = f32[96,128]{1,0:T(8,128)S(1)} collective-permute-done((f32[96,128]{1,0:T(8,128)S(1)}, f32[96,128]{1,0:T(8,128)S(1)}, u32[]{:S(2)}, u32[]{:S(2)}) %collective-permute-start.1) | collective-permute-done | bytes 49184 | tf_op jit(solution)/shard_map/ppermute | solution.py:255
  12.6 1.2 %collective-permute-start.2 = (f32[96,128]{1,0:T(8,128)S(1)}, f32[96,128]{1,0:T(8,128)S(1)}, u32[]{:S(2)}, u32[]{:S(2)}) collective-permute-start(f32[96,128]{1,0:T(8,128)S(1)} %add.11), channel_id=1, source_target_pairs={{0,2},{1,3},{2,0},{3,1},{4,6},{5,7},{6,4},{7,5},{8,10},{9,11},{10,... | collective-permute-start | bytes 147464 | tf_op jit(solution)/shard_map/ppermute | solution.py:255
  13.9 1.7 %collective-permute-done.2 = f32[96,128]{1,0:T(8,128)S(1)} collective-permute-done((f32[96,128]{1,0:T(8,128)S(1)}, f32[96,128]{1,0:T(8,128)S(1)}, u32[]{:S(2)}, u32[]{:S(2)}) %collective-permute-start.2) | collective-permute-done | bytes 49184 | tf_op jit(solution)/shard_map/ppermute | solution.py:255
  15.6 0.0 collective-permute-done.3
  15.6 0.5 %collective-permute-start.4 = (f32[96,128]{1,0:T(8,128)S(1)}, f32[96,128]{1,0:T(8,128)S(1)}, u32[]{:S(2)}, u32[]{:S(2)}) collective-permute-start(f32[96,128]{1,0:T(8,128)S(1)} %add.12.a_ref), channel_id=1, source_target_pairs={{0,8},{1,9},{2,10},{3,11},{4,12},{5,13},{6,14},{7,15},{8,0},{9,1},... | collective-permute-start | bytes 147464 | tf_op jit(solution)/shard_map/ppermute | solution.py:255
  16.2 1.2 %collective-permute-start.9 = (bf16[16,8192]{1,0:T(8,128)(2,1)S(1)}, bf16[16,8192]{1,0:T(8,128)(2,1)S(1)}, u32[]{:S(2)}, u32[]{:S(2)}) collective-permute-start(bf16[16,8192]{1,0:T(8,128)(2,1)S(1)} %pad_maximum_fusion), channel_id=1, source_target_pairs={{0,2},{1,3},{2,0},{3,1},{4,6},{5,7},{6,4},{7,5},{8,10},{9,11},{10,... | collective-permute-start | bytes 786440 | tf_op jit(solution)/shard_map/ppermute | solution.py:255
  17.4 1.2 %collective-permute-start.7 = (bf16[16,8192]{1,0:T(8,128)(2,1)S(1)}, bf16[16,8192]{1,0:T(8,128)(2,1)S(1)}, u32[]{:S(2)}, u32[]{:S(2)}) collective-permute-start(bf16[16,8192]{1,0:T(8,128)(2,1)S(1)} %pad_maximum_fusion), channel_id=1, source_target_pairs={{0,4},{1,5},{2,6},{3,7},{4,0},{5,1},{6,2},{7,3},{8,12},{9,13},{10,... | collective-permute-start | bytes 786440 | tf_op jit(solution)/shard_map/ppermute | solution.py:255
  18.6 0.0 collective-permute-done.4.b_ref
  18.6 0.1 collective-permute-start.5
  18.8 3.7 %collective-permute-done.9 = bf16[16,8192]{1,0:T(8,128)(2,1)S(1)} collective-permute-done((bf16[16,8192]{1,0:T(8,128)(2,1)S(1)}, bf16[16,8192]{1,0:T(8,128)(2,1)S(1)}, u32[]{:S(2)}, u32[]{:S(2)}) %collective-permute-start.9) | collective-permute-done | bytes 262176 | tf_op jit(solution)/shard_map/ppermute | solution.py:255
  22.4 1.3 %collective-permute-start.10 = (bf16[8,8192]{1,0:T(8,128)(2,1)S(1)}, bf16[8,8192]{1,0:T(8,128)(2,1)S(1)}, u32[]{:S(2)}, u32[]{:S(2)}) collective-permute-start(bf16[8,8192]{1,0:T(8,128)(2,1)S(1)} %slice.9), channel_id=1, source_target_pairs={{0,4},{1,5},{2,6},{3,7},{4,0},{5,1},{6,2},{7,3},{8,12},{9,13},{10,... | collective-permute-start | bytes 393224 | tf_op jit(solution)/shard_map/ppermute | solution.py:255
  23.7 0.0 collective-permute-done.7
  23.7 1.3 %collective-permute-start.8 = (bf16[8,8192]{1,0:T(8,128)(2,1)S(1)}, bf16[8,8192]{1,0:T(8,128)(2,1)S(1)}, u32[]{:S(2)}, u32[]{:S(2)}) collective-permute-start(bf16[8,8192]{1,0:T(8,128)(2,1)S(1)} %slice.8), channel_id=1, source_target_pairs={{0,2},{1,3},{2,0},{3,1},{4,6},{5,7},{6,4},{7,5},{8,10},{9,11},{10,... | collective-permute-start | bytes 393224 | tf_op jit(solution)/shard_map/ppermute | solution.py:255
  25.0 0.0 collective-permute-done.5.b_ref
  25.0 0.3 collective-permute-start.6
  25.3 3.2 %collective-permute-done.6 = f32[96,128]{1,0:T(8,128)S(1)} collective-permute-done((f32[96,128]{1,0:T(8,128)S(1)}, f32[96,128]{1,0:T(8,128)S(1)}, u32[]{:S(2)}, u32[]{:S(2)}) %collective-permute-start.6) | collective-permute-done | bytes 49184 | tf_op jit(solution)/shard_map/ppermute | solution.py:255
  28.5 0.0 collective-permute-done.10
  28.6 0.0 collective-permute-done.8
  28.7 3.7 %collective-permute-start.11 = (bf16[64,8192]{1,0:T(8,128)(2,1)S(1)}, bf16[64,8192]{1,0:T(8,128)(2,1)S(1)}, u32[]{:S(2)}, u32[]{:S(2)}) collective-permute-start(bf16[64,8192]{1,0:T(8,128)(2,1)S(1)} %constant_dynamic-update-slice_fusion.tests_ref), channel_id=1, source_target_pairs={{0,1},{1,0},{2,3},{3,2},{4,5},{5,4},{6,7},{7,6},{8,9},{9,8},{10,11... | collective-permute-start | bytes 3145736 | tf_op jit(solution)/shard_map/ppermute | solution.py:255
  32.4 2.6 %precondition.1 = (f32[1,64,128]{2,1,0:T(8,128)S(1)}, f32[1,128]{1,0:T(1,128)S(1)}) custom-call(s32[1]{0:T(128)} %bitcast.me_ref, f32[96,128]{1,0:T(8,128)S(1)} %add.13.packed_ref, f32[1,64,128]{2,1,0:T(8,128)S(1)} %get-tuple-element.29.grads_ref, bf16[64,8192]{1,0:T(8,128)(2,1)S(1)} %constant_dynamic-update-slice_fusion.tests_ref), custom_call_target="tpu_custom_call" | custom-call | tf_op jit(solution)/shard_map/precondition/pallas_call | solution.py:224
  35.0 0.0 collective-permute-done.11.refs_0_
  35.0 0.9 %score.1 = f32[1,128]{1,0:T(1,128)} custom-call(s32[1]{0:T(128)} %bitcast.me_ref, f32[1,64,128]{2,1,0:T(8,128)S(1)} %get-tuple-element.35.p_ref, f32[1,128]{1,0:T(1,128)S(1)} %get-tuple-element.36.part_ref, bf16[64,8192]{1,0:T(8,128)(2,1)S(1)} %collective-permute-done.11.refs_0_), custom_call_target="tpu_custom_call" | custom-call | tf_op jit(solution)/shard_map/score/pallas_call | solution.py:244
  (13 shorter events, 0.2 us)
Async XLA Ops:
  0.0 9.1 %copy-start = (bf16[4,8192]{1,0:T(4,128)(2,1)S(1)}, bf16[4,8192]{1,0:T(4,128)(2,1)}, u32[]{:S(2)}) copy-start(bf16[4,8192]{1,0:T(4,128)(2,1)} %param.9) | copy-start | bytes 196612
  0.0 9.1 %collective-permute-start = (bf16[4,8192]{1,0:T(4,128)(2,1)}, bf16[4,8192]{1,0:T(4,128)(2,1)S(1)}, u32[]{:S(2)}, u32[]{:S(2)}) collective-permute-start(bf16[4,8192]{1,0:T(4,128)(2,1)} %param.9), channel_id=1, source_target_pairs={{0,16},{1,17},{2,18},{3,19},{4,20},{5,21},{6,22},{7,23},{8,24},{9,... | collective-permute-start | bytes 196616 | tf_op jit(solution)/shard_map/ppermute | solution.py:255
  9.2 6.4 %collective-permute-start.3 = (bf16[8,8192]{1,0:T(8,128)(2,1)S(1)}, bf16[8,8192]{1,0:T(8,128)(2,1)S(1)}, u32[]{:S(2)}, u32[]{:S(2)}) collective-permute-start(bf16[8,8192]{1,0:T(8,128)(2,1)S(1)} %pad_maximum_fusion.1), channel_id=1, source_target_pairs={{0,8},{1,9},{2,10},{3,11},{4,12},{5,13},{6,14},{7,15},{8,0},{9,1},... | collective-permute-start | bytes 393224 | tf_op jit(solution)/shard_map/ppermute | solution.py:255
  10.5 2.1 %collective-permute-start.1 = (f32[96,128]{1,0:T(8,128)S(1)}, f32[96,128]{1,0:T(8,128)S(1)}, u32[]{:S(2)}, u32[]{:S(2)}) collective-permute-start(f32[96,128]{1,0:T(8,128)S(1)} %get-tuple-element.24), channel_id=1, source_target_pairs={{0,1},{1,0},{2,3},{3,2},{4,5},{5,4},{6,7},{7,6},{8,9},{9,8},{10,11... | collective-permute-start | bytes 147464 | tf_op jit(solution)/shard_map/ppermute | solution.py:255
  12.6 2.9 %collective-permute-start.2 = (f32[96,128]{1,0:T(8,128)S(1)}, f32[96,128]{1,0:T(8,128)S(1)}, u32[]{:S(2)}, u32[]{:S(2)}) collective-permute-start(f32[96,128]{1,0:T(8,128)S(1)} %add.11), channel_id=1, source_target_pairs={{0,2},{1,3},{2,0},{3,1},{4,6},{5,7},{6,4},{7,5},{8,10},{9,11},{10,... | collective-permute-start | bytes 147464 | tf_op jit(solution)/shard_map/ppermute | solution.py:255
  15.6 3.0 %collective-permute-start.4 = (f32[96,128]{1,0:T(8,128)S(1)}, f32[96,128]{1,0:T(8,128)S(1)}, u32[]{:S(2)}, u32[]{:S(2)}) collective-permute-start(f32[96,128]{1,0:T(8,128)S(1)} %add.12.a_ref), channel_id=1, source_target_pairs={{0,8},{1,9},{2,10},{3,11},{4,12},{5,13},{6,14},{7,15},{8,0},{9,1},... | collective-permute-start | bytes 147464 | tf_op jit(solution)/shard_map/ppermute | solution.py:255
  16.2 6.3 %collective-permute-start.9 = (bf16[16,8192]{1,0:T(8,128)(2,1)S(1)}, bf16[16,8192]{1,0:T(8,128)(2,1)S(1)}, u32[]{:S(2)}, u32[]{:S(2)}) collective-permute-start(bf16[16,8192]{1,0:T(8,128)(2,1)S(1)} %pad_maximum_fusion), channel_id=1, source_target_pairs={{0,2},{1,3},{2,0},{3,1},{4,6},{5,7},{6,4},{7,5},{8,10},{9,11},{10,... | collective-permute-start | bytes 786440 | tf_op jit(solution)/shard_map/ppermute | solution.py:255
  17.4 6.4 %collective-permute-start.7 = (bf16[16,8192]{1,0:T(8,128)(2,1)S(1)}, bf16[16,8192]{1,0:T(8,128)(2,1)S(1)}, u32[]{:S(2)}, u32[]{:S(2)}) collective-permute-start(bf16[16,8192]{1,0:T(8,128)(2,1)S(1)} %pad_maximum_fusion), channel_id=1, source_target_pairs={{0,4},{1,5},{2,6},{3,7},{4,0},{5,1},{6,2},{7,3},{8,12},{9,13},{10,... | collective-permute-start | bytes 786440 | tf_op jit(solution)/shard_map/ppermute | solution.py:255
  18.6 6.4 %collective-permute-start.5 = (f32[96,128]{1,0:T(8,128)S(1)}, f32[96,128]{1,0:T(8,128)S(1)}, u32[]{:S(2)}, u32[]{:S(2)}) collective-permute-start(f32[96,128]{1,0:T(8,128)S(1)} %add.14.a_ref), channel_id=1, source_target_pairs={{0,16},{1,17},{2,18},{3,19},{4,20},{5,21},{6,22},{7,23},{8,24},{9,... | collective-permute-start | bytes 147464 | tf_op jit(solution)/shard_map/ppermute | solution.py:255
  22.4 6.1 %collective-permute-start.10 = (bf16[8,8192]{1,0:T(8,128)(2,1)S(1)}, bf16[8,8192]{1,0:T(8,128)(2,1)S(1)}, u32[]{:S(2)}, u32[]{:S(2)}) collective-permute-start(bf16[8,8192]{1,0:T(8,128)(2,1)S(1)} %slice.9), channel_id=1, source_target_pairs={{0,4},{1,5},{2,6},{3,7},{4,0},{5,1},{6,2},{7,3},{8,12},{9,13},{10,... | collective-permute-start | bytes 393224 | tf_op jit(solution)/shard_map/ppermute | solution.py:255
  23.7 4.8 %collective-permute-start.8 = (bf16[8,8192]{1,0:T(8,128)(2,1)S(1)}, bf16[8,8192]{1,0:T(8,128)(2,1)S(1)}, u32[]{:S(2)}, u32[]{:S(2)}) collective-permute-start(bf16[8,8192]{1,0:T(8,128)(2,1)S(1)} %slice.8), channel_id=1, source_target_pairs={{0,2},{1,3},{2,0},{3,1},{4,6},{5,7},{6,4},{7,5},{8,10},{9,11},{10,... | collective-permute-start | bytes 393224 | tf_op jit(solution)/shard_map/ppermute | solution.py:255
  25.0 3.5 %collective-permute-start.6 = (f32[96,128]{1,0:T(8,128)S(1)}, f32[96,128]{1,0:T(8,128)S(1)}, u32[]{:S(2)}, u32[]{:S(2)}) collective-permute-start(f32[96,128]{1,0:T(8,128)S(1)} %add.15), channel_id=1, source_target_pairs={{0,4},{1,5},{2,6},{3,7},{4,0},{5,1},{6,2},{7,3},{8,12},{9,13},{10,... | collective-permute-start | bytes 147464 | tf_op jit(solution)/shard_map/ppermute | solution.py:255
  28.7 6.3 %collective-permute-start.11 = (bf16[64,8192]{1,0:T(8,128)(2,1)S(1)}, bf16[64,8192]{1,0:T(8,128)(2,1)S(1)}, u32[]{:S(2)}, u32[]{:S(2)}) collective-permute-start(bf16[64,8192]{1,0:T(8,128)(2,1)S(1)} %constant_dynamic-update-slice_fusion.tests_ref), channel_id=1, source_target_pairs={{0,1},{1,0},{2,3},{3,2},{4,5},{5,4},{6,7},{7,6},{8,9},{9,8},{10,11... | collective-permute-start | bytes 3145736 | tf_op jit(solution)/shard_map/ppermute | solution.py:255
